TPU v7x, 256 devices: a whole 4x4x8 slice. The times are simulated.
256 devices in a mesh: gx: 8 (over y, core), gy: 16 (over z_lo, x), ka: 2 (over z_hi).
Axes of the slice: x: 4, y: 4, z: 8 (z_hi: 2, z_lo: 4; z = z_hi * 4 + z_lo), core: 2. Of those that a mesh axis runs over, the one named last changes fastest.
Arguments:
- mask_param: float32 [24576, 2048], P('gy', 'gx'), may hold values from -6 to 6
- target: int32 [24576, 2048], P('gy', 'gx'), may hold values 0 or 1
- kernels: float32 [12, 2, 4096], P('ka'), may hold values from -4 to 4
- weights: float32 [12], P('ka'), may hold values from 0.05 to 0.3
Outputs:
- mask_gradient: float32 [24576, 2048], P('gy', 'gx')
- resist_image: float32 [24576, 2048], P('gy', 'gx')
All inputs are finite; a program needn't handle non-finite values. No bound on the sum of `target` on one device may be relied on, other than what follows from the above.
Results may differ from a plain program's by a relative error of at most 0.0003.
Values sent between devices are 32-bit elements; how exact they have to be, the bound alone decides.
No kernel may reach another device: no remote copies, remote signals or barrier semaphores. Data moves between devices by JAX's collectives and lax.ppermute only.
A program may use at most 128 MiB of HBM per device.

v0:
```python
import math

import jax
import jax.numpy as jnp
import ml_dtypes
import numpy as np
from jax import lax
from jax.experimental import pallas as pl
from jax.experimental.pallas import tpu as pltpu
from jax.sharding import PartitionSpec as P

WIN = 512
HALO = 128
FB = 64
TILE = 256
COARSE = 128
HALF = COARSE // 2
VMEM_LIMIT = 48 * 1024 * 1024

bf16 = ml_dtypes.bfloat16


def halves(table):
    high = table.astype(np.float32).astype(bf16)
    low = (table - high.astype(np.float64)).astype(np.float32).astype(bf16)
    return high, low


def as_left(table):
    high, low = halves(table)
    return np.concatenate([high, low, high], axis=1)


def as_right(table):
    high, low = halves(table)
    return np.concatenate([high, high, low], axis=0)


def angles(points):
    frequencies = np.arange(FB) - FB // 2
    windings = np.mod(frequencies[:, None] * np.asarray(points)[None, :], WIN)
    return windings * (2.0 * math.pi / WIN)


ORDER = np.concatenate([np.arange(0, FB, 2), np.arange(1, FB, 2)])


def blocks(table):
    return [table[:, i : i + 128] for i in range(0, table.shape[1], 128)]


def make_tables():
    factor = 1.0 / (WIN * FB)
    pixels = np.arange(HALO)
    columns, rows, outs, pixs = [], [], [], []
    for points in (pixels + 3 * HALO, pixels):
        cos, sin = np.cos(angles(points)), np.sin(angles(points))
        columns.append(as_right(np.concatenate([cos.T, -sin.T], axis=1)))
        pixs.append(as_right(np.concatenate([cos, -sin], axis=0)))
        cos, sin = cos[ORDER], sin[ORDER]
        rows += blocks(as_left(factor * np.concatenate([cos, sin], axis=0)))
        outs += blocks(as_left(factor * np.concatenate([cos.T, sin.T], axis=1)))
    plus = 4 * np.arange(HALF) + 2
    samples = np.concatenate([plus, -plus])
    cos, sin = np.cos(angles(samples)), np.sin(angles(samples))
    spread = as_right(
        np.concatenate(
            [np.concatenate([cos, sin], axis=1), np.concatenate([-sin, cos], axis=1)], axis=0
        )
    )
    gather = np.concatenate(
        [np.concatenate([cos.T, -sin.T], axis=1), np.concatenate([sin.T, cos.T], axis=1)], axis=0
    )
    gather = np.concatenate(halves(gather), axis=1)
    cos, sin = np.cos(angles(plus))[ORDER], np.sin(angles(plus))[ORDER]
    lift = as_left(np.concatenate([cos.T, sin.T], axis=0))
    lift = np.concatenate([lift, np.zeros((COARSE, 64), bf16)], axis=1)
    high, low = halves(np.concatenate([cos, sin], axis=1))
    fold = np.concatenate(
        [np.concatenate([high, high], axis=1), np.concatenate([low, 0 * low], axis=1)], axis=0
    )
    offset = (np.arange(TILE) + HALO)[:, None] - samples[None, :]
    orders = np.arange(1, COARSE // 2)
    turns = np.mod(offset[..., None] * orders, WIN) * (2.0 * math.pi / WIN)
    interp = (1.0 + 2.0 * np.cos(turns).sum(-1)) / COARSE
    high, low = halves(interp)
    fine_left = np.concatenate(
        [np.concatenate([high, high], axis=1), np.concatenate([low, 0 * low], axis=1)], axis=0
    )
    coarse_left = np.concatenate(halves(interp.T), axis=0)
    coarse_right = np.concatenate(halves(interp), axis=1)
    return {
        "analysis": np.concatenate(columns + rows, axis=0),
        "synthesis": np.concatenate(pixs + outs, axis=0),
        "imaging": np.concatenate(
            [spread, gather, lift, fold, as_right(interp.T), fine_left, coarse_left, coarse_right],
            axis=0,
        ),
    }


TABLES = make_tables()
SPREAD, GATHER, LIFT, FOLD, FINE_RIGHT, FINE_LEFT, COARSE_LEFT, COARSE_RIGHT = (
    slice(a, b)
    for a, b in (
        (0, 384), (384, 640), (640, 768), (768, 896), (896, 1280), (1280, 1792), (1792, 2048),
        (2048, 2304),
    )
)


def split(value):
    high = value.astype(jnp.bfloat16)
    low = (value - high.astype(jnp.float32)).astype(jnp.bfloat16)
    return high, low


def dot(left, right):
    return jnp.dot(left, right, preferred_element_type=jnp.float32)


def times_table(value, table):
    high, low = split(value)
    return dot(jnp.concatenate([high, low, high], axis=1), table)


def table_times(table, value):
    high, low = split(value)
    return dot(table, jnp.concatenate([high, high, low], axis=0))


def stacked_times(table, value):
    high, low = split(value)
    found = dot(table, jnp.concatenate([high, low], axis=0))
    size = found.shape[0] // 2
    return found[:size] + found[size:]


def times_paired(value, table):
    high, low = split(value)
    width = table.shape[1] // 2
    first = dot(high, table)
    return first[:, :width] + (first[:, width:] + dot(low, table[:, :width]))


def col_table(packed, index):
    return packed[index * 384 : (index + 1) * 384, :]


def row_table(packed, index):
    start = 768 + index * 384
    return jnp.concatenate(
        [packed[start + i : start + i + 128, :] for i in (0, 128, 256)], axis=1
    )


def parity(shape):
    index = lax.broadcasted_iota(jnp.int32, shape, 1)
    return (1 - 2 * (index % 2)).astype(jnp.float32)


def row_parity(shape):
    index = lax.broadcasted_iota(jnp.int32, shape, 0)
    return jnp.where(index < FB // 2, 1.0, -1.0)


def low_lanes(shape):
    return lax.broadcasted_iota(jnp.int32, shape, 1) < FB


def swapped(value):
    return pltpu.roll(value, FB, 1)


def preparation_kernel(roots, own, other, straight, crossed, real, imag):
    count = own.shape[0]
    lanes = low_lanes((FB // 2, 2 * FB))
    for group, source in enumerate((own, other)):
        for index in range(count):
            for row in range(FB // 2):
                place = slice(row * 2 * FB, (row + 1) * 2 * FB)
                real[row : row + 1, :] = source[index, 0:1, place]
                imag[row : row + 1, :] = source[index, 1:2, place]
            root = roots[group, index]
            re, im = root * real[...], root * imag[...]
            re_turned, im_turned = swapped(re), swapped(im)
            at = group * count + index
            straight[at, : FB // 2] = jnp.where(lanes, re, re_turned)
            straight[at, FB // 2 :] = jnp.where(lanes, re_turned, re)
            crossed[at, : FB // 2] = jnp.where(lanes, -im, im_turned)
            crossed[at, FB // 2 :] = jnp.where(lanes, -im_turned, im)


def analysis_kernel(mask, above, below, tables, left, right, slope, total):
    step = pl.program_id(0)
    count = left.shape[0]
    sign = jnp.where(low_lanes((FB, 2 * FB)), 1.0, -1.0)
    flip = row_parity((FB, 4 * FB))

    def spectra(transmit):
        high, low = split(transmit)
        rows = []
        for side in (0, 1):
            lanes = slice(side * HALO, (side + 1) * HALO)
            three = jnp.concatenate([high[:, lanes], low[:, lanes], high[:, lanes]], axis=1)
            rows.append(dot(three, col_table(tables, side)))
        rows = jnp.concatenate(rows, axis=1)
        found = []
        for part in (0, 1):
            both = table_times(row_table(tables, part), rows[part * HALO : (part + 1) * HALO])
            sine = both[FB:]
            turned = [sign * swapped(sine[:, : 2 * FB]), sign * swapped(sine[:, 2 * FB :])]
            found.append(both[:FB] + jnp.concatenate(turned, axis=1))
        return found

    @pl.when(step == 0)
    def _():
        outer = jnp.concatenate([below[...], above[...]], axis=0)
        upper, lower = spectra(jnp.tanh(outer))
        total[...] = jnp.zeros_like(total)
        total[1] = lower
        total[count] = upper

    transmit = jnp.tanh(mask[...])
    slope[...] = 1.0 - transmit * transmit
    upper, lower = spectra(transmit)
    total[step] += upper
    total[step + 1] += flip * (upper + lower)
    total[step + 2] += lower

    @pl.when(step == count - 1)
    def _():
        left[...] = total[1 : count + 1, :, : 2 * FB]
        right[...] = total[1 : count + 1, :, 2 * FB :]


def imaging_kernel(
    left, right, from_left, from_right, straight, crossed, target, wide,
    resist_ref, grad, fields, intensity, weight, adjoint, sides,
):
    count = straight.shape[0] // 2
    flip = parity((FB, 2 * FB))
    spectrum = flip * (left[0] + right[0]) + from_left[0] + from_right[0]
    turned = swapped(spectrum)

    def forward(group, carry):
        first = group * count
        products = [
            straight[first + i] * spectrum + crossed[first + i] * turned for i in range(count)
        ]
        rows = times_table(jnp.concatenate(products, axis=0), wide[SPREAD, :])
        total = jnp.zeros((COARSE, COARSE), jnp.float32)
        for i in range(count):
            both = table_times(wide[LIFT, :192], rows[i * FB : (i + 1) * FB])
            cosine, sine = both[:HALF], both[HALF:]
            sine_re, sine_im = sine[:, :COARSE], sine[:, COARSE:]
            cosine_re, cosine_im = cosine[:, :COARSE], cosine[:, COARSE:]
            real = jnp.concatenate([cosine_re - sine_im, cosine_re + sine_im], axis=0)
            imag = jnp.concatenate([cosine_im + sine_re, cosine_im - sine_re], axis=0)
            fields[first + i, :, :COARSE] = real
            fields[first + i, :, COARSE:] = imag
            total = total + (real * real + imag * imag)
        intensity[group] = total
        return carry

    lax.fori_loop(0, 2, forward, 0)

    half_fine = times_table(intensity[0] + intensity[1], wide[FINE_RIGHT, :])
    fine = stacked_times(wide[FINE_LEFT, :], half_fine)
    resist = jax.nn.sigmoid(4.0 * (fine - 1.0))
    resist_ref[...] = resist
    misfit = resist - target[...].astype(jnp.float32)
    push = 16.0 * misfit * resist * (1.0 - resist)
    high, low = split(push)
    from_high = dot(wide[COARSE_LEFT, :], high)
    half_coarse = from_high[:COARSE] + (
        from_high[COARSE:] + dot(wide[COARSE_LEFT, :][:COARSE], low)
    )
    weight[...] = times_paired(half_coarse, wide[COARSE_RIGHT, :])

    sign = jnp.where(low_lanes((HALF, 2 * FB)), 1.0, -1.0)

    def backward(group, carry):
        first = group * count
        scale = jnp.concatenate([weight[...], weight[...]], axis=1)
        scaled = jnp.concatenate([fields[first + i] * scale for i in range(count)], axis=0)
        sides[...] = times_paired(scaled, wide[GATHER, :])
        total = jnp.zeros((FB, 2 * FB), jnp.float32)
        for i in range(0, count, 2):
            pair = []
            for j in (i, i + 1):
                plus = sides[j * COARSE : j * COARSE + HALF, :]
                minus = sides[j * COARSE + HALF : (j + 1) * COARSE, :]
                pair.append(
                    jnp.concatenate([plus + minus, sign * swapped(plus - minus)], axis=0)
                )
            found = stacked_times(wide[FOLD, :], jnp.concatenate(pair, axis=1))
            for j in (0, 1):
                part = found[:, j * 2 * FB : (j + 1) * 2 * FB]
                total = total + (
                    straight[first + i + j] * part - crossed[first + i + j] * swapped(part)
                )
        adjoint[group] = total
        return carry

    lax.fori_loop(0, 2, backward, 0)
    grad[0] = adjoint[0] + adjoint[1]


def synthesis_kernel(own, from_left, from_right, above, below, slope, tables, result, mixed):
    step = pl.program_id(0)
    count = own.shape[0]
    flip_col = parity((FB, 2 * FB))
    flip_row = row_parity((FB, 4 * FB))
    sign = jnp.where(low_lanes((FB, 2 * FB)), -1.0, 1.0)

    @pl.when(step == 0)
    def _():
        mixed[0] = above[...]
        mixed[count + 1] = below[...]
        for index in range(count):
            base = flip_col * own[index]
            mixed[index + 1, :, : 2 * FB] = base + from_left[index]
            mixed[index + 1, :, 2 * FB :] = base + from_right[index]

    base = flip_row * mixed[step + 1]
    rows = []
    for near, part in ((step, 0), (step + 2, 1)):
        block = base + mixed[near]
        turned = [sign * swapped(block[:, : 2 * FB]), sign * swapped(block[:, 2 * FB :])]
        stacked = jnp.concatenate([block, jnp.concatenate(turned, axis=1)], axis=0)
        rows.append(table_times(row_table(tables, part), stacked))
    high, low = split(jnp.concatenate(rows, axis=0))
    sides = []
    for side in (0, 1):
        lanes = slice(side * 2 * FB, (side + 1) * 2 * FB)
        three = jnp.concatenate([high[:, lanes], low[:, lanes], high[:, lanes]], axis=1)
        sides.append(dot(three, col_table(tables, side)))
    result[...] = jnp.concatenate(sides, axis=1) * slope[...]


def whole(array):
    zeros = (0,) * len(array.shape)
    return pl.BlockSpec(array.shape, lambda step: zeros)


def tile_rows():
    return pl.BlockSpec((TILE, TILE), lambda step: (step, 0))


def spectra_of_tile():
    return pl.BlockSpec((1, FB, 2 * FB), lambda step: (step, 0, 0))


def params():
    return pltpu.CompilerParams(
        dimension_semantics=("arbitrary",), vmem_limit_bytes=VMEM_LIMIT
    )


def preparation(roots, own, other):
    shape = jax.ShapeDtypeStruct((2 * own.shape[0], FB, 2 * FB), jnp.float32)
    part = pltpu.VMEM((FB // 2, 2 * FB), jnp.float32)
    return pl.pallas_call(
        preparation_kernel,
        out_shape=(shape, shape),
        in_specs=[pl.BlockSpec(memory_space=pltpu.SMEM)]
        + [pl.BlockSpec(memory_space=pltpu.VMEM)] * 2,
        out_specs=[pl.BlockSpec(memory_space=pltpu.VMEM)] * 2,
        scratch_shapes=[part, part],
        compiler_params=pltpu.CompilerParams(vmem_limit_bytes=VMEM_LIMIT),
        cost_estimate=pl.CostEstimate(flops=400000, bytes_accessed=1600000, transcendentals=0),
        name="preparation",
    )(roots, own, other)


def analysis(mask, above, below):
    tiles = mask.shape[0] // TILE
    tables = jnp.asarray(TABLES["analysis"])
    spectra = jax.ShapeDtypeStruct((tiles, FB, 2 * FB), jnp.float32)
    return pl.pallas_call(
        analysis_kernel,
        grid=(tiles,),
        out_shape=(spectra, spectra, jax.ShapeDtypeStruct(mask.shape, jnp.float32)),
        in_specs=[tile_rows(), whole(above), whole(below), whole(tables)],
        out_specs=[whole(spectra), whole(spectra), tile_rows()],
        scratch_shapes=[pltpu.VMEM((tiles + 2, FB, 4 * FB), jnp.float32)],
        compiler_params=params(),
        name="analysis",
    )(mask, above, below, tables)


def imaging(left, right, from_left, from_right, straight, crossed, target):
    tiles = left.shape[0]
    kernels = straight.shape[0]
    tables = jnp.asarray(TABLES["imaging"])
    return pl.pallas_call(
        imaging_kernel,
        grid=(tiles,),
        out_shape=(
            jax.ShapeDtypeStruct(target.shape, jnp.float32),
            jax.ShapeDtypeStruct(left.shape, jnp.float32),
        ),
        in_specs=[spectra_of_tile()] * 4
        + [whole(straight), whole(crossed), tile_rows(), whole(tables)],
        out_specs=[tile_rows(), spectra_of_tile()],
        scratch_shapes=[
            pltpu.VMEM((kernels, COARSE, 2 * COARSE), jnp.float32),
            pltpu.VMEM((2, COARSE, COARSE), jnp.float32),
            pltpu.VMEM((COARSE, COARSE), jnp.float32),
            pltpu.VMEM((2, FB, 2 * FB), jnp.float32),
            pltpu.VMEM((kernels // 2 * COARSE, 2 * FB), jnp.float32),
        ],
        compiler_params=params(),
        name="imaging",
    )(left, right, from_left, from_right, straight, crossed, target, tables)


def synthesis(own, from_left, from_right, above, below, slope):
    tiles = own.shape[0]
    tables = jnp.asarray(TABLES["synthesis"])
    return pl.pallas_call(
        synthesis_kernel,
        grid=(tiles,),
        out_shape=jax.ShapeDtypeStruct(slope.shape, jnp.float32),
        in_specs=[whole(own)] * 3 + [whole(above), whole(below), tile_rows(), whole(tables)],
        out_specs=tile_rows(),
        scratch_shapes=[pltpu.VMEM((tiles + 2, FB, 4 * FB), jnp.float32)],
        compiler_params=params(),
        name="synthesis",
    )(own, from_left, from_right, above, below, slope, tables)


def shifted(value, axis, steps):
    count = lax.axis_size(axis)
    pairs = [(i, i + steps) for i in range(count) if 0 <= i + steps < count]
    return lax.ppermute(value, axis, pairs)


def local(mask_param, target, kernels, weights):
    above = shifted(mask_param[-HALO:], "gy", 1)
    below = shifted(mask_param[:HALO], "gy", -1)
    rows = lax.axis_size("gy")
    inner = rows // 4
    pairs = []
    for place in range(rows):
        mirror = (3 - place // inner) * inner + place % inner
        pairs += [(2 * place, 2 * mirror + 1), (2 * place + 1, 2 * mirror)]
    other = lax.ppermute(kernels, ("gy", "ka"), pairs)
    roots = jnp.sqrt(lax.all_gather(weights, "ka"))
    roots = jnp.where(lax.axis_index("ka") == 0, roots, roots[::-1])
    left, right, slope = analysis(mask_param, above, below)
    from_right = shifted(left, "gx", -1)
    from_left = shifted(right, "gx", 1)
    straight, crossed = preparation(roots, kernels, other)
    resist, grad = imaging(left, right, from_left, from_right, straight, crossed, target)
    grad_left = shifted(grad, "gx", 1)
    grad_right = shifted(grad, "gx", -1)

    flip = jnp.asarray(np.where(np.arange(2 * FB) % 2 == 0, 1.0, -1.0).astype(np.float32))

    def edge(index):
        base = flip * grad[index]
        return jnp.concatenate([base + grad_left[index], base + grad_right[index]], axis=-1)

    from_above = shifted(edge(-1), "gy", 1)
    from_below = shifted(edge(0), "gy", -1)
    gradient = synthesis(grad, grad_left, grad_right, from_above, from_below, slope)
    return (gradient, resist)


def solution(mesh):
    placed = (P("gy", "gx"), P("gy", "gx"), P("ka", None, None), P("ka"))
    return jax.shard_map(
        local, mesh=mesh, in_specs=placed, out_specs=(P("gy", "gx"), P("gy", "gx")), check_vma=False
    )
```

profile of v0, /device:TPU:22, one launch (start us, length us, event | category | flops | bytes accessed | tf_op | source)
XLA Modules:
  0.0 90.1 jit_solution(7944266722795644672)
XLA Ops:
  0.6 0.0 copy-start.5
  0.6 1.0 %fusion.4 = (f32[128,256]{1,0:T(8,128)S(1)}, f32[128,256]{1,0:T(8,128)S(1)}) fusion(f32[1536,256]{1,0:T(8,128)} %mask.1), kind=kLoop, calls=%fused_computation.13 | loop fusion | bytes 524288 | tf_op jit(solution)/shard_map/slice | solution.py:442
  1.7 2.7 %collective-permute-start.1 = (f32[128,256]{1,0:T(8,128)S(1)}, f32[128,256]{1,0:T(8,128)S(1)}, u32[]{:S(2)}, u32[]{:S(2)}) collective-permute-start(f32[128,256]{1,0:T(8,128)S(1)} %get-tuple-element.16), channel_id=1, source_target_pairs={{2,0},{4,2},{6,4},{8,6},{10,8},{12,10},{14,12},{16,14},{18,16},{20... | collective-permute-start | bytes 393224 | tf_op jit(solution)/shard_map/ppermute | solution.py:437
  4.4 5.2 %collective-permute-start = (f32[128,256]{1,0:T(8,128)S(1)}, f32[128,256]{1,0:T(8,128)S(1)}, u32[]{:S(2)}, u32[]{:S(2)}) collective-permute-start(f32[128,256]{1,0:T(8,128)S(1)} %get-tuple-element.17), channel_id=1, source_target_pairs={{0,2},{2,4},{4,6},{6,8},{8,10},{10,12},{12,14},{14,16},{16,18},{18... | collective-permute-start | bytes 393224 | tf_op jit(solution)/shard_map/ppermute | solution.py:437
  9.6 1.3 %dynamic-slice = u32[1]{0:T(128)} dynamic-slice(u32[256]{0:T(256)} %constant.20, u32[]{:T(128)S(6)} %add.16), dynamic_slice_sizes={1} | dynamic-slice | bytes 12
  11.6 0.9 dynamic-update-slice
  12.4 2.0 %collective-permute-start.4 = (f32[6,2,4096]{2,1,0:T(2,128)}, f32[6,2,4096]{2,1,0:T(2,128)S(1)}, u32[]{:S(2)}, u32[]{:S(2)}) collective-permute-start(f32[6,2,4096]{2,1,0:T(2,128)} %own.1), channel_id=1, source_target_pairs={{0,25},{1,24},{2,27},{3,26},{4,29},{5,28},{6,31},{7,30},{8,17},{9,... | collective-permute-start | bytes 589832 | tf_op jit(solution)/shard_map/ppermute | solution.py:449
  14.4 9.0 %all-reduce = f32[12]{0:T(128)S(1)} all-reduce(f32[12]{0:T(128)S(1)} %dynamic-update-slice), channel_id=2, replica_groups=mesh['gx'=8,'gy'=16,'ka'=2] {'ka'}, use_global_device_ids=true, to_apply=%add | all-reduce | flops 12 | bytes 96
  23.4 0.1 reshape.6
  23.5 0.0 collective-permute-done.1.below
  23.5 0.0 collective-permute-done.above
  23.5 0.0 copy-start
  23.5 1.4 %copy-done = f32[1536,256]{1,0:T(8,128)S(1)} copy-done((f32[1536,256]{1,0:T(8,128)S(1)}, f32[1536,256]{1,0:T(8,128)}, u32[]{:S(2)}) %copy-start) | copy-done | bytes 1572888
  24.9 1.0 %copy-done.4 = bf16[1536,128]{1,0:T(8,128)(2,1)S(1)} copy-done((bf16[1536,128]{1,0:T(8,128)(2,1)S(1)}, bf16[1536,128]{1,0:T(8,128)(2,1)}, u32[]{:S(2)}) %copy-start.4) | copy-done | bytes 393240
  25.9 3.9 %analysis.1 = (f32[6,64,128]{2,1,0:T(8,128)S(1)}, f32[6,64,128]{2,1,0:T(8,128)S(1)}, f32[1536,256]{1,0:T(8,128)S(1)}) custom-call(f32[1536,256]{1,0:T(8,128)S(1)} %copy-done, f32[128,256]{1,0:T(8,128)S(1)} %collective-permute-done.above, f32[128,256]{1,0:T(8,128)S(1)} %collective-permute-done.1.below, bf16[1536,128]{1,0:T(8,128)(2,1)S(1)} %copy-done.4), custom_call_target="tpu_custom_call" | custom-call | tf_op jit(solution)/shard_map/analysis/pallas_call | solution.py:381
  29.9 1.9 %collective-permute-start.3 = (f32[6,64,128]{2,1,0:T(8,128)S(1)}, f32[6,64,128]{2,1,0:T(8,128)S(1)}, u32[]{:S(2)}, u32[]{:S(2)}) collective-permute-start(f32[6,64,128]{2,1,0:T(8,128)S(1)} %get-tuple-element.9.left), channel_id=1, source_target_pairs={{32,0},{64,32},{96,64},{128,96},{160,128},{192,160},{224,192},{33,... | collective-permute-start | bytes 589832 | tf_op jit(solution)/shard_map/ppermute | solution.py:437
  31.8 2.4 %collective-permute-start.2 = (f32[6,64,128]{2,1,0:T(8,128)S(1)}, f32[6,64,128]{2,1,0:T(8,128)S(1)}, u32[]{:S(2)}, u32[]{:S(2)}) collective-permute-start(f32[6,64,128]{2,1,0:T(8,128)S(1)} %get-tuple-element.10.right), channel_id=1, source_target_pairs={{0,32},{32,64},{64,96},{96,128},{128,160},{160,192},{192,224},{1,3... | collective-permute-start | bytes 589832 | tf_op jit(solution)/shard_map/ppermute | solution.py:437
  34.2 0.0 collective-permute-done.4.other
  34.2 0.9 %preparation.1 = (f32[12,64,128]{2,1,0:T(8,128)S(1)}, f32[12,64,128]{2,1,0:T(8,128)S(1)}) custom-call(f32[2,6]{1,0:T(2,128)S(1)} %broadcast_select_fusion.roots, f32[6,2,4096]{2,1,0:T(2,128)S(1)} %copy-done.5, f32[6,2,4096]{2,1,0:T(2,128)S(1)} %collective-permute-done.4.other), custom_call_target="tpu_custom_call" | custom-call | flops 400000 | bytes 1600000 | tf_op jit(solution)/shard_map/preparation/pallas_call | solution.py:364
  35.2 0.0 collective-permute-done.3.from_right
  35.2 3.6 %collective-permute-done.2.from_left = f32[6,64,128]{2,1,0:T(8,128)S(1)} collective-permute-done((f32[6,64,128]{2,1,0:T(8,128)S(1)}, f32[6,64,128]{2,1,0:T(8,128)S(1)}, u32[]{:S(2)}, u32[]{:S(2)}) %collective-permute-start.2) | collective-permute-done | bytes 196640 | tf_op jit(solution)/shard_map/ppermute | solution.py:437
  38.8 1.3 %copy-done.2 = bf16[2304,256]{1,0:T(8,128)(2,1)S(1)} copy-done((bf16[2304,256]{1,0:T(8,128)(2,1)S(1)}, bf16[2304,256]{1,0:T(8,128)(2,1)}, u32[]{:S(2)}) %copy-start.2) | copy-done | bytes 1179672
  40.0 22.0 %imaging.1 = (f32[1536,256]{1,0:T(8,128)}, f32[6,64,128]{2,1,0:T(8,128)S(1)}) custom-call(f32[6,64,128]{2,1,0:T(8,128)S(1)} %get-tuple-element.9.left, f32[6,64,128]{2,1,0:T(8,128)S(1)} %get-tuple-element.10.right, f32[6,64,128]{2,1,0:T(8,128)S(1)} %collective-permute-done.2.from_left, f32[6,64,128]{2,1,0:T(8,128)S(1)} %collective-permute-done.3.from_right, ...), custom_call_target="tpu_custom_call" | custom-call | tf_op jit(solution)/shard_map/imaging/pallas_call | solution.py:397
  62.1 1.9 %collective-permute-start.6 = (f32[6,64,128]{2,1,0:T(8,128)S(1)}, f32[6,64,128]{2,1,0:T(8,128)S(1)}, u32[]{:S(2)}, u32[]{:S(2)}) collective-permute-start(f32[6,64,128]{2,1,0:T(8,128)S(1)} %get-tuple-element.13.own), channel_id=1, source_target_pairs={{32,0},{64,32},{96,64},{128,96},{160,128},{192,160},{224,192},{33,... | collective-permute-start | bytes 589832 | tf_op jit(solution)/shard_map/ppermute | solution.py:437
  64.0 2.4 %collective-permute-start.5 = (f32[6,64,128]{2,1,0:T(8,128)S(1)}, f32[6,64,128]{2,1,0:T(8,128)S(1)}, u32[]{:S(2)}, u32[]{:S(2)}) collective-permute-start(f32[6,64,128]{2,1,0:T(8,128)S(1)} %get-tuple-element.13.own), channel_id=1, source_target_pairs={{0,32},{32,64},{64,96},{96,128},{128,160},{160,192},{192,224},{1,3... | collective-permute-start | bytes 589832 | tf_op jit(solution)/shard_map/ppermute | solution.py:437
  66.4 0.8 collective-permute-done.6.from_right
  67.1 3.8 %collective-permute-done.5.from_left = f32[6,64,128]{2,1,0:T(8,128)S(1)} collective-permute-done((f32[6,64,128]{2,1,0:T(8,128)S(1)}, f32[6,64,128]{2,1,0:T(8,128)S(1)}, u32[]{:S(2)}, u32[]{:S(2)}) %collective-permute-start.5) | collective-permute-done | bytes 196640 | tf_op jit(solution)/shard_map/ppermute | solution.py:437
  71.0 6.6 %collective-permute-start.7 = (f32[64,256]{1,0:T(8,128)S(1)}, f32[64,256]{1,0:T(8,128)S(1)}, u32[]{:S(2)}, u32[]{:S(2)}) collective-permute-start(f32[64,256]{1,0:T(8,128)S(1)} %pad_maximum_fusion), channel_id=1, source_target_pairs={{0,2},{2,4},{4,6},{6,8},{8,10},{10,12},{12,14},{14,16},{16,18},{18... | collective-permute-start | bytes 196616 | tf_op jit(solution)/shard_map/ppermute | solution.py:437
  77.6 1.9 %collective-permute-start.8 = (f32[64,256]{1,0:T(8,128)S(1)}, f32[64,256]{1,0:T(8,128)S(1)}, u32[]{:S(2)}, u32[]{:S(2)}) collective-permute-start(f32[64,256]{1,0:T(8,128)S(1)} %pad_maximum_fusion.1), channel_id=1, source_target_pairs={{2,0},{4,2},{6,4},{8,6},{10,8},{12,10},{14,12},{16,14},{18,16},{20... | collective-permute-start | bytes 196616 | tf_op jit(solution)/shard_map/ppermute | solution.py:437
  79.5 0.0 collective-permute-done.7.above
  79.5 6.3 %collective-permute-done.8.below = f32[64,256]{1,0:T(8,128)S(1)} collective-permute-done((f32[64,256]{1,0:T(8,128)S(1)}, f32[64,256]{1,0:T(8,128)S(1)}, u32[]{:S(2)}, u32[]{:S(2)}) %collective-permute-start.8) | collective-permute-done | bytes 65568 | tf_op jit(solution)/shard_map/ppermute | solution.py:437
  85.9 4.2 %synthesis.1 = f32[1536,256]{1,0:T(8,128)} custom-call(f32[6,64,128]{2,1,0:T(8,128)S(1)} %get-tuple-element.13.own, f32[6,64,128]{2,1,0:T(8,128)S(1)} %collective-permute-done.5.from_left, f32[6,64,128]{2,1,0:T(8,128)S(1)} %collective-permute-done.6.from_right, f32[64,256]{1,0:T(8,128)S(1)} %collective-permute-done.7.above, ...), custom_call_target="tpu_custom_call" | custom-call | tf_op jit(solution)/shard_map/synthesis/pallas_call | solution.py:422
  (16 shorter events, 0.1 us)
Async XLA Ops:
  0.6 33.6 %copy-start.5 = (f32[6,2,4096]{2,1,0:T(2,128)S(1)}, f32[6,2,4096]{2,1,0:T(2,128)}, u32[]{:S(2)}) copy-start(f32[6,2,4096]{2,1,0:T(2,128)} %own.1) | copy-start | bytes 589828
  1.7 21.8 %collective-permute-start.1 = (f32[128,256]{1,0:T(8,128)S(1)}, f32[128,256]{1,0:T(8,128)S(1)}, u32[]{:S(2)}, u32[]{:S(2)}) collective-permute-start(f32[128,256]{1,0:T(8,128)S(1)} %get-tuple-element.16), channel_id=1, source_target_pairs={{2,0},{4,2},{6,4},{8,6},{10,8},{12,10},{14,12},{16,14},{18,16},{20... | collective-permute-start | bytes 393224 | tf_op jit(solution)/shard_map/ppermute | solution.py:437
  4.4 19.1 %collective-permute-start = (f32[128,256]{1,0:T(8,128)S(1)}, f32[128,256]{1,0:T(8,128)S(1)}, u32[]{:S(2)}, u32[]{:S(2)}) collective-permute-start(f32[128,256]{1,0:T(8,128)S(1)} %get-tuple-element.17), channel_id=1, source_target_pairs={{0,2},{2,4},{4,6},{6,8},{8,10},{10,12},{12,14},{14,16},{16,18},{18... | collective-permute-start | bytes 393224 | tf_op jit(solution)/shard_map/ppermute | solution.py:437
  12.4 21.8 %collective-permute-start.4 = (f32[6,2,4096]{2,1,0:T(2,128)}, f32[6,2,4096]{2,1,0:T(2,128)S(1)}, u32[]{:S(2)}, u32[]{:S(2)}) collective-permute-start(f32[6,2,4096]{2,1,0:T(2,128)} %own.1), channel_id=1, source_target_pairs={{0,25},{1,24},{2,27},{3,26},{4,29},{5,28},{6,31},{7,30},{8,17},{9,... | collective-permute-start | bytes 589832 | tf_op jit(solution)/shard_map/ppermute | solution.py:449
  23.5 1.4 %copy-start = (f32[1536,256]{1,0:T(8,128)S(1)}, f32[1536,256]{1,0:T(8,128)}, u32[]{:S(2)}) copy-start(f32[1536,256]{1,0:T(8,128)} %mask.1) | copy-start | bytes 4718596
  24.9 1.0 %copy-start.4 = (bf16[1536,128]{1,0:T(8,128)(2,1)S(1)}, bf16[1536,128]{1,0:T(8,128)(2,1)}, u32[]{:S(2)}) copy-start(bf16[1536,128]{1,0:T(8,128)(2,1)} %constant.14.clone.tables) | copy-start | bytes 1179652
  25.9 12.8 %copy-start.1 = (s32[1536,256]{1,0:T(8,128)S(1)}, s32[1536,256]{1,0:T(8,128)}, u32[]{:S(2)}) copy-start(s32[1536,256]{1,0:T(8,128)} %target.1) | copy-start | bytes 4718596
  29.9 5.3 %collective-permute-start.3 = (f32[6,64,128]{2,1,0:T(8,128)S(1)}, f32[6,64,128]{2,1,0:T(8,128)S(1)}, u32[]{:S(2)}, u32[]{:S(2)}) collective-permute-start(f32[6,64,128]{2,1,0:T(8,128)S(1)} %get-tuple-element.9.left), channel_id=1, source_target_pairs={{32,0},{64,32},{96,64},{128,96},{160,128},{192,160},{224,192},{33,... | collective-permute-start | bytes 589832 | tf_op jit(solution)/shard_map/ppermute | solution.py:437
  31.8 7.0 %collective-permute-start.2 = (f32[6,64,128]{2,1,0:T(8,128)S(1)}, f32[6,64,128]{2,1,0:T(8,128)S(1)}, u32[]{:S(2)}, u32[]{:S(2)}) collective-permute-start(f32[6,64,128]{2,1,0:T(8,128)S(1)} %get-tuple-element.10.right), channel_id=1, source_target_pairs={{0,32},{32,64},{64,96},{96,128},{128,160},{160,192},{192,224},{1,3... | collective-permute-start | bytes 589832 | tf_op jit(solution)/shard_map/ppermute | solution.py:437
  38.8 1.3 %copy-start.2 = (bf16[2304,256]{1,0:T(8,128)(2,1)S(1)}, bf16[2304,256]{1,0:T(8,128)(2,1)}, u32[]{:S(2)}) copy-start(bf16[2304,256]{1,0:T(8,128)(2,1)} %constant.15.clone.wide) | copy-start | bytes 3538948
  40.0 30.9 %copy-start.6 = (f32[128]{0:T(128)S(1)}, f32[128]{0:T(128)}, u32[]{:S(2)}) copy-start(f32[128]{0:T(128)} %constant.16.clone) | copy-start | bytes 1540
  40.0 45.8 %copy-start.3 = (bf16[1536,128]{1,0:T(8,128)(2,1)S(1)}, bf16[1536,128]{1,0:T(8,128)(2,1)}, u32[]{:S(2)}) copy-start(bf16[1536,128]{1,0:T(8,128)(2,1)} %constant.17.clone.tables) | copy-start | bytes 1179652
  62.1 5.1 %collective-permute-start.6 = (f32[6,64,128]{2,1,0:T(8,128)S(1)}, f32[6,64,128]{2,1,0:T(8,128)S(1)}, u32[]{:S(2)}, u32[]{:S(2)}) collective-permute-start(f32[6,64,128]{2,1,0:T(8,128)S(1)} %get-tuple-element.13.own), channel_id=1, source_target_pairs={{32,0},{64,32},{96,64},{128,96},{160,128},{192,160},{224,192},{33,... | collective-permute-start | bytes 589832 | tf_op jit(solution)/shard_map/ppermute | solution.py:437
  64.0 7.0 %collective-permute-start.5 = (f32[6,64,128]{2,1,0:T(8,128)S(1)}, f32[6,64,128]{2,1,0:T(8,128)S(1)}, u32[]{:S(2)}, u32[]{:S(2)}) collective-permute-start(f32[6,64,128]{2,1,0:T(8,128)S(1)} %get-tuple-element.13.own), channel_id=1, source_target_pairs={{0,32},{32,64},{64,96},{96,128},{128,160},{160,192},{192,224},{1,3... | collective-permute-start | bytes 589832 | tf_op jit(solution)/shard_map/ppermute | solution.py:437
  71.0 8.5 %collective-permute-start.7 = (f32[64,256]{1,0:T(8,128)S(1)}, f32[64,256]{1,0:T(8,128)S(1)}, u32[]{:S(2)}, u32[]{:S(2)}) collective-permute-start(f32[64,256]{1,0:T(8,128)S(1)} %pad_maximum_fusion), channel_id=1, source_target_pairs={{0,2},{2,4},{4,6},{6,8},{8,10},{10,12},{12,14},{14,16},{16,18},{18... | collective-permute-start | bytes 196616 | tf_op jit(solution)/shard_map/ppermute | solution.py:437
  77.6 8.3 %collective-permute-start.8 = (f32[64,256]{1,0:T(8,128)S(1)}, f32[64,256]{1,0:T(8,128)S(1)}, u32[]{:S(2)}, u32[]{:S(2)}) collective-permute-start(f32[64,256]{1,0:T(8,128)S(1)} %pad_maximum_fusion.1), channel_id=1, source_target_pairs={{2,0},{4,2},{6,4},{8,6},{10,8},{12,10},{14,12},{16,14},{18,16},{20... | collective-permute-start | bytes 196616 | tf_op jit(solution)/shard_map/ppermute | solution.py:437
where the time goes:
time: 90.5 us; the launch traced here: 90.1 us
  Pallas kernels  31.1 us (34%)
  starting transfers between devices  27.1 us (30%)
  waiting for transfers between devices  14.5 us (16%)
  blocking collectives  8.98 us (10%)
  local copies, waits for them, and re-layouts  6.96 us (8%)
  between operations  1.46 us (2%)
    ppermute x8, starting transfers between devices, shifted(): return lax.ppermute(value, axis, pairs)  25.1 us
    pallas_call x1, Pallas kernels, imaging(): pl.pallas_call(imaging_kernel, grid=(tiles,), out_shape=(jax.ShapeDtypeSt...  22 us
    ppermute x8, waiting for transfers between devices, shifted(): return lax.ppermute(value, axis, pairs)  14.5 us
    unnamed x1, blocking collectives  8.98 us
    unnamed x17, local copies, waits for them, and re-layouts  5.81 us
    pallas_call x1, Pallas kernels, synthesis(): pl.pallas_call(synthesis_kernel, grid=(tiles,), out_shape=jax.ShapeDtypeS...  4.2 us
    pallas_call x1, Pallas kernels, analysis(): pl.pallas_call(analysis_kernel, grid=(tiles,), out_shape=(spectra, spectr...  3.91 us
    ppermute x1, starting transfers between devices, local(): other = lax.ppermute(kernels, ('gy', 'ka'), pairs)  1.98 us
  transfers between devices with their start and end apart: 9, of which 4 were waited for; matrix products, arithmetic and copies ran while one was open for 3% of the time, Pallas kernels for 5%

commit v1 on v0

--- a/solution.py
+++ b/solution.py
@@ -15,7 +15,7 @@
 TILE = 256
 COARSE = 128
 HALF = COARSE // 2
-VMEM_LIMIT = 48 * 1024 * 1024
+VMEM_LIMIT = 32 * 1024 * 1024
 
 bf16 = ml_dtypes.bfloat16
 
@@ -93,7 +93,16 @@
         "analysis": np.concatenate(columns + rows, axis=0),
         "synthesis": np.concatenate(pixs + outs, axis=0),
         "imaging": np.concatenate(
-            [spread, gather, lift, fold, as_right(interp.T), fine_left, coarse_left, coarse_right],
+            sum(
+                map(
+                    blocks,
+                    (
+                        spread, gather, lift, fold, as_right(interp.T), fine_left, coarse_left,
+                        coarse_right,
+                    ),
+                ),
+                [],
+            ),
             axis=0,
         ),
     }
@@ -101,7 +110,7 @@
 
 TABLES = make_tables()
 SPREAD, GATHER, LIFT, FOLD, FINE_RIGHT, FINE_LEFT, COARSE_LEFT, COARSE_RIGHT = (
-    slice(a, b)
+    (2 * a, b - a)
     for a, b in (
         (0, 384), (384, 640), (640, 768), (768, 896), (896, 1280), (1280, 1792), (1792, 2048),
         (2048, 2304),
@@ -154,6 +163,13 @@
     )
 
 
+def wide_table(packed, place):
+    start, size = place
+    return jnp.concatenate(
+        [packed[start : start + size, :], packed[start + size : start + 2 * size, :]], axis=1
+    )
+
+
 def parity(shape):
     index = lax.broadcasted_iota(jnp.int32, shape, 1)
     return (1 - 2 * (index % 2)).astype(jnp.float32)
@@ -172,23 +188,30 @@
     return pltpu.roll(value, FB, 1)
 
 
-def preparation_kernel(roots, own, other, straight, crossed, real, imag):
+def prelude_kernel(first, last, kernels, weights, first_out, last_out, packed, real, imag):
+    first_out[...] = first[...]
+    last_out[...] = last[...]
+    lanes = low_lanes((FB // 2, 2 * FB))
+    for index in range(kernels.shape[0]):
+        for row in range(FB // 2):
+            place = slice(row * 2 * FB, (row + 1) * 2 * FB)
+            real[row : row + 1, :] = kernels[index, 0:1, place]
+            imag[row : row + 1, :] = kernels[index, 1:2, place]
+        root = jnp.sqrt(jnp.full((FB // 2, 2 * FB), weights[index], jnp.float32))
+        re, im = root * real[...], root * imag[...]
+        packed[index, : FB // 2] = jnp.where(lanes, re, swapped(im))
+        packed[index, FB // 2 :] = jnp.where(lanes, swapped(re), im)
+
+
+def preparation_kernel(own, other, straight, crossed):
     count = own.shape[0]
-    lanes = low_lanes((FB // 2, 2 * FB))
+    lanes = low_lanes((FB, 2 * FB))
     for group, source in enumerate((own, other)):
         for index in range(count):
-            for row in range(FB // 2):
-                place = slice(row * 2 * FB, (row + 1) * 2 * FB)
-                real[row : row + 1, :] = source[index, 0:1, place]
-                imag[row : row + 1, :] = source[index, 1:2, place]
-            root = roots[group, index]
-            re, im = root * real[...], root * imag[...]
-            re_turned, im_turned = swapped(re), swapped(im)
-            at = group * count + index
-            straight[at, : FB // 2] = jnp.where(lanes, re, re_turned)
-            straight[at, FB // 2 :] = jnp.where(lanes, re_turned, re)
-            crossed[at, : FB // 2] = jnp.where(lanes, -im, im_turned)
-            crossed[at, FB // 2 :] = jnp.where(lanes, -im_turned, im)
+            spectrum = source[index]
+            turned = swapped(spectrum)
+            straight[group * count + index] = jnp.where(lanes, spectrum, turned)
+            crossed[group * count + index] = jnp.where(lanes, -turned, spectrum)
 
 
 def analysis_kernel(mask, above, below, tables, left, right, slope, total):
@@ -243,15 +266,15 @@
     spectrum = flip * (left[0] + right[0]) + from_left[0] + from_right[0]
     turned = swapped(spectrum)
 
-    def forward(group, carry):
+    for group in range(2):
         first = group * count
         products = [
             straight[first + i] * spectrum + crossed[first + i] * turned for i in range(count)
         ]
-        rows = times_table(jnp.concatenate(products, axis=0), wide[SPREAD, :])
+        rows = times_table(jnp.concatenate(products, axis=0), wide_table(wide, SPREAD))
         total = jnp.zeros((COARSE, COARSE), jnp.float32)
         for i in range(count):
-            both = table_times(wide[LIFT, :192], rows[i * FB : (i + 1) * FB])
+            both = table_times(wide_table(wide, LIFT)[:, :192], rows[i * FB : (i + 1) * FB])
             cosine, sine = both[:HALF], both[HALF:]
             sine_re, sine_im = sine[:, :COARSE], sine[:, COARSE:]
             cosine_re, cosine_im = cosine[:, :COARSE], cosine[:, COARSE:]
@@ -261,72 +284,53 @@
             fields[first + i, :, COARSE:] = imag
             total = total + (real * real + imag * imag)
         intensity[group] = total
-        return carry
-
-    lax.fori_loop(0, 2, forward, 0)
-
-    half_fine = times_table(intensity[0] + intensity[1], wide[FINE_RIGHT, :])
-    fine = stacked_times(wide[FINE_LEFT, :], half_fine)
+
+    half_fine = times_table(intensity[0] + intensity[1], wide_table(wide, FINE_RIGHT))
+    fine = stacked_times(wide_table(wide, FINE_LEFT), half_fine)
     resist = jax.nn.sigmoid(4.0 * (fine - 1.0))
     resist_ref[...] = resist
     misfit = resist - target[...].astype(jnp.float32)
     push = 16.0 * misfit * resist * (1.0 - resist)
     high, low = split(push)
-    from_high = dot(wide[COARSE_LEFT, :], high)
+    from_high = dot(wide_table(wide, COARSE_LEFT), high)
     half_coarse = from_high[:COARSE] + (
-        from_high[COARSE:] + dot(wide[COARSE_LEFT, :][:COARSE], low)
-    )
-    weight[...] = times_paired(half_coarse, wide[COARSE_RIGHT, :])
+        from_high[COARSE:] + dot(wide_table(wide, COARSE_LEFT)[:COARSE], low)
+    )
+    weight[...] = times_paired(half_coarse, wide_table(wide, COARSE_RIGHT))
 
     sign = jnp.where(low_lanes((HALF, 2 * FB)), 1.0, -1.0)
 
-    def backward(group, carry):
+    for group in range(2):
         first = group * count
         scale = jnp.concatenate([weight[...], weight[...]], axis=1)
         scaled = jnp.concatenate([fields[first + i] * scale for i in range(count)], axis=0)
-        sides[...] = times_paired(scaled, wide[GATHER, :])
+        sides[group] = times_paired(scaled, wide_table(wide, GATHER))
         total = jnp.zeros((FB, 2 * FB), jnp.float32)
         for i in range(0, count, 2):
             pair = []
             for j in (i, i + 1):
-                plus = sides[j * COARSE : j * COARSE + HALF, :]
-                minus = sides[j * COARSE + HALF : (j + 1) * COARSE, :]
+                plus = sides[group, j * COARSE : j * COARSE + HALF, :]
+                minus = sides[group, j * COARSE + HALF : (j + 1) * COARSE, :]
                 pair.append(
                     jnp.concatenate([plus + minus, sign * swapped(plus - minus)], axis=0)
                 )
-            found = stacked_times(wide[FOLD, :], jnp.concatenate(pair, axis=1))
+            found = stacked_times(wide_table(wide, FOLD), jnp.concatenate(pair, axis=1))
             for j in (0, 1):
                 part = found[:, j * 2 * FB : (j + 1) * 2 * FB]
                 total = total + (
                     straight[first + i + j] * part - crossed[first + i + j] * swapped(part)
                 )
         adjoint[group] = total
-        return carry
-
-    lax.fori_loop(0, 2, backward, 0)
+
     grad[0] = adjoint[0] + adjoint[1]
 
 
-def synthesis_kernel(own, from_left, from_right, above, below, slope, tables, result, mixed):
-    step = pl.program_id(0)
-    count = own.shape[0]
-    flip_col = parity((FB, 2 * FB))
-    flip_row = row_parity((FB, 4 * FB))
+def synthesis_block(upper, middle, lower, slope, tables):
     sign = jnp.where(low_lanes((FB, 2 * FB)), -1.0, 1.0)
-
-    @pl.when(step == 0)
-    def _():
-        mixed[0] = above[...]
-        mixed[count + 1] = below[...]
-        for index in range(count):
-            base = flip_col * own[index]
-            mixed[index + 1, :, : 2 * FB] = base + from_left[index]
-            mixed[index + 1, :, 2 * FB :] = base + from_right[index]
-
-    base = flip_row * mixed[step + 1]
+    base = row_parity((FB, 4 * FB)) * middle
     rows = []
-    for near, part in ((step, 0), (step + 2, 1)):
-        block = base + mixed[near]
+    for part, near in enumerate((upper, lower)):
+        block = base + near
         turned = [sign * swapped(block[:, : 2 * FB]), sign * swapped(block[:, 2 * FB :])]
         stacked = jnp.concatenate([block, jnp.concatenate(turned, axis=1)], axis=0)
         rows.append(table_times(row_table(tables, part), stacked))
@@ -336,7 +340,39 @@
         lanes = slice(side * 2 * FB, (side + 1) * 2 * FB)
         three = jnp.concatenate([high[:, lanes], low[:, lanes], high[:, lanes]], axis=1)
         sides.append(dot(three, col_table(tables, side)))
-    result[...] = jnp.concatenate(sides, axis=1) * slope[...]
+    return jnp.concatenate(sides, axis=1) * slope
+
+
+def mixed_row(own, from_left, from_right, index):
+    base = parity((FB, 2 * FB)) * own[index]
+    return jnp.concatenate([base + from_left[index], base + from_right[index]], axis=1)
+
+
+def inner_kernel(own, from_left, from_right, slope, tables, result, mixed):
+    step = pl.program_id(0)
+
+    @pl.when(step == 0)
+    def _():
+        for index in range(own.shape[0]):
+            mixed[index] = mixed_row(own, from_left, from_right, index)
+
+    result[...] = synthesis_block(
+        mixed[step], mixed[step + 1], mixed[step + 2], slope[...], tables
+    )
+
+
+def outer_kernel(own, from_left, from_right, above, below, slope, tables, partial, result):
+    del partial
+    last = own.shape[0] - 1
+    rows = [mixed_row(own, from_left, from_right, i) for i in (0, 1, last - 1, last)]
+
+    @pl.when(pl.program_id(0) == 0)
+    def _():
+        result[...] = synthesis_block(above[...], rows[0], rows[1], slope[...], tables)
+
+    @pl.when(pl.program_id(0) == 1)
+    def _():
+        result[...] = synthesis_block(rows[2], rows[3], below[...], slope[...], tables)
 
 
 def whole(array):
@@ -358,20 +394,40 @@
     )
 
 
-def preparation(roots, own, other):
+def prelude(mask, kernels, weights):
+    count = kernels.shape[0]
+    last = mask.shape[0] // HALO - 1
+    edge = jax.ShapeDtypeStruct((HALO, TILE), jnp.float32)
+    part = pltpu.VMEM((FB // 2, 2 * FB), jnp.float32)
+    packed = jax.ShapeDtypeStruct((count, FB, 2 * FB), jnp.float32)
+    return pl.pallas_call(
+        prelude_kernel,
+        grid=(1,),
+        out_shape=(edge, edge, packed),
+        in_specs=[
+            pl.BlockSpec((HALO, TILE), lambda step: (0, 0)),
+            pl.BlockSpec((HALO, TILE), lambda step: (last, 0)),
+            whole(kernels),
+            pl.BlockSpec(memory_space=pltpu.SMEM),
+        ],
+        out_specs=[whole(edge), whole(edge), whole(packed)],
+        scratch_shapes=[part, part],
+        compiler_params=params(),
+        name="prelude",
+    )(mask, mask, kernels, weights)
+
+
+def preparation(own, other):
     shape = jax.ShapeDtypeStruct((2 * own.shape[0], FB, 2 * FB), jnp.float32)
-    part = pltpu.VMEM((FB // 2, 2 * FB), jnp.float32)
     return pl.pallas_call(
         preparation_kernel,
         out_shape=(shape, shape),
-        in_specs=[pl.BlockSpec(memory_space=pltpu.SMEM)]
-        + [pl.BlockSpec(memory_space=pltpu.VMEM)] * 2,
+        in_specs=[pl.BlockSpec(memory_space=pltpu.VMEM)] * 2,
         out_specs=[pl.BlockSpec(memory_space=pltpu.VMEM)] * 2,
-        scratch_shapes=[part, part],
         compiler_params=pltpu.CompilerParams(vmem_limit_bytes=VMEM_LIMIT),
         cost_estimate=pl.CostEstimate(flops=400000, bytes_accessed=1600000, transcendentals=0),
         name="preparation",
-    )(roots, own, other)
+    )(own, other)
 
 
 def analysis(mask, above, below):
@@ -409,26 +465,47 @@
             pltpu.VMEM((2, COARSE, COARSE), jnp.float32),
             pltpu.VMEM((COARSE, COARSE), jnp.float32),
             pltpu.VMEM((2, FB, 2 * FB), jnp.float32),
-            pltpu.VMEM((kernels // 2 * COARSE, 2 * FB), jnp.float32),
+            pltpu.VMEM((2, kernels // 2 * COARSE, 2 * FB), jnp.float32),
         ],
         compiler_params=params(),
         name="imaging",
     )(left, right, from_left, from_right, straight, crossed, target, tables)
 
 
-def synthesis(own, from_left, from_right, above, below, slope):
+def inner_synthesis(own, from_left, from_right, slope):
     tiles = own.shape[0]
     tables = jnp.asarray(TABLES["synthesis"])
+    place = pl.BlockSpec((TILE, TILE), lambda step: (step + 1, 0))
     return pl.pallas_call(
-        synthesis_kernel,
-        grid=(tiles,),
+        inner_kernel,
+        grid=(tiles - 2,),
         out_shape=jax.ShapeDtypeStruct(slope.shape, jnp.float32),
-        in_specs=[whole(own)] * 3 + [whole(above), whole(below), tile_rows(), whole(tables)],
-        out_specs=tile_rows(),
-        scratch_shapes=[pltpu.VMEM((tiles + 2, FB, 4 * FB), jnp.float32)],
+        in_specs=[whole(own)] * 3 + [place, whole(tables)],
+        out_specs=place,
+        scratch_shapes=[pltpu.VMEM((tiles, FB, 4 * FB), jnp.float32)],
         compiler_params=params(),
-        name="synthesis",
-    )(own, from_left, from_right, above, below, slope, tables)
+        cost_estimate=pl.CostEstimate(
+            flops=1500000000, bytes_accessed=2500000, transcendentals=0
+        ),
+        name="inner_synthesis",
+    )(own, from_left, from_right, slope, tables)
+
+
+def outer_synthesis(own, from_left, from_right, above, below, slope, partial):
+    tiles = own.shape[0]
+    tables = jnp.asarray(TABLES["synthesis"])
+    place = pl.BlockSpec((TILE, TILE), lambda step: (step * (tiles - 1), 0))
+    return pl.pallas_call(
+        outer_kernel,
+        grid=(2,),
+        out_shape=jax.ShapeDtypeStruct(slope.shape, jnp.float32),
+        in_specs=[whole(own)] * 3
+        + [whole(above), whole(below), place, whole(tables), pl.BlockSpec(memory_space=pl.ANY)],
+        out_specs=place,
+        input_output_aliases={7: 0},
+        compiler_params=params(),
+        name="outer_synthesis",
+    )(own, from_left, from_right, above, below, slope, tables, partial)
 
 
 def shifted(value, axis, steps):
@@ -438,21 +515,20 @@
 
 
 def local(mask_param, target, kernels, weights):
-    above = shifted(mask_param[-HALO:], "gy", 1)
-    below = shifted(mask_param[:HALO], "gy", -1)
+    first, last, own = prelude(mask_param, kernels, weights)
+    above = shifted(last, "gy", 1)
+    below = shifted(first, "gy", -1)
     rows = lax.axis_size("gy")
     inner = rows // 4
     pairs = []
     for place in range(rows):
         mirror = (3 - place // inner) * inner + place % inner
         pairs += [(2 * place, 2 * mirror + 1), (2 * place + 1, 2 * mirror)]
-    other = lax.ppermute(kernels, ("gy", "ka"), pairs)
-    roots = jnp.sqrt(lax.all_gather(weights, "ka"))
-    roots = jnp.where(lax.axis_index("ka") == 0, roots, roots[::-1])
+    other = lax.ppermute(own, ("gy", "ka"), pairs)
     left, right, slope = analysis(mask_param, above, below)
     from_right = shifted(left, "gx", -1)
     from_left = shifted(right, "gx", 1)
-    straight, crossed = preparation(roots, kernels, other)
+    straight, crossed = preparation(own, other)
     resist, grad = imaging(left, right, from_left, from_right, straight, crossed, target)
     grad_left = shifted(grad, "gx", 1)
     grad_right = shifted(grad, "gx", -1)
@@ -465,7 +541,10 @@
 
     from_above = shifted(edge(-1), "gy", 1)
     from_below = shifted(edge(0), "gy", -1)
-    gradient = synthesis(grad, grad_left, grad_right, from_above, from_below, slope)
+    partial = inner_synthesis(grad, grad_left, grad_right, slope)
+    gradient = outer_synthesis(
+        grad, grad_left, grad_right, from_above, from_below, slope, partial
+    )
     return (gradient, resist)
 
 

time: 90.5 us -> 72.8 us (0.80)
  the two profiles are of different devices: /device:TPU:22 before, /device:TPU:40 now
where the time goes in v1:
time: 72.8 us; the launch traced here: 71.5 us
  starting transfers between devices  30.6 us (42%)
  Pallas kernels  28.1 us (39%)
  waiting for transfers between devices  8.98 us (12%)
  local copies, waits for them, and re-layouts  3 us (4%)
  between operations  0.79 us (1%)
    ppermute x8, starting transfers between devices, shifted(): return lax.ppermute(value, axis, pairs)  24.7 us
    pallas_call x1, Pallas kernels, imaging(): pl.pallas_call(imaging_kernel, grid=(tiles,), out_shape=(jax.ShapeDtypeSt...  18.4 us
    ppermute x8, waiting for transfers between devices, shifted(): return lax.ppermute(value, axis, pairs)  8.97 us
    ppermute x1, starting transfers between devices, local(): other = lax.ppermute(own, ('gy', 'ka'), pairs)  5.93 us
    pallas_call x1, Pallas kernels, analysis(): pl.pallas_call(analysis_kernel, grid=(tiles,), out_shape=(spectra, spectr...  3.93 us
    unnamed x16, local copies, waits for them, and re-layouts  3 us
    pallas_call x1, Pallas kernels, inner_synthesis(): pl.pallas_call(inner_kernel, grid=(tiles - 2,), out_shape=jax.ShapeDtypeS...  3 us
    pallas_call x1, Pallas kernels, outer_synthesis(): pl.pallas_call(outer_kernel, grid=(2,), out_shape=jax.ShapeDtypeStruct(sl...  1.8 us
  transfers between devices with their start and end apart: 9, of which 4 were waited for; matrix products, arithmetic and copies ran while one was open for 0% of the time, Pallas kernels for 10%

profile of v1, /device:TPU:40, one launch (start us, length us, event | category | flops | bytes accessed | tf_op | source)
XLA Modules:
  0.0 71.5 jit_solution(9353049793393560536)
XLA Ops:
  0.6 0.0 copy-start
  0.6 1.4 %copy-done = f32[1536,256]{1,0:T(8,128)S(1)} copy-done((f32[1536,256]{1,0:T(8,128)S(1)}, f32[1536,256]{1,0:T(8,128)}, u32[]{:S(2)}) %copy-start) | copy-done | bytes 1572888
  2.0 0.9 %copy-done.5 = f32[6,2,4096]{2,1,0:T(2,128)S(1)} copy-done((f32[6,2,4096]{2,1,0:T(2,128)S(1)}, f32[6,2,4096]{2,1,0:T(2,128)}, u32[]{:S(2)}) %copy-start.5) | copy-done | bytes 196632
  3.0 0.7 copy-done.6
  3.6 0.8 %prelude.1 = (f32[128,256]{1,0:T(8,128)S(1)}, f32[128,256]{1,0:T(8,128)S(1)}, f32[6,64,128]{2,1,0:T(8,128)S(1)}) custom-call(f32[1536,256]{1,0:T(8,128)S(1)} %copy-done, f32[1536,256]{1,0:T(8,128)S(1)} %copy-done, f32[6,2,4096]{2,1,0:T(2,128)S(1)} %copy-done.5, f32[6]{0:T(128)S(1)} %copy-done.6), custom_call_target="tpu_custom_call" | custom-call | tf_op jit(solution)/shard_map/prelude/pallas_call | solution.py:403
  4.4 3.5 %collective-permute-start = (f32[128,256]{1,0:T(8,128)S(1)}, f32[128,256]{1,0:T(8,128)S(1)}, u32[]{:S(2)}, u32[]{:S(2)}) collective-permute-start(f32[128,256]{1,0:T(8,128)S(1)} %get-tuple-element.12), channel_id=1, source_target_pairs={{0,2},{2,4},{4,6},{6,8},{8,10},{10,12},{12,14},{14,16},{16,18},{18... | collective-permute-start | bytes 393224 | tf_op jit(solution)/shard_map/ppermute | solution.py:514
  7.9 4.6 %collective-permute-start.1 = (f32[128,256]{1,0:T(8,128)S(1)}, f32[128,256]{1,0:T(8,128)S(1)}, u32[]{:S(2)}, u32[]{:S(2)}) collective-permute-start(f32[128,256]{1,0:T(8,128)S(1)} %get-tuple-element.13), channel_id=1, source_target_pairs={{2,0},{4,2},{6,4},{8,6},{10,8},{12,10},{14,12},{16,14},{18,16},{20... | collective-permute-start | bytes 393224 | tf_op jit(solution)/shard_map/ppermute | solution.py:514
  12.5 5.9 %collective-permute-start.4 = (f32[6,64,128]{2,1,0:T(8,128)S(1)}, f32[6,64,128]{2,1,0:T(8,128)S(1)}, u32[]{:S(2)}, u32[]{:S(2)}) collective-permute-start(f32[6,64,128]{2,1,0:T(8,128)S(1)} %get-tuple-element.16.own), channel_id=1, source_target_pairs={{0,25},{1,24},{2,27},{3,26},{4,29},{5,28},{6,31},{7,30},{8,17},{9,... | collective-permute-start | bytes 589832 | tf_op jit(solution)/shard_map/ppermute | solution.py:527
  18.4 0.0 collective-permute-done.above
  18.4 0.0 collective-permute-done.1.below
  18.4 0.0 copy-done.4
  18.4 3.9 %analysis.1 = (f32[6,64,128]{2,1,0:T(8,128)S(1)}, f32[6,64,128]{2,1,0:T(8,128)S(1)}, f32[1536,256]{1,0:T(8,128)S(1)}) custom-call(f32[1536,256]{1,0:T(8,128)S(1)} %copy-done, f32[128,256]{1,0:T(8,128)S(1)} %collective-permute-done.above, f32[128,256]{1,0:T(8,128)S(1)} %collective-permute-done.1.below, bf16[1536,128]{1,0:T(8,128)(2,1)S(1)} %copy-done.4), custom_call_target="tpu_custom_call" | custom-call | tf_op jit(solution)/shard_map/analysis/pallas_call | solution.py:437
  22.4 1.9 %collective-permute-start.3 = (f32[6,64,128]{2,1,0:T(8,128)S(1)}, f32[6,64,128]{2,1,0:T(8,128)S(1)}, u32[]{:S(2)}, u32[]{:S(2)}) collective-permute-start(f32[6,64,128]{2,1,0:T(8,128)S(1)} %get-tuple-element.14.left), channel_id=1, source_target_pairs={{32,0},{64,32},{96,64},{128,96},{160,128},{192,160},{224,192},{33,... | collective-permute-start | bytes 589832 | tf_op jit(solution)/shard_map/ppermute | solution.py:514
  24.3 2.4 %collective-permute-start.2 = (f32[6,64,128]{2,1,0:T(8,128)S(1)}, f32[6,64,128]{2,1,0:T(8,128)S(1)}, u32[]{:S(2)}, u32[]{:S(2)}) collective-permute-start(f32[6,64,128]{2,1,0:T(8,128)S(1)} %get-tuple-element.15.right), channel_id=1, source_target_pairs={{0,32},{32,64},{64,96},{96,128},{128,160},{160,192},{192,224},{1,3... | collective-permute-start | bytes 589832 | tf_op jit(solution)/shard_map/ppermute | solution.py:514
  26.7 0.0 collective-permute-done.4.other
  26.7 0.2 preparation.1
  26.9 0.6 collective-permute-done.3.from_right
  27.5 3.8 %collective-permute-done.2.from_left = f32[6,64,128]{2,1,0:T(8,128)S(1)} collective-permute-done((f32[6,64,128]{2,1,0:T(8,128)S(1)}, f32[6,64,128]{2,1,0:T(8,128)S(1)}, u32[]{:S(2)}, u32[]{:S(2)}) %collective-permute-start.2) | collective-permute-done | bytes 196640 | tf_op jit(solution)/shard_map/ppermute | solution.py:514
  31.3 0.0 copy-done.2
  31.3 0.0 copy-done.1
  31.3 18.4 %imaging.1 = (f32[1536,256]{1,0:T(8,128)}, f32[6,64,128]{2,1,0:T(8,128)S(1)}) custom-call(f32[6,64,128]{2,1,0:T(8,128)S(1)} %get-tuple-element.14.left, f32[6,64,128]{2,1,0:T(8,128)S(1)} %get-tuple-element.15.right, f32[6,64,128]{2,1,0:T(8,128)S(1)} %collective-permute-done.2.from_left, f32[6,64,128]{2,1,0:T(8,128)S(1)} %collective-permute-done.3.from_right, ...), custom_call_target="tpu_custom_call" | custom-call | tf_op jit(solution)/shard_map/imaging/pallas_call | solution.py:453
  49.7 1.9 %collective-permute-start.6 = (f32[6,64,128]{2,1,0:T(8,128)S(1)}, f32[6,64,128]{2,1,0:T(8,128)S(1)}, u32[]{:S(2)}, u32[]{:S(2)}) collective-permute-start(f32[6,64,128]{2,1,0:T(8,128)S(1)} %get-tuple-element.19.own), channel_id=1, source_target_pairs={{32,0},{64,32},{96,64},{128,96},{160,128},{192,160},{224,192},{33,... | collective-permute-start | bytes 589832 | tf_op jit(solution)/shard_map/ppermute | solution.py:514
  51.6 2.4 %collective-permute-start.5 = (f32[6,64,128]{2,1,0:T(8,128)S(1)}, f32[6,64,128]{2,1,0:T(8,128)S(1)}, u32[]{:S(2)}, u32[]{:S(2)}) collective-permute-start(f32[6,64,128]{2,1,0:T(8,128)S(1)} %get-tuple-element.19.own), channel_id=1, source_target_pairs={{0,32},{32,64},{64,96},{96,128},{128,160},{160,192},{192,224},{1,3... | collective-permute-start | bytes 589832 | tf_op jit(solution)/shard_map/ppermute | solution.py:514
  54.1 0.8 %collective-permute-done.6.from_right = f32[6,64,128]{2,1,0:T(8,128)S(1)} collective-permute-done((f32[6,64,128]{2,1,0:T(8,128)S(1)}, f32[6,64,128]{2,1,0:T(8,128)S(1)}, u32[]{:S(2)}, u32[]{:S(2)}) %collective-permute-start.6) | collective-permute-done | bytes 196640 | tf_op jit(solution)/shard_map/ppermute | solution.py:514
  54.8 3.8 %collective-permute-done.5.from_left = f32[6,64,128]{2,1,0:T(8,128)S(1)} collective-permute-done((f32[6,64,128]{2,1,0:T(8,128)S(1)}, f32[6,64,128]{2,1,0:T(8,128)S(1)}, u32[]{:S(2)}, u32[]{:S(2)}) %collective-permute-start.5) | collective-permute-done | bytes 196640 | tf_op jit(solution)/shard_map/ppermute | solution.py:514
  58.6 0.0 copy-done.7
  58.7 1.9 %collective-permute-start.7 = (f32[64,256]{1,0:T(8,128)S(1)}, f32[64,256]{1,0:T(8,128)S(1)}, u32[]{:S(2)}, u32[]{:S(2)}) collective-permute-start(f32[64,256]{1,0:T(8,128)S(1)} %pad_maximum_fusion), channel_id=1, source_target_pairs={{0,2},{2,4},{4,6},{6,8},{8,10},{10,12},{12,14},{14,16},{16,18},{18... | collective-permute-start | bytes 196616 | tf_op jit(solution)/shard_map/ppermute | solution.py:514
  60.6 6.0 %collective-permute-start.8 = (f32[64,256]{1,0:T(8,128)S(1)}, f32[64,256]{1,0:T(8,128)S(1)}, u32[]{:S(2)}, u32[]{:S(2)}) collective-permute-start(f32[64,256]{1,0:T(8,128)S(1)} %pad_maximum_fusion.1), channel_id=1, source_target_pairs={{2,0},{4,2},{6,4},{8,6},{10,8},{12,10},{14,12},{16,14},{18,16},{20... | collective-permute-start | bytes 196616 | tf_op jit(solution)/shard_map/ppermute | solution.py:514
  66.7 3.0 %inner_synthesis.1.partial = f32[1536,256]{1,0:T(8,128)} custom-call(f32[6,64,128]{2,1,0:T(8,128)S(1)} %get-tuple-element.19.own, f32[6,64,128]{2,1,0:T(8,128)S(1)} %collective-permute-done.5.from_left, f32[6,64,128]{2,1,0:T(8,128)S(1)} %collective-permute-done.6.from_right, f32[1536,256]{1,0:T(8,128)S(1)} %get-tuple-element.20.slope, ...), custom_call_target="tpu_custom_call" | custom-call | flops 1500000000 | bytes 2500000 | tf_op jit(solution)/shard_map/inner_synthesis/pallas_call | solution.py:479
  69.7 0.0 collective-permute-done.7.above
  69.7 0.0 collective-permute-done.8.below
  69.7 1.8 %outer_synthesis.1 = f32[1536,256]{1,0:T(8,128)} custom-call(f32[6,64,128]{2,1,0:T(8,128)S(1)} %get-tuple-element.19.own, f32[6,64,128]{2,1,0:T(8,128)S(1)} %collective-permute-done.5.from_left, f32[6,64,128]{2,1,0:T(8,128)S(1)} %collective-permute-done.6.from_right, f32[64,256]{1,0:T(8,128)S(1)} %collective-permute-done.7.above, ...), custom_call_target="tpu_custom_call", output_to_operand_aliasing={{}: (7, {})} | custom-call | tf_op jit(solution)/shard_map/outer_synthesis/pallas_call | solution.py:498
  (11 shorter events, 0.0 us)
Async XLA Ops:
  0.6 1.4 %copy-start = (f32[1536,256]{1,0:T(8,128)S(1)}, f32[1536,256]{1,0:T(8,128)}, u32[]{:S(2)}) copy-start(f32[1536,256]{1,0:T(8,128)} %mask.1) | copy-start | bytes 4718596
  2.0 0.9 %copy-start.5 = (f32[6,2,4096]{2,1,0:T(2,128)S(1)}, f32[6,2,4096]{2,1,0:T(2,128)}, u32[]{:S(2)}) copy-start(f32[6,2,4096]{2,1,0:T(2,128)} %kernels.1) | copy-start | bytes 589828
  3.0 0.7 copy-start.6
  3.6 14.8 %copy-start.4 = (bf16[1536,128]{1,0:T(8,128)(2,1)S(1)}, bf16[1536,128]{1,0:T(8,128)(2,1)}, u32[]{:S(2)}) copy-start(bf16[1536,128]{1,0:T(8,128)(2,1)} %constant.8.clone.tables) | copy-start | bytes 1179652
  3.6 27.7 %copy-start.2 = (bf16[4608,128]{1,0:T(8,128)(2,1)S(1)}, bf16[4608,128]{1,0:T(8,128)(2,1)}, u32[]{:S(2)}) copy-start(bf16[4608,128]{1,0:T(8,128)(2,1)} %constant.9.clone.wide) | copy-start | bytes 3538948
  4.4 26.9 %copy-start.1 = (s32[1536,256]{1,0:T(8,128)S(1)}, s32[1536,256]{1,0:T(8,128)}, u32[]{:S(2)}) copy-start(s32[1536,256]{1,0:T(8,128)} %target.1) | copy-start | bytes 4718596
  4.4 14.0 %collective-permute-start = (f32[128,256]{1,0:T(8,128)S(1)}, f32[128,256]{1,0:T(8,128)S(1)}, u32[]{:S(2)}, u32[]{:S(2)}) collective-permute-start(f32[128,256]{1,0:T(8,128)S(1)} %get-tuple-element.12), channel_id=1, source_target_pairs={{0,2},{2,4},{4,6},{6,8},{8,10},{10,12},{12,14},{14,16},{16,18},{18... | collective-permute-start | bytes 393224 | tf_op jit(solution)/shard_map/ppermute | solution.py:514
  7.9 10.5 %collective-permute-start.1 = (f32[128,256]{1,0:T(8,128)S(1)}, f32[128,256]{1,0:T(8,128)S(1)}, u32[]{:S(2)}, u32[]{:S(2)}) collective-permute-start(f32[128,256]{1,0:T(8,128)S(1)} %get-tuple-element.13), channel_id=1, source_target_pairs={{2,0},{4,2},{6,4},{8,6},{10,8},{12,10},{14,12},{16,14},{18,16},{20... | collective-permute-start | bytes 393224 | tf_op jit(solution)/shard_map/ppermute | solution.py:514
  12.5 14.2 %collective-permute-start.4 = (f32[6,64,128]{2,1,0:T(8,128)S(1)}, f32[6,64,128]{2,1,0:T(8,128)S(1)}, u32[]{:S(2)}, u32[]{:S(2)}) collective-permute-start(f32[6,64,128]{2,1,0:T(8,128)S(1)} %get-tuple-element.16.own), channel_id=1, source_target_pairs={{0,25},{1,24},{2,27},{3,26},{4,29},{5,28},{6,31},{7,30},{8,17},{9,... | collective-permute-start | bytes 589832 | tf_op jit(solution)/shard_map/ppermute | solution.py:527
  22.4 5.1 %collective-permute-start.3 = (f32[6,64,128]{2,1,0:T(8,128)S(1)}, f32[6,64,128]{2,1,0:T(8,128)S(1)}, u32[]{:S(2)}, u32[]{:S(2)}) collective-permute-start(f32[6,64,128]{2,1,0:T(8,128)S(1)} %get-tuple-element.14.left), channel_id=1, source_target_pairs={{32,0},{64,32},{96,64},{128,96},{160,128},{192,160},{224,192},{33,... | collective-permute-start | bytes 589832 | tf_op jit(solution)/shard_map/ppermute | solution.py:514
  24.3 7.0 %collective-permute-start.2 = (f32[6,64,128]{2,1,0:T(8,128)S(1)}, f32[6,64,128]{2,1,0:T(8,128)S(1)}, u32[]{:S(2)}, u32[]{:S(2)}) collective-permute-start(f32[6,64,128]{2,1,0:T(8,128)S(1)} %get-tuple-element.15.right), channel_id=1, source_target_pairs={{0,32},{32,64},{64,96},{96,128},{128,160},{160,192},{192,224},{1,3... | collective-permute-start | bytes 589832 | tf_op jit(solution)/shard_map/ppermute | solution.py:514
  31.3 27.3 %copy-start.7 = (f32[128]{0:T(128)S(1)}, f32[128]{0:T(128)}, u32[]{:S(2)}) copy-start(f32[128]{0:T(128)} %constant.10.clone) | copy-start | bytes 1540
  31.3 35.3 %copy-start.3 = (bf16[1536,128]{1,0:T(8,128)(2,1)S(1)}, bf16[1536,128]{1,0:T(8,128)(2,1)}, u32[]{:S(2)}) copy-start(bf16[1536,128]{1,0:T(8,128)(2,1)} %constant.11.clone.tables) | copy-start | bytes 1179652
  49.7 5.1 %collective-permute-start.6 = (f32[6,64,128]{2,1,0:T(8,128)S(1)}, f32[6,64,128]{2,1,0:T(8,128)S(1)}, u32[]{:S(2)}, u32[]{:S(2)}) collective-permute-start(f32[6,64,128]{2,1,0:T(8,128)S(1)} %get-tuple-element.19.own), channel_id=1, source_target_pairs={{32,0},{64,32},{96,64},{128,96},{160,128},{192,160},{224,192},{33,... | collective-permute-start | bytes 589832 | tf_op jit(solution)/shard_map/ppermute | solution.py:514
  51.6 7.0 %collective-permute-start.5 = (f32[6,64,128]{2,1,0:T(8,128)S(1)}, f32[6,64,128]{2,1,0:T(8,128)S(1)}, u32[]{:S(2)}, u32[]{:S(2)}) collective-permute-start(f32[6,64,128]{2,1,0:T(8,128)S(1)} %get-tuple-element.19.own), channel_id=1, source_target_pairs={{0,32},{32,64},{64,96},{96,128},{128,160},{160,192},{192,224},{1,3... | collective-permute-start | bytes 589832 | tf_op jit(solution)/shard_map/ppermute | solution.py:514
  58.7 11.0 %collective-permute-start.7 = (f32[64,256]{1,0:T(8,128)S(1)}, f32[64,256]{1,0:T(8,128)S(1)}, u32[]{:S(2)}, u32[]{:S(2)}) collective-permute-start(f32[64,256]{1,0:T(8,128)S(1)} %pad_maximum_fusion), channel_id=1, source_target_pairs={{0,2},{2,4},{4,6},{6,8},{8,10},{10,12},{12,14},{14,16},{16,18},{18... | collective-permute-start | bytes 196616 | tf_op jit(solution)/shard_map/ppermute | solution.py:514
  60.6 9.1 %collective-permute-start.8 = (f32[64,256]{1,0:T(8,128)S(1)}, f32[64,256]{1,0:T(8,128)S(1)}, u32[]{:S(2)}, u32[]{:S(2)}) collective-permute-start(f32[64,256]{1,0:T(8,128)S(1)} %pad_maximum_fusion.1), channel_id=1, source_target_pairs={{2,0},{4,2},{6,4},{8,6},{10,8},{12,10},{14,12},{16,14},{18,16},{20... | collective-permute-start | bytes 196616 | tf_op jit(solution)/shard_map/ppermute | solution.py:514

commit v2 on v1

--- a/solution.py
+++ b/solution.py
@@ -16,6 +16,8 @@
 COARSE = 128
 HALF = COARSE // 2
 VMEM_LIMIT = 32 * 1024 * 1024
+PAIR = 2
+PRELUDE_LIMIT = 63 * 1024 * 1024
 
 bf16 = ml_dtypes.bfloat16
 
@@ -188,9 +190,10 @@
     return pltpu.roll(value, FB, 1)
 
 
-def prelude_kernel(first, last, kernels, weights, first_out, last_out, packed, real, imag):
-    first_out[...] = first[...]
-    last_out[...] = last[...]
+def prelude_kernel(odd, first, last, kernels, weights, even_out, odd_out, packed, real, imag):
+    odd_row = odd[0] == 1
+    even_out[...] = jnp.where(odd_row, first[...], last[...])
+    odd_out[...] = jnp.where(odd_row, last[...], first[...])
     lanes = low_lanes((FB // 2, 2 * FB))
     for index in range(kernels.shape[0]):
         for row in range(FB // 2):
@@ -214,9 +217,11 @@
             crossed[group * count + index] = jnp.where(lanes, -turned, spectrum)
 
 
-def analysis_kernel(mask, above, below, tables, left, right, slope, total):
+def analysis_kernel(
+    odd, mask, halo_even, halo_odd, tables, share, to_even, to_odd, slope, total
+):
     step = pl.program_id(0)
-    count = left.shape[0]
+    count = share.shape[0]
     sign = jnp.where(low_lanes((FB, 2 * FB)), 1.0, -1.0)
     flip = row_parity((FB, 4 * FB))
 
@@ -238,7 +243,10 @@
 
     @pl.when(step == 0)
     def _():
-        outer = jnp.concatenate([below[...], above[...]], axis=0)
+        odd_row = odd[0] == 1
+        below = jnp.where(odd_row, halo_odd[...], halo_even[...])
+        above = jnp.where(odd_row, halo_even[...], halo_odd[...])
+        outer = jnp.concatenate([below, above], axis=0)
         upper, lower = spectra(jnp.tanh(outer))
         total[...] = jnp.zeros_like(total)
         total[1] = lower
@@ -253,76 +261,101 @@
 
     @pl.when(step == count - 1)
     def _():
-        left[...] = total[1 : count + 1, :, : 2 * FB]
-        right[...] = total[1 : count + 1, :, 2 * FB :]
+        odd_col = odd[1] == 1
+        for index in range(count):
+            left, right = total[index + 1, :, : 2 * FB], total[index + 1, :, 2 * FB :]
+            share[index] = parity((FB, 2 * FB)) * (left + right)
+            to_even[index] = jnp.where(odd_col, left, right)
+            to_odd[index] = jnp.where(odd_col, right, left)
 
 
 def imaging_kernel(
-    left, right, from_left, from_right, straight, crossed, target, wide,
-    resist_ref, grad, fields, intensity, weight, adjoint, sides,
+    share, from_even, from_odd, straight, crossed, target, wide,
+    resist_ref, grad, fields, sides,
 ):
     count = straight.shape[0] // 2
-    flip = parity((FB, 2 * FB))
-    spectrum = flip * (left[0] + right[0]) + from_left[0] + from_right[0]
-    turned = swapped(spectrum)
-
-    for group in range(2):
-        first = group * count
-        products = [
-            straight[first + i] * spectrum + crossed[first + i] * turned for i in range(count)
-        ]
-        rows = times_table(jnp.concatenate(products, axis=0), wide_table(wide, SPREAD))
-        total = jnp.zeros((COARSE, COARSE), jnp.float32)
-        for i in range(count):
-            both = table_times(wide_table(wide, LIFT)[:, :192], rows[i * FB : (i + 1) * FB])
-            cosine, sine = both[:HALF], both[HALF:]
-            sine_re, sine_im = sine[:, :COARSE], sine[:, COARSE:]
-            cosine_re, cosine_im = cosine[:, :COARSE], cosine[:, COARSE:]
-            real = jnp.concatenate([cosine_re - sine_im, cosine_re + sine_im], axis=0)
-            imag = jnp.concatenate([cosine_im + sine_re, cosine_im - sine_re], axis=0)
-            fields[first + i, :, :COARSE] = real
-            fields[first + i, :, COARSE:] = imag
-            total = total + (real * real + imag * imag)
-        intensity[group] = total
-
-    half_fine = times_table(intensity[0] + intensity[1], wide_table(wide, FINE_RIGHT))
-    fine = stacked_times(wide_table(wide, FINE_LEFT), half_fine)
-    resist = jax.nn.sigmoid(4.0 * (fine - 1.0))
-    resist_ref[...] = resist
-    misfit = resist - target[...].astype(jnp.float32)
-    push = 16.0 * misfit * resist * (1.0 - resist)
-    high, low = split(push)
-    from_high = dot(wide_table(wide, COARSE_LEFT), high)
-    half_coarse = from_high[:COARSE] + (
-        from_high[COARSE:] + dot(wide_table(wide, COARSE_LEFT)[:COARSE], low)
-    )
-    weight[...] = times_paired(half_coarse, wide_table(wide, COARSE_RIGHT))
-
     sign = jnp.where(low_lanes((HALF, 2 * FB)), 1.0, -1.0)
-
-    for group in range(2):
-        first = group * count
-        scale = jnp.concatenate([weight[...], weight[...]], axis=1)
-        scaled = jnp.concatenate([fields[first + i] * scale for i in range(count)], axis=0)
-        sides[group] = times_paired(scaled, wide_table(wide, GATHER))
-        total = jnp.zeros((FB, 2 * FB), jnp.float32)
-        for i in range(0, count, 2):
-            pair = []
-            for j in (i, i + 1):
-                plus = sides[group, j * COARSE : j * COARSE + HALF, :]
-                minus = sides[group, j * COARSE + HALF : (j + 1) * COARSE, :]
-                pair.append(
-                    jnp.concatenate([plus + minus, sign * swapped(plus - minus)], axis=0)
+    tiles = range(PAIR)
+    weights = []
+    intensities = [[] for tile in tiles]
+
+    for tile in tiles:
+        spectrum = share[tile] + from_even[tile] + from_odd[tile]
+        turned = swapped(spectrum)
+        for group in range(2):
+            first = group * count
+            products = [
+                straight[first + i] * spectrum + crossed[first + i] * turned
+                for i in range(count)
+            ]
+            rows = times_table(jnp.concatenate(products, axis=0), wide_table(wide, SPREAD))
+            total = jnp.zeros((COARSE, COARSE), jnp.float32)
+            for i in range(count):
+                both = table_times(
+                    wide_table(wide, LIFT)[:, :192], rows[i * FB : (i + 1) * FB]
                 )
-            found = stacked_times(wide_table(wide, FOLD), jnp.concatenate(pair, axis=1))
-            for j in (0, 1):
-                part = found[:, j * 2 * FB : (j + 1) * 2 * FB]
-                total = total + (
-                    straight[first + i + j] * part - crossed[first + i + j] * swapped(part)
+                cosine, sine = both[:HALF], both[HALF:]
+                sine_re, sine_im = sine[:, :COARSE], sine[:, COARSE:]
+                cosine_re, cosine_im = cosine[:, :COARSE], cosine[:, COARSE:]
+                real = jnp.concatenate([cosine_re - sine_im, cosine_re + sine_im], axis=0)
+                imag = jnp.concatenate([cosine_im + sine_re, cosine_im - sine_re], axis=0)
+                fields[tile, first + i, :, :COARSE] = real
+                fields[tile, first + i, :, COARSE:] = imag
+                total = total + (real * real + imag * imag)
+            intensities[tile].append(total)
+
+    for tile in tiles:
+        intensity = intensities[tile][0] + intensities[tile][1]
+        half_fine = times_table(intensity, wide_table(wide, FINE_RIGHT))
+        fine = stacked_times(wide_table(wide, FINE_LEFT), half_fine)
+        resist = jax.nn.sigmoid(4.0 * (fine - 1.0))
+        place = slice(tile * TILE, (tile + 1) * TILE)
+        resist_ref[place, :] = resist
+        misfit = resist - target[place, :].astype(jnp.float32)
+        push = 16.0 * misfit * resist * (1.0 - resist)
+        high, low = split(push)
+        from_high = dot(wide_table(wide, COARSE_LEFT), high)
+        half_coarse = from_high[:COARSE] + (
+            from_high[COARSE:] + dot(wide_table(wide, COARSE_LEFT)[:COARSE], low)
+        )
+        weights.append(times_paired(half_coarse, wide_table(wide, COARSE_RIGHT)))
+
+    for tile in tiles:
+        scale = jnp.concatenate([weights[tile], weights[tile]], axis=1)
+        adjoint = []
+        for group in range(2):
+            first = group * count
+            scaled = jnp.concatenate(
+                [fields[tile, first + i] * scale for i in range(count)], axis=0
+            )
+            sides[tile, group] = times_paired(scaled, wide_table(wide, GATHER))
+            total = jnp.zeros((FB, 2 * FB), jnp.float32)
+            for i in range(0, count, 2):
+                pair = []
+                for j in (i, i + 1):
+                    plus = sides[tile, group, j * COARSE : j * COARSE + HALF, :]
+                    minus = sides[tile, group, j * COARSE + HALF : (j + 1) * COARSE, :]
+                    pair.append(
+                        jnp.concatenate([plus + minus, sign * swapped(plus - minus)], axis=0)
+                    )
+                found = stacked_times(
+                    wide_table(wide, FOLD), jnp.concatenate(pair, axis=1)
                 )
-        adjoint[group] = total
-
-    grad[0] = adjoint[0] + adjoint[1]
+                for j in (0, 1):
+                    part = found[:, j * 2 * FB : (j + 1) * 2 * FB]
+                    total = total + (
+                        straight[first + i + j] * part - crossed[first + i + j] * swapped(part)
+                    )
+            adjoint.append(total)
+        grad[tile] = adjoint[0] + adjoint[1]
+
+
+def sides_of(odd, even_in, odd_in, index):
+    odd_col = odd[1] == 1
+    return (
+        jnp.where(odd_col, even_in[index], odd_in[index]),
+        jnp.where(odd_col, odd_in[index], even_in[index]),
+    )
 
 
 def synthesis_block(upper, middle, lower, slope, tables):
@@ -343,36 +376,50 @@
     return jnp.concatenate(sides, axis=1) * slope
 
 
-def mixed_row(own, from_left, from_right, index):
+def mixed_row(odd, own, even_in, odd_in, index):
     base = parity((FB, 2 * FB)) * own[index]
-    return jnp.concatenate([base + from_left[index], base + from_right[index]], axis=1)
-
-
-def inner_kernel(own, from_left, from_right, slope, tables, result, mixed):
+    from_left, from_right = sides_of(odd, even_in, odd_in, index)
+    return jnp.concatenate([base + from_left, base + from_right], axis=1)
+
+
+def edges_kernel(odd, own, even_in, odd_in, side_even, side_odd):
+    first = mixed_row(odd, own, even_in, odd_in, 0)
+    last = mixed_row(odd, own, even_in, odd_in, own.shape[0] - 1)
+    odd_row = odd[0] == 1
+    side_even[...] = jnp.where(odd_row, first, last)
+    side_odd[...] = jnp.where(odd_row, last, first)
+
+
+def inner_kernel(odd, own, even_in, odd_in, slope, tables, result, mixed):
     step = pl.program_id(0)
 
     @pl.when(step == 0)
     def _():
         for index in range(own.shape[0]):
-            mixed[index] = mixed_row(own, from_left, from_right, index)
+            mixed[index] = mixed_row(odd, own, even_in, odd_in, index)
 
     result[...] = synthesis_block(
         mixed[step], mixed[step + 1], mixed[step + 2], slope[...], tables
     )
 
 
-def outer_kernel(own, from_left, from_right, above, below, slope, tables, partial, result):
+def outer_kernel(
+    odd, own, even_in, odd_in, near_even, near_odd, slope, tables, partial, result
+):
     del partial
     last = own.shape[0] - 1
-    rows = [mixed_row(own, from_left, from_right, i) for i in (0, 1, last - 1, last)]
+    rows = [mixed_row(odd, own, even_in, odd_in, i) for i in (0, 1, last - 1, last)]
+    odd_row = odd[0] == 1
 
     @pl.when(pl.program_id(0) == 0)
     def _():
-        result[...] = synthesis_block(above[...], rows[0], rows[1], slope[...], tables)
+        above = jnp.where(odd_row, near_even[...], near_odd[...])
+        result[...] = synthesis_block(above, rows[0], rows[1], slope[...], tables)
 
     @pl.when(pl.program_id(0) == 1)
     def _():
-        result[...] = synthesis_block(rows[2], rows[3], below[...], slope[...], tables)
+        below = jnp.where(odd_row, near_odd[...], near_even[...])
+        result[...] = synthesis_block(rows[2], rows[3], below, slope[...], tables)
 
 
 def whole(array):
@@ -384,17 +431,11 @@
     return pl.BlockSpec((TILE, TILE), lambda step: (step, 0))
 
 
-def spectra_of_tile():
-    return pl.BlockSpec((1, FB, 2 * FB), lambda step: (step, 0, 0))
-
-
-def params():
-    return pltpu.CompilerParams(
-        dimension_semantics=("arbitrary",), vmem_limit_bytes=VMEM_LIMIT
-    )
-
-
-def prelude(mask, kernels, weights):
+def params(limit=VMEM_LIMIT):
+    return pltpu.CompilerParams(dimension_semantics=("arbitrary",), vmem_limit_bytes=limit)
+
+
+def prelude(odd, mask, kernels, weights):
     count = kernels.shape[0]
     last = mask.shape[0] // HALO - 1
     edge = jax.ShapeDtypeStruct((HALO, TILE), jnp.float32)
@@ -405,6 +446,7 @@
         grid=(1,),
         out_shape=(edge, edge, packed),
         in_specs=[
+            pl.BlockSpec(memory_space=pltpu.SMEM),
             pl.BlockSpec((HALO, TILE), lambda step: (0, 0)),
             pl.BlockSpec((HALO, TILE), lambda step: (last, 0)),
             whole(kernels),
@@ -412,9 +454,9 @@
         ],
         out_specs=[whole(edge), whole(edge), whole(packed)],
         scratch_shapes=[part, part],
-        compiler_params=params(),
+        compiler_params=params(PRELUDE_LIMIT),
         name="prelude",
-    )(mask, mask, kernels, weights)
+    )(odd, mask, mask, kernels, weights)
 
 
 def preparation(own, other):
@@ -430,49 +472,66 @@
     )(own, other)
 
 
-def analysis(mask, above, below):
+def analysis(odd, mask, halo_even, halo_odd):
     tiles = mask.shape[0] // TILE
     tables = jnp.asarray(TABLES["analysis"])
     spectra = jax.ShapeDtypeStruct((tiles, FB, 2 * FB), jnp.float32)
     return pl.pallas_call(
         analysis_kernel,
         grid=(tiles,),
-        out_shape=(spectra, spectra, jax.ShapeDtypeStruct(mask.shape, jnp.float32)),
-        in_specs=[tile_rows(), whole(above), whole(below), whole(tables)],
-        out_specs=[whole(spectra), whole(spectra), tile_rows()],
+        out_shape=(spectra, spectra, spectra, jax.ShapeDtypeStruct(mask.shape, jnp.float32)),
+        in_specs=[
+            pl.BlockSpec(memory_space=pltpu.SMEM),
+            tile_rows(),
+            whole(halo_even),
+            whole(halo_odd),
+            whole(tables),
+        ],
+        out_specs=[whole(spectra)] * 3 + [tile_rows()],
         scratch_shapes=[pltpu.VMEM((tiles + 2, FB, 4 * FB), jnp.float32)],
         compiler_params=params(),
         name="analysis",
-    )(mask, above, below, tables)
-
-
-def imaging(left, right, from_left, from_right, straight, crossed, target):
-    tiles = left.shape[0]
+    )(odd, mask, halo_even, halo_odd, tables)
+
+
+def imaging(share, from_even, from_odd, straight, crossed, target):
+    tiles = share.shape[0]
     kernels = straight.shape[0]
     tables = jnp.asarray(TABLES["imaging"])
+    spectra = pl.BlockSpec((PAIR, FB, 2 * FB), lambda step: (step, 0, 0))
+    pixels = pl.BlockSpec((PAIR * TILE, TILE), lambda step: (step, 0))
     return pl.pallas_call(
         imaging_kernel,
-        grid=(tiles,),
+        grid=(tiles // PAIR,),
         out_shape=(
             jax.ShapeDtypeStruct(target.shape, jnp.float32),
-            jax.ShapeDtypeStruct(left.shape, jnp.float32),
+            jax.ShapeDtypeStruct(share.shape, jnp.float32),
         ),
-        in_specs=[spectra_of_tile()] * 4
-        + [whole(straight), whole(crossed), tile_rows(), whole(tables)],
-        out_specs=[tile_rows(), spectra_of_tile()],
+        in_specs=[spectra] * 3 + [whole(straight), whole(crossed), pixels, whole(tables)],
+        out_specs=[pixels, spectra],
         scratch_shapes=[
-            pltpu.VMEM((kernels, COARSE, 2 * COARSE), jnp.float32),
-            pltpu.VMEM((2, COARSE, COARSE), jnp.float32),
-            pltpu.VMEM((COARSE, COARSE), jnp.float32),
-            pltpu.VMEM((2, FB, 2 * FB), jnp.float32),
-            pltpu.VMEM((2, kernels // 2 * COARSE, 2 * FB), jnp.float32),
+            pltpu.VMEM((PAIR, kernels, COARSE, 2 * COARSE), jnp.float32),
+            pltpu.VMEM((PAIR, 2, kernels // 2 * COARSE, 2 * FB), jnp.float32),
         ],
         compiler_params=params(),
         name="imaging",
-    )(left, right, from_left, from_right, straight, crossed, target, tables)
-
-
-def inner_synthesis(own, from_left, from_right, slope):
+    )(share, from_even, from_odd, straight, crossed, target, tables)
+
+
+def edges(odd, grad, grad_even, grad_odd):
+    side = jax.ShapeDtypeStruct((FB, 4 * FB), jnp.float32)
+    vmem = pl.BlockSpec(memory_space=pltpu.VMEM)
+    return pl.pallas_call(
+        edges_kernel,
+        out_shape=(side, side),
+        in_specs=[pl.BlockSpec(memory_space=pltpu.SMEM)] + [vmem] * 3,
+        out_specs=[vmem] * 2,
+        compiler_params=pltpu.CompilerParams(vmem_limit_bytes=VMEM_LIMIT),
+        name="edges",
+    )(odd, grad, grad_even, grad_odd)
+
+
+def inner_synthesis(odd, own, even_in, odd_in, slope):
     tiles = own.shape[0]
     tables = jnp.asarray(TABLES["synthesis"])
     place = pl.BlockSpec((TILE, TILE), lambda step: (step + 1, 0))
@@ -480,7 +539,9 @@
         inner_kernel,
         grid=(tiles - 2,),
         out_shape=jax.ShapeDtypeStruct(slope.shape, jnp.float32),
-        in_specs=[whole(own)] * 3 + [place, whole(tables)],
+        in_specs=[pl.BlockSpec(memory_space=pltpu.SMEM)]
+        + [whole(own)] * 3
+        + [place, whole(tables)],
         out_specs=place,
         scratch_shapes=[pltpu.VMEM((tiles, FB, 4 * FB), jnp.float32)],
         compiler_params=params(),
@@ -488,10 +549,10 @@
             flops=1500000000, bytes_accessed=2500000, transcendentals=0
         ),
         name="inner_synthesis",
-    )(own, from_left, from_right, slope, tables)
-
-
-def outer_synthesis(own, from_left, from_right, above, below, slope, partial):
+    )(odd, own, even_in, odd_in, slope, tables)
+
+
+def outer_synthesis(odd, own, even_in, odd_in, near_even, near_odd, slope, partial):
     tiles = own.shape[0]
     tables = jnp.asarray(TABLES["synthesis"])
     place = pl.BlockSpec((TILE, TILE), lambda step: (step * (tiles - 1), 0))
@@ -499,51 +560,54 @@
         outer_kernel,
         grid=(2,),
         out_shape=jax.ShapeDtypeStruct(slope.shape, jnp.float32),
-        in_specs=[whole(own)] * 3
-        + [whole(above), whole(below), place, whole(tables), pl.BlockSpec(memory_space=pl.ANY)],
+        in_specs=[pl.BlockSpec(memory_space=pltpu.SMEM)]
+        + [whole(own)] * 3
+        + [whole(near_even), whole(near_odd), place, whole(tables)]
+        + [pl.BlockSpec(memory_space=pl.ANY)],
         out_specs=place,
-        input_output_aliases={7: 0},
+        input_output_aliases={8: 0},
         compiler_params=params(),
         name="outer_synthesis",
-    )(own, from_left, from_right, above, below, slope, tables, partial)
-
-
-def shifted(value, axis, steps):
-    count = lax.axis_size(axis)
-    pairs = [(i, i + steps) for i in range(count) if 0 <= i + steps < count]
-    return lax.ppermute(value, axis, pairs)
+    )(odd, own, even_in, odd_in, near_even, near_odd, slope, tables, partial)
+
+
+def swap_pairs(count, first):
+    pairs = []
+    for place in range(first, count - 1, 2):
+        pairs += [(place, place + 1), (place + 1, place)]
+    return pairs
 
 
 def local(mask_param, target, kernels, weights):
-    first, last, own = prelude(mask_param, kernels, weights)
-    above = shifted(last, "gy", 1)
-    below = shifted(first, "gy", -1)
-    rows = lax.axis_size("gy")
+    rows, cols = lax.axis_size("gy"), lax.axis_size("gx")
+    odd_row, odd_col = lax.axis_index("gy") % 2, lax.axis_index("gx") % 2
+    odd = jnp.stack([odd_row, odd_col]).astype(jnp.int32)
+
+    def swap(value, axis, first):
+        return lax.ppermute(value, axis, swap_pairs(lax.axis_size(axis), first))
+
+    edge_even, edge_odd, own = prelude(odd, mask_param, kernels, weights)
+    halo_odd = swap(edge_odd, "gy", 1)
+    halo_even = swap(edge_even, "gy", 0)
     inner = rows // 4
     pairs = []
     for place in range(rows):
         mirror = (3 - place // inner) * inner + place % inner
         pairs += [(2 * place, 2 * mirror + 1), (2 * place + 1, 2 * mirror)]
     other = lax.ppermute(own, ("gy", "ka"), pairs)
-    left, right, slope = analysis(mask_param, above, below)
-    from_right = shifted(left, "gx", -1)
-    from_left = shifted(right, "gx", 1)
+    share, to_even, to_odd, slope = analysis(odd, mask_param, halo_even, halo_odd)
+    from_odd = swap(to_odd, "gx", 1)
+    from_even = swap(to_even, "gx", 0)
     straight, crossed = preparation(own, other)
-    resist, grad = imaging(left, right, from_left, from_right, straight, crossed, target)
-    grad_left = shifted(grad, "gx", 1)
-    grad_right = shifted(grad, "gx", -1)
-
-    flip = jnp.asarray(np.where(np.arange(2 * FB) % 2 == 0, 1.0, -1.0).astype(np.float32))
-
-    def edge(index):
-        base = flip * grad[index]
-        return jnp.concatenate([base + grad_left[index], base + grad_right[index]], axis=-1)
-
-    from_above = shifted(edge(-1), "gy", 1)
-    from_below = shifted(edge(0), "gy", -1)
-    partial = inner_synthesis(grad, grad_left, grad_right, slope)
+    resist, grad = imaging(share, from_even, from_odd, straight, crossed, target)
+    grad_odd = swap(grad, "gx", 1)
+    grad_even = swap(grad, "gx", 0)
+    side_even, side_odd = edges(odd, grad, grad_even, grad_odd)
+    near_odd = swap(side_odd, "gy", 1)
+    near_even = swap(side_even, "gy", 0)
+    partial = inner_synthesis(odd, grad, grad_even, grad_odd, slope)
     gradient = outer_synthesis(
-        grad, grad_left, grad_right, from_above, from_below, slope, partial
+        odd, grad, grad_even, grad_odd, near_even, near_odd, slope, partial
     )
     return (gradient, resist)
 

time: 72.8 us -> 63.6 us (0.87); the launches traced: 71.5 us -> 63.1 us
  starting transfers between devices: 30.6 us -> 20.5 us
  waiting for transfers between devices: 8.98 us -> 10.2 us
    ppermute x8, starting transfers between devices: 24.7 us -> 13.6 us  [swap(): return lax.ppermute(value, axis, swap_pairs(lax.axis_size(axis), first))]
    pallas_call x1 -> x2, Pallas kernels: 18.4 us -> 15.6 us  [the longest x1 15 us: imaging(): pl.pallas_call(imaging_kernel, grid=(tiles // PAIR,), out_shape=(jax.Shap...]
    pallas_call x1, Pallas kernels: 0.77 us -> 2.04 us  [prelude(): pl.pallas_call(prelude_kernel, grid=(1,), out_shape=(edge, edge, packed),...]
    ppermute x8, waiting for transfers between devices: 8.97 us -> 10.2 us  [swap(): return lax.ppermute(value, axis, swap_pairs(lax.axis_size(axis), first))]
    ppermute x1, starting transfers between devices: 5.93 us -> 6.83 us  [local(): other = lax.ppermute(own, ('gy', 'ka'), pairs)]
    unnamed x16 -> x14, local copies, waits for them, and re-layouts: 3 us -> 2.69 us
  transfers between devices with their start and end apart: 9 -> 9, of which waited for: 4 -> 3; matrix products, arithmetic and copies ran while one was open for 0% -> 0% of each run, Pallas kernels for 10% -> 13%
where the time goes in v2:
time: 63.6 us; the launch traced here: 63.1 us
  Pallas kernels  28.2 us (44%)
  starting transfers between devices  20.5 us (32%)
  waiting for transfers between devices  10.2 us (16%)
  local copies, waits for them, and re-layouts  2.69 us (4%)
  between operations  0.77 us (1%)
  other arithmetic  0.67 us (1%)
    pallas_call x1, Pallas kernels, imaging(): pl.pallas_call(imaging_kernel, grid=(tiles // PAIR,), out_shape=(jax.Shap...  15 us
    ppermute x8, starting transfers between devices, swap(): return lax.ppermute(value, axis, swap_pairs(lax.axis_size(axis), first))  13.6 us
    ppermute x8, waiting for transfers between devices, swap(): return lax.ppermute(value, axis, swap_pairs(lax.axis_size(axis), first))  10.2 us
    ppermute x1, starting transfers between devices, local(): other = lax.ppermute(own, ('gy', 'ka'), pairs)  6.83 us
    pallas_call x1, Pallas kernels, analysis(): pl.pallas_call(analysis_kernel, grid=(tiles,), out_shape=(spectra, spectr...  4.51 us
    pallas_call x1, Pallas kernels, inner_synthesis(): pl.pallas_call(inner_kernel, grid=(tiles - 2,), out_shape=jax.ShapeDtypeS...  3.59 us
    unnamed x14, local copies, waits for them, and re-layouts  2.69 us
    pallas_call x1, Pallas kernels, outer_synthesis(): pl.pallas_call(outer_kernel, grid=(2,), out_shape=jax.ShapeDtypeStruct(sl...  2.35 us
  transfers between devices with their start and end apart: 9, of which 3 were waited for; matrix products, arithmetic and copies ran while one was open for 0% of the time, Pallas kernels for 13%

profile of v2, /device:TPU:40, one launch (start us, length us, event | category | flops | bytes accessed | tf_op | source)
XLA Modules:
  0.0 63.1 jit_solution(16273535597926377756)
XLA Ops:
  0.6 0.7 %pad_add_fusion.odd = s32[2]{0:T(128)} fusion(s32[1]{0:T(128)} %bitcast.1, s32[1]{0:T(128)} %bitcast), kind=kLoop, calls=%fused_computation | loop fusion | flops 2 | bytes 16 | tf_op jit(solution)/shard_map/stack | solution.py:584
  1.3 2.0 %prelude.1 = (f32[128,256]{1,0:T(8,128)}, f32[128,256]{1,0:T(8,128)}, f32[6,64,128]{2,1,0:T(8,128)}) custom-call(s32[2]{0:T(128)} %pad_add_fusion.odd, f32[1536,256]{1,0:T(8,128)} %mask.1, f32[1536,256]{1,0:T(8,128)} %mask.1, f32[6,2,4096]{2,1,0:T(2,128)} %kernels.1, f32[6]{0:T(128)} %weights.1), custom_call_target="tpu_custom_call" | custom-call | tf_op jit(solution)/shard_map/prelude/pallas_call | solution.py:444
  3.4 1.5 %collective-permute-start = (f32[128,256]{1,0:T(8,128)}, f32[128,256]{1,0:T(8,128)S(1)}, u32[]{:S(2)}, u32[]{:S(2)}) collective-permute-start(f32[128,256]{1,0:T(8,128)} %get-tuple-element.15), channel_id=1, source_target_pairs={{0,2},{2,0},{4,6},{6,4},{8,10},{10,8},{12,14},{14,12},{16,18},{18,... | collective-permute-start | bytes 393224 | tf_op jit(solution)/shard_map/ppermute | solution.py:587
  4.9 3.5 %collective-permute-start.1 = (f32[128,256]{1,0:T(8,128)}, f32[128,256]{1,0:T(8,128)S(1)}, u32[]{:S(2)}, u32[]{:S(2)}) collective-permute-start(f32[128,256]{1,0:T(8,128)} %get-tuple-element.16), channel_id=1, source_target_pairs={{2,4},{4,2},{6,8},{8,6},{10,12},{12,10},{14,16},{16,14},{18,20},{2... | collective-permute-start | bytes 393224 | tf_op jit(solution)/shard_map/ppermute | solution.py:587
  8.4 6.8 %collective-permute-start.4 = (f32[6,64,128]{2,1,0:T(8,128)}, f32[6,64,128]{2,1,0:T(8,128)S(1)}, u32[]{:S(2)}, u32[]{:S(2)}) collective-permute-start(f32[6,64,128]{2,1,0:T(8,128)} %get-tuple-element.20.own), channel_id=1, source_target_pairs={{0,25},{1,24},{2,27},{3,26},{4,29},{5,28},{6,31},{7,30},{8,17},{9,... | collective-permute-start | bytes 589832 | tf_op jit(solution)/shard_map/ppermute | solution.py:597
  15.2 0.0 collective-permute-done.halo_even
  15.2 0.0 collective-permute-done.1.halo_odd
  15.2 0.0 copy-done.4
  15.2 0.0 copy-done.6
  15.3 0.0 copy-start
  15.3 1.4 %copy-done = f32[1536,256]{1,0:T(8,128)S(1)} copy-done((f32[1536,256]{1,0:T(8,128)S(1)}, f32[1536,256]{1,0:T(8,128)}, u32[]{:S(2)}) %copy-start) | copy-done | bytes 1572888
  16.7 4.5 %analysis.1 = (f32[6,64,128]{2,1,0:T(8,128)S(1)}, f32[6,64,128]{2,1,0:T(8,128)S(1)}, f32[6,64,128]{2,1,0:T(8,128)S(1)}, f32[1536,256]{1,0:T(8,128)S(1)}) custom-call(s32[2]{0:T(128)S(1)} %copy-done.6, f32[1536,256]{1,0:T(8,128)S(1)} %copy-done, f32[128,256]{1,0:T(8,128)S(1)} %collective-permute-done.halo_even, ...), custom_call_target="tpu_custom_call" | custom-call | tf_op jit(solution)/shard_map/analysis/pallas_call | solution.py:479
  21.2 0.1 collective-permute-start.2
  21.3 2.4 %collective-permute-start.3 = (f32[6,64,128]{2,1,0:T(8,128)S(1)}, f32[6,64,128]{2,1,0:T(8,128)S(1)}, u32[]{:S(2)}, u32[]{:S(2)}) collective-permute-start(f32[6,64,128]{2,1,0:T(8,128)S(1)} %get-tuple-element.19), channel_id=1, source_target_pairs={{32,64},{64,32},{96,128},{128,96},{160,192},{192,160},{33,65},{65,... | collective-permute-start | bytes 589832 | tf_op jit(solution)/shard_map/ppermute | solution.py:587
  23.7 0.0 collective-permute-done.4.other
  23.7 0.0 copy-done.5
  23.8 0.2 preparation.1
  23.9 0.0 collective-permute-done.2.from_even
  23.9 4.3 %collective-permute-done.3.from_odd = f32[6,64,128]{2,1,0:T(8,128)S(1)} collective-permute-done((f32[6,64,128]{2,1,0:T(8,128)S(1)}, f32[6,64,128]{2,1,0:T(8,128)S(1)}, u32[]{:S(2)}, u32[]{:S(2)}) %collective-permute-start.3) | collective-permute-done | bytes 196640 | tf_op jit(solution)/shard_map/ppermute | solution.py:587
  28.3 1.3 %copy-done.2 = bf16[4608,128]{1,0:T(8,128)(2,1)S(1)} copy-done((bf16[4608,128]{1,0:T(8,128)(2,1)S(1)}, bf16[4608,128]{1,0:T(8,128)(2,1)}, u32[]{:S(2)}) %copy-start.2) | copy-done | bytes 1179672
  29.5 15.0 %imaging.1 = (f32[1536,256]{1,0:T(8,128)}, f32[6,64,128]{2,1,0:T(8,128)S(1)}) custom-call(f32[6,64,128]{2,1,0:T(8,128)S(1)} %get-tuple-element.17.share, f32[6,64,128]{2,1,0:T(8,128)S(1)} %collective-permute-done.2.from_even, f32[6,64,128]{2,1,0:T(8,128)S(1)} %collective-permute-done.3.from_odd, f32[12,64,128]{2,1,0:T(8,128)S(1)} %get-tuple-element.21.straight, ...), custom_call_target="tpu_custom_call" | custom-call | tf_op jit(solution)/shard_map/imaging/pallas_call | solution.py:503
  44.6 2.4 %collective-permute-start.6 = (f32[6,64,128]{2,1,0:T(8,128)S(1)}, f32[6,64,128]{2,1,0:T(8,128)S(1)}, u32[]{:S(2)}, u32[]{:S(2)}) collective-permute-start(f32[6,64,128]{2,1,0:T(8,128)S(1)} %get-tuple-element.23.own), channel_id=1, source_target_pairs={{32,64},{64,32},{96,128},{128,96},{160,192},{192,160},{33,65},{65,... | collective-permute-start | bytes 589832 | tf_op jit(solution)/shard_map/ppermute | solution.py:587
  47.0 1.2 %collective-permute-start.5 = (f32[6,64,128]{2,1,0:T(8,128)S(1)}, f32[6,64,128]{2,1,0:T(8,128)S(1)}, u32[]{:S(2)}, u32[]{:S(2)}) collective-permute-start(f32[6,64,128]{2,1,0:T(8,128)S(1)} %get-tuple-element.23.own), channel_id=1, source_target_pairs={{0,32},{32,0},{64,96},{96,64},{128,160},{160,128},{192,224},{224,1... | collective-permute-start | bytes 589832 | tf_op jit(solution)/shard_map/ppermute | solution.py:587
  48.2 3.3 %collective-permute-done.6.odd_in = f32[6,64,128]{2,1,0:T(8,128)S(1)} collective-permute-done((f32[6,64,128]{2,1,0:T(8,128)S(1)}, f32[6,64,128]{2,1,0:T(8,128)S(1)}, u32[]{:S(2)}, u32[]{:S(2)}) %collective-permute-start.6) | collective-permute-done | bytes 196640 | tf_op jit(solution)/shard_map/ppermute | solution.py:587
  51.5 0.0 collective-permute-done.5.even_in
  51.5 0.6 edges.1
  52.1 0.2 collective-permute-start.7
  52.3 2.2 %collective-permute-start.8 = (f32[64,256]{1,0:T(8,128)S(1)}, f32[64,256]{1,0:T(8,128)S(1)}, u32[]{:S(2)}, u32[]{:S(2)}) collective-permute-start(f32[64,256]{1,0:T(8,128)S(1)} %get-tuple-element.25), channel_id=1, source_target_pairs={{2,4},{4,2},{6,8},{8,6},{10,12},{12,10},{14,16},{16,14},{18,20},{2... | collective-permute-start | bytes 196616 | tf_op jit(solution)/shard_map/ppermute | solution.py:587
  54.5 3.6 %inner_synthesis.1.partial = f32[1536,256]{1,0:T(8,128)} custom-call(s32[2]{0:T(128)S(1)} %copy-done.6, f32[6,64,128]{2,1,0:T(8,128)S(1)} %get-tuple-element.23.own, f32[6,64,128]{2,1,0:T(8,128)S(1)} %collective-permute-done.5.even_in, f32[6,64,128]{2,1,0:T(8,128)S(1)} %collective-permute-done.6.odd_in, f32[1536,256]{1,0:T(8,128)S(1)} %get-tuple-element.26.slope, ...), custom_call_target="tpu_custom_call" | custom-call | flops 1500000000 | bytes 2500000 | tf_op jit(solution)/shard_map/inner_synthesis/pallas_call | solution.py:538
  58.1 0.0 collective-permute-done.7.near_even
  58.1 2.6 %collective-permute-done.8.near_odd = f32[64,256]{1,0:T(8,128)S(1)} collective-permute-done((f32[64,256]{1,0:T(8,128)S(1)}, f32[64,256]{1,0:T(8,128)S(1)}, u32[]{:S(2)}, u32[]{:S(2)}) %collective-permute-start.8) | collective-permute-done | bytes 65568 | tf_op jit(solution)/shard_map/ppermute | solution.py:587
  60.7 2.4 %outer_synthesis.1 = f32[1536,256]{1,0:T(8,128)} custom-call(s32[2]{0:T(128)S(1)} %copy-done.6, f32[6,64,128]{2,1,0:T(8,128)S(1)} %get-tuple-element.23.own, f32[6,64,128]{2,1,0:T(8,128)S(1)} %collective-permute-done.5.even_in, f32[6,64,128]{2,1,0:T(8,128)S(1)} %collective-permute-done.6.odd_in, ...), custom_call_target="tpu_custom_call", output_to_operand_aliasing={{}: (8, {})} | custom-call | tf_op jit(solution)/shard_map/outer_synthesis/pallas_call | solution.py:559
  (8 shorter events, 0.0 us)
Async XLA Ops:
  1.3 13.9 %copy-start.4 = (bf16[1536,128]{1,0:T(8,128)(2,1)S(1)}, bf16[1536,128]{1,0:T(8,128)(2,1)}, u32[]{:S(2)}) copy-start(bf16[1536,128]{1,0:T(8,128)(2,1)} %constant.35.clone.tables) | copy-start | bytes 1179652
  1.3 13.9 %copy-start.6 = (s32[2]{0:T(128)S(1)}, s32[2]{0:T(128)}, u32[]{:S(2)}) copy-start(s32[2]{0:T(128)} %pad_add_fusion.odd) | copy-start | bytes 28
  3.4 11.9 %collective-permute-start = (f32[128,256]{1,0:T(8,128)}, f32[128,256]{1,0:T(8,128)S(1)}, u32[]{:S(2)}, u32[]{:S(2)}) collective-permute-start(f32[128,256]{1,0:T(8,128)} %get-tuple-element.15), channel_id=1, source_target_pairs={{0,2},{2,0},{4,6},{6,4},{8,10},{10,8},{12,14},{14,12},{16,18},{18,... | collective-permute-start | bytes 393224 | tf_op jit(solution)/shard_map/ppermute | solution.py:587
  4.9 10.4 %collective-permute-start.1 = (f32[128,256]{1,0:T(8,128)}, f32[128,256]{1,0:T(8,128)S(1)}, u32[]{:S(2)}, u32[]{:S(2)}) collective-permute-start(f32[128,256]{1,0:T(8,128)} %get-tuple-element.16), channel_id=1, source_target_pairs={{2,4},{4,2},{6,8},{8,6},{10,12},{12,10},{14,16},{16,14},{18,20},{2... | collective-permute-start | bytes 393224 | tf_op jit(solution)/shard_map/ppermute | solution.py:587
  8.4 15.3 %collective-permute-start.4 = (f32[6,64,128]{2,1,0:T(8,128)}, f32[6,64,128]{2,1,0:T(8,128)S(1)}, u32[]{:S(2)}, u32[]{:S(2)}) collective-permute-start(f32[6,64,128]{2,1,0:T(8,128)} %get-tuple-element.20.own), channel_id=1, source_target_pairs={{0,25},{1,24},{2,27},{3,26},{4,29},{5,28},{6,31},{7,30},{8,17},{9,... | collective-permute-start | bytes 589832 | tf_op jit(solution)/shard_map/ppermute | solution.py:597
  15.3 1.4 %copy-start = (f32[1536,256]{1,0:T(8,128)S(1)}, f32[1536,256]{1,0:T(8,128)}, u32[]{:S(2)}) copy-start(f32[1536,256]{1,0:T(8,128)} %mask.1) | copy-start | bytes 4718596
  16.7 7.1 %copy-start.5 = (f32[6,64,128]{2,1,0:T(8,128)S(1)}, f32[6,64,128]{2,1,0:T(8,128)}, u32[]{:S(2)}) copy-start(f32[6,64,128]{2,1,0:T(8,128)} %get-tuple-element.20.own) | copy-start | bytes 589828
  16.7 11.6 %copy-start.1 = (s32[1536,256]{1,0:T(8,128)S(1)}, s32[1536,256]{1,0:T(8,128)}, u32[]{:S(2)}) copy-start(s32[1536,256]{1,0:T(8,128)} %target.1) | copy-start | bytes 4718596
  21.2 2.7 %collective-permute-start.2 = (f32[6,64,128]{2,1,0:T(8,128)S(1)}, f32[6,64,128]{2,1,0:T(8,128)S(1)}, u32[]{:S(2)}, u32[]{:S(2)}) collective-permute-start(f32[6,64,128]{2,1,0:T(8,128)S(1)} %get-tuple-element.18), channel_id=1, source_target_pairs={{0,32},{32,0},{64,96},{96,64},{128,160},{160,128},{192,224},{224,1... | collective-permute-start | bytes 589832 | tf_op jit(solution)/shard_map/ppermute | solution.py:587
  21.3 7.0 %collective-permute-start.3 = (f32[6,64,128]{2,1,0:T(8,128)S(1)}, f32[6,64,128]{2,1,0:T(8,128)S(1)}, u32[]{:S(2)}, u32[]{:S(2)}) collective-permute-start(f32[6,64,128]{2,1,0:T(8,128)S(1)} %get-tuple-element.19), channel_id=1, source_target_pairs={{32,64},{64,32},{96,128},{128,96},{160,192},{192,160},{33,65},{65,... | collective-permute-start | bytes 589832 | tf_op jit(solution)/shard_map/ppermute | solution.py:587
  28.3 1.3 %copy-start.2 = (bf16[4608,128]{1,0:T(8,128)(2,1)S(1)}, bf16[4608,128]{1,0:T(8,128)(2,1)}, u32[]{:S(2)}) copy-start(bf16[4608,128]{1,0:T(8,128)(2,1)} %constant.36.clone.wide) | copy-start | bytes 3538948
  29.5 25.0 %copy-start.3 = (bf16[1536,128]{1,0:T(8,128)(2,1)S(1)}, bf16[1536,128]{1,0:T(8,128)(2,1)}, u32[]{:S(2)}) copy-start(bf16[1536,128]{1,0:T(8,128)(2,1)} %constant.37.clone.tables) | copy-start | bytes 1179652
  44.6 7.0 %collective-permute-start.6 = (f32[6,64,128]{2,1,0:T(8,128)S(1)}, f32[6,64,128]{2,1,0:T(8,128)S(1)}, u32[]{:S(2)}, u32[]{:S(2)}) collective-permute-start(f32[6,64,128]{2,1,0:T(8,128)S(1)} %get-tuple-element.23.own), channel_id=1, source_target_pairs={{32,64},{64,32},{96,128},{128,96},{160,192},{192,160},{33,65},{65,... | collective-permute-start | bytes 589832 | tf_op jit(solution)/shard_map/ppermute | solution.py:587
  47.0 4.5 %collective-permute-start.5 = (f32[6,64,128]{2,1,0:T(8,128)S(1)}, f32[6,64,128]{2,1,0:T(8,128)S(1)}, u32[]{:S(2)}, u32[]{:S(2)}) collective-permute-start(f32[6,64,128]{2,1,0:T(8,128)S(1)} %get-tuple-element.23.own), channel_id=1, source_target_pairs={{0,32},{32,0},{64,96},{96,64},{128,160},{160,128},{192,224},{224,1... | collective-permute-start | bytes 589832 | tf_op jit(solution)/shard_map/ppermute | solution.py:587
  52.1 6.0 %collective-permute-start.7 = (f32[64,256]{1,0:T(8,128)S(1)}, f32[64,256]{1,0:T(8,128)S(1)}, u32[]{:S(2)}, u32[]{:S(2)}) collective-permute-start(f32[64,256]{1,0:T(8,128)S(1)} %get-tuple-element.24), channel_id=1, source_target_pairs={{0,2},{2,0},{4,6},{6,4},{8,10},{10,8},{12,14},{14,12},{16,18},{18,... | collective-permute-start | bytes 196616 | tf_op jit(solution)/shard_map/ppermute | solution.py:587
  52.3 8.4 %collective-permute-start.8 = (f32[64,256]{1,0:T(8,128)S(1)}, f32[64,256]{1,0:T(8,128)S(1)}, u32[]{:S(2)}, u32[]{:S(2)}) collective-permute-start(f32[64,256]{1,0:T(8,128)S(1)} %get-tuple-element.25), channel_id=1, source_target_pairs={{2,4},{4,2},{6,8},{8,6},{10,12},{12,10},{14,16},{16,14},{18,20},{2... | collective-permute-start | bytes 196616 | tf_op jit(solution)/shard_map/ppermute | solution.py:587

commit v3 on v2

--- a/solution.py
+++ b/solution.py
@@ -17,7 +17,8 @@
 HALF = COARSE // 2
 VMEM_LIMIT = 32 * 1024 * 1024
 PAIR = 2
-PRELUDE_LIMIT = 63 * 1024 * 1024
+TILES_AT_ONCE = 3
+FIRST_LIMIT = 63 * 1024 * 1024
 
 bf16 = ml_dtypes.bfloat16
 
@@ -177,6 +178,10 @@
     return (1 - 2 * (index % 2)).astype(jnp.float32)
 
 
+def is_odd(axis):
+    return lax.axis_index(axis) % 2 == 1
+
+
 def row_parity(shape):
     index = lax.broadcasted_iota(jnp.int32, shape, 0)
     return jnp.where(index < FB // 2, 1.0, -1.0)
@@ -190,10 +195,21 @@
     return pltpu.roll(value, FB, 1)
 
 
-def prelude_kernel(odd, first, last, kernels, weights, even_out, odd_out, packed, real, imag):
-    odd_row = odd[0] == 1
-    even_out[...] = jnp.where(odd_row, first[...], last[...])
-    odd_out[...] = jnp.where(odd_row, last[...], first[...])
+def preparation_kernel(own, other, tables, straight, crossed, loaded, semaphore):
+    copy = pltpu.make_async_copy(tables, loaded, semaphore)
+    copy.start()
+    count = own.shape[0]
+    lanes = low_lanes((FB, 2 * FB))
+    for group, source in enumerate((own, other)):
+        for index in range(count):
+            spectrum = source[index]
+            turned = swapped(spectrum)
+            straight[group * count + index] = jnp.where(lanes, spectrum, turned)
+            crossed[group * count + index] = jnp.where(lanes, -turned, spectrum)
+    copy.wait()
+
+
+def pack_kernels(kernels, weights, packed, real, imag):
     lanes = low_lanes((FB // 2, 2 * FB))
     for index in range(kernels.shape[0]):
         for row in range(FB // 2):
@@ -206,67 +222,72 @@
         packed[index, FB // 2 :] = jnp.where(lanes, swapped(re), im)
 
 
-def preparation_kernel(own, other, straight, crossed):
-    count = own.shape[0]
-    lanes = low_lanes((FB, 2 * FB))
-    for group, source in enumerate((own, other)):
-        for index in range(count):
-            spectrum = source[index]
-            turned = swapped(spectrum)
-            straight[group * count + index] = jnp.where(lanes, spectrum, turned)
-            crossed[group * count + index] = jnp.where(lanes, -turned, spectrum)
+def block_spectra(transmit, tables):
+    sign = jnp.where(low_lanes((FB, 2 * FB)), 1.0, -1.0)
+    high, low = split(transmit)
+    rows = []
+    for side in (0, 1):
+        lanes = slice(side * HALO, (side + 1) * HALO)
+        three = jnp.concatenate([high[:, lanes], low[:, lanes], high[:, lanes]], axis=1)
+        rows.append(dot(three, col_table(tables, side)))
+    rows = jnp.concatenate(rows, axis=1)
+    found = []
+    for block in range(transmit.shape[0] // HALO):
+        both = table_times(
+            row_table(tables, block % 2), rows[block * HALO : (block + 1) * HALO]
+        )
+        sine = both[FB:]
+        turned = [sign * swapped(sine[:, : 2 * FB]), sign * swapped(sine[:, 2 * FB :])]
+        found.append(both[:FB] + jnp.concatenate(turned, axis=1))
+    return found
 
 
 def analysis_kernel(
-    odd, mask, halo_even, halo_odd, tables, share, to_even, to_odd, slope, total
+    mask, kernels, weights, tables, total, packed, edge_even, edge_odd, slope, real, imag, sums
 ):
     step = pl.program_id(0)
-    count = share.shape[0]
-    sign = jnp.where(low_lanes((FB, 2 * FB)), 1.0, -1.0)
-    flip = row_parity((FB, 4 * FB))
-
-    def spectra(transmit):
-        high, low = split(transmit)
-        rows = []
-        for side in (0, 1):
-            lanes = slice(side * HALO, (side + 1) * HALO)
-            three = jnp.concatenate([high[:, lanes], low[:, lanes], high[:, lanes]], axis=1)
-            rows.append(dot(three, col_table(tables, side)))
-        rows = jnp.concatenate(rows, axis=1)
-        found = []
-        for part in (0, 1):
-            both = table_times(row_table(tables, part), rows[part * HALO : (part + 1) * HALO])
-            sine = both[FB:]
-            turned = [sign * swapped(sine[:, : 2 * FB]), sign * swapped(sine[:, 2 * FB :])]
-            found.append(both[:FB] + jnp.concatenate(turned, axis=1))
-        return found
+    count = total.shape[0]
 
     @pl.when(step == 0)
     def _():
-        odd_row = odd[0] == 1
-        below = jnp.where(odd_row, halo_odd[...], halo_even[...])
-        above = jnp.where(odd_row, halo_even[...], halo_odd[...])
-        outer = jnp.concatenate([below, above], axis=0)
-        upper, lower = spectra(jnp.tanh(outer))
-        total[...] = jnp.zeros_like(total)
-        total[1] = lower
-        total[count] = upper
+        sums[...] = jnp.zeros_like(sums)
+        pack_kernels(kernels, weights, packed, real, imag)
 
     transmit = jnp.tanh(mask[...])
     slope[...] = 1.0 - transmit * transmit
-    upper, lower = spectra(transmit)
-    total[step] += upper
-    total[step + 1] += flip * (upper + lower)
-    total[step + 2] += lower
-
-    @pl.when(step == count - 1)
+    found = block_spectra(transmit, tables)
+    flip = row_parity((FB, 4 * FB))
+    first = step * PAIR
+    for tile in range(PAIR):
+        upper, lower = found[2 * tile], found[2 * tile + 1]
+        sums[first + tile] += upper
+        sums[first + tile + 1] += flip * (upper + lower)
+        sums[first + tile + 2] += lower
+
+    @pl.when(step == pl.num_programs(0) - 1)
     def _():
-        odd_col = odd[1] == 1
-        for index in range(count):
-            left, right = total[index + 1, :, : 2 * FB], total[index + 1, :, 2 * FB :]
-            share[index] = parity((FB, 2 * FB)) * (left + right)
-            to_even[index] = jnp.where(odd_col, left, right)
-            to_odd[index] = jnp.where(odd_col, right, left)
+        total[...] = sums[1 : count + 1]
+        up, down = sums[0], sums[count + 1]
+        odd_row = is_odd("gy")
+        edge_even[...] = jnp.where(odd_row, up, down)
+        edge_odd[...] = jnp.where(odd_row, down, up)
+
+
+def merge_kernel(total, near_even, near_odd, share, to_even, to_odd):
+    count = share.shape[0]
+    odd_row, odd_col = is_odd("gy"), is_odd("gx")
+    above = jnp.where(odd_row, near_even[...], near_odd[...])
+    below = jnp.where(odd_row, near_odd[...], near_even[...])
+    for index in range(count):
+        both = total[index]
+        if index == 0:
+            both = both + above
+        if index == count - 1:
+            both = both + below
+        left, right = both[:, : 2 * FB], both[:, 2 * FB :]
+        share[index] = parity((FB, 2 * FB)) * (left + right)
+        to_even[index] = jnp.where(odd_col, left, right)
+        to_odd[index] = jnp.where(odd_col, right, left)
 
 
 def imaging_kernel(
@@ -275,7 +296,7 @@
 ):
     count = straight.shape[0] // 2
     sign = jnp.where(low_lanes((HALF, 2 * FB)), 1.0, -1.0)
-    tiles = range(PAIR)
+    tiles = range(share.shape[0])
     weights = []
     intensities = [[] for tile in tiles]
 
@@ -350,24 +371,26 @@
         grad[tile] = adjoint[0] + adjoint[1]
 
 
-def sides_of(odd, even_in, odd_in, index):
-    odd_col = odd[1] == 1
+def sides_of(even_in, odd_in, index):
+    odd_col = is_odd("gx")
     return (
         jnp.where(odd_col, even_in[index], odd_in[index]),
         jnp.where(odd_col, odd_in[index], even_in[index]),
     )
 
 
-def synthesis_block(upper, middle, lower, slope, tables):
+def synthesis_rows(rows, slope, tables):
     sign = jnp.where(low_lanes((FB, 2 * FB)), -1.0, 1.0)
-    base = row_parity((FB, 4 * FB)) * middle
-    rows = []
-    for part, near in enumerate((upper, lower)):
-        block = base + near
-        turned = [sign * swapped(block[:, : 2 * FB]), sign * swapped(block[:, 2 * FB :])]
-        stacked = jnp.concatenate([block, jnp.concatenate(turned, axis=1)], axis=0)
-        rows.append(table_times(row_table(tables, part), stacked))
-    high, low = split(jnp.concatenate(rows, axis=0))
+    flip = row_parity((FB, 4 * FB))
+    outer = []
+    for index in range(1, len(rows) - 1):
+        base = flip * rows[index]
+        for part, near in enumerate((rows[index - 1], rows[index + 1])):
+            block = base + near
+            turned = [sign * swapped(block[:, : 2 * FB]), sign * swapped(block[:, 2 * FB :])]
+            stacked = jnp.concatenate([block, jnp.concatenate(turned, axis=1)], axis=0)
+            outer.append(table_times(row_table(tables, part), stacked))
+    high, low = split(jnp.concatenate(outer, axis=0))
     sides = []
     for side in (0, 1):
         lanes = slice(side * 2 * FB, (side + 1) * 2 * FB)
@@ -376,50 +399,41 @@
     return jnp.concatenate(sides, axis=1) * slope
 
 
-def mixed_row(odd, own, even_in, odd_in, index):
+def mixed_row(own, even_in, odd_in, index):
     base = parity((FB, 2 * FB)) * own[index]
-    from_left, from_right = sides_of(odd, even_in, odd_in, index)
+    from_left, from_right = sides_of(even_in, odd_in, index)
     return jnp.concatenate([base + from_left, base + from_right], axis=1)
 
 
-def edges_kernel(odd, own, even_in, odd_in, side_even, side_odd):
-    first = mixed_row(odd, own, even_in, odd_in, 0)
-    last = mixed_row(odd, own, even_in, odd_in, own.shape[0] - 1)
-    odd_row = odd[0] == 1
+def edges_kernel(own, even_in, odd_in, side_even, side_odd):
+    first = mixed_row(own, even_in, odd_in, 0)
+    last = mixed_row(own, even_in, odd_in, own.shape[0] - 1)
+    odd_row = is_odd("gy")
     side_even[...] = jnp.where(odd_row, first, last)
     side_odd[...] = jnp.where(odd_row, last, first)
 
 
-def inner_kernel(odd, own, even_in, odd_in, slope, tables, result, mixed):
-    step = pl.program_id(0)
-
-    @pl.when(step == 0)
-    def _():
-        for index in range(own.shape[0]):
-            mixed[index] = mixed_row(odd, own, even_in, odd_in, index)
-
-    result[...] = synthesis_block(
-        mixed[step], mixed[step + 1], mixed[step + 2], slope[...], tables
-    )
-
-
-def outer_kernel(
-    odd, own, even_in, odd_in, near_even, near_odd, slope, tables, partial, result
-):
+def inner_kernel(own, even_in, odd_in, slope, tables, result):
+    rows = [mixed_row(own, even_in, odd_in, i) for i in range(PAIR - 1, 2 * PAIR + 1)]
+    result[...] = synthesis_rows(rows, slope[...], tables)
+
+
+def outer_kernel(own, even_in, odd_in, near_even, near_odd, slope, tables, partial, result):
     del partial
-    last = own.shape[0] - 1
-    rows = [mixed_row(odd, own, even_in, odd_in, i) for i in (0, 1, last - 1, last)]
-    odd_row = odd[0] == 1
+    count = own.shape[0]
+    odd_row = is_odd("gy")
 
     @pl.when(pl.program_id(0) == 0)
     def _():
-        above = jnp.where(odd_row, near_even[...], near_odd[...])
-        result[...] = synthesis_block(above, rows[0], rows[1], slope[...], tables)
+        rows = [jnp.where(odd_row, near_even[...], near_odd[...])]
+        rows += [mixed_row(own, even_in, odd_in, i) for i in range(PAIR + 1)]
+        result[...] = synthesis_rows(rows, slope[...], tables)
 
     @pl.when(pl.program_id(0) == 1)
     def _():
-        below = jnp.where(odd_row, near_odd[...], near_even[...])
-        result[...] = synthesis_block(rows[2], rows[3], below, slope[...], tables)
+        rows = [mixed_row(own, even_in, odd_in, i) for i in range(count - PAIR - 1, count)]
+        rows += [jnp.where(odd_row, near_odd[...], near_even[...])]
+        result[...] = synthesis_rows(rows, slope[...], tables)
 
 
 def whole(array):
@@ -427,82 +441,86 @@
     return pl.BlockSpec(array.shape, lambda step: zeros)
 
 
-def tile_rows():
-    return pl.BlockSpec((TILE, TILE), lambda step: (step, 0))
+def tile_pair():
+    return pl.BlockSpec((PAIR * TILE, TILE), lambda step: (step, 0))
 
 
 def params(limit=VMEM_LIMIT):
     return pltpu.CompilerParams(dimension_semantics=("arbitrary",), vmem_limit_bytes=limit)
 
 
-def prelude(odd, mask, kernels, weights):
-    count = kernels.shape[0]
-    last = mask.shape[0] // HALO - 1
-    edge = jax.ShapeDtypeStruct((HALO, TILE), jnp.float32)
+def analysis(mask, kernels, weights):
+    tiles = mask.shape[0] // TILE
+    tables = jnp.asarray(TABLES["analysis"])
     part = pltpu.VMEM((FB // 2, 2 * FB), jnp.float32)
-    packed = jax.ShapeDtypeStruct((count, FB, 2 * FB), jnp.float32)
+    total = jax.ShapeDtypeStruct((tiles, FB, 4 * FB), jnp.float32)
+    packed = jax.ShapeDtypeStruct((kernels.shape[0], FB, 2 * FB), jnp.float32)
+    edge = jax.ShapeDtypeStruct((FB, 4 * FB), jnp.float32)
     return pl.pallas_call(
-        prelude_kernel,
-        grid=(1,),
-        out_shape=(edge, edge, packed),
+        analysis_kernel,
+        grid=(tiles // PAIR,),
+        out_shape=(total, packed, edge, edge, jax.ShapeDtypeStruct(mask.shape, jnp.float32)),
         in_specs=[
-            pl.BlockSpec(memory_space=pltpu.SMEM),
-            pl.BlockSpec((HALO, TILE), lambda step: (0, 0)),
-            pl.BlockSpec((HALO, TILE), lambda step: (last, 0)),
+            tile_pair(),
             whole(kernels),
             pl.BlockSpec(memory_space=pltpu.SMEM),
+            whole(tables),
         ],
-        out_specs=[whole(edge), whole(edge), whole(packed)],
-        scratch_shapes=[part, part],
-        compiler_params=params(PRELUDE_LIMIT),
-        name="prelude",
-    )(odd, mask, mask, kernels, weights)
+        out_specs=[whole(total), whole(packed), whole(edge), whole(edge), tile_pair()],
+        scratch_shapes=[part, part, pltpu.VMEM((tiles + 2, FB, 4 * FB), jnp.float32)],
+        compiler_params=params(FIRST_LIMIT),
+        name="analysis",
+    )(mask, kernels, weights, tables)
+
+
+def simple_call(kernel, out_shape, *operands, name):
+    vmem = pl.BlockSpec(memory_space=pltpu.VMEM)
+    return pl.pallas_call(
+        kernel,
+        out_shape=out_shape,
+        in_specs=[vmem] * len(operands),
+        out_specs=[vmem] * len(out_shape),
+        compiler_params=pltpu.CompilerParams(vmem_limit_bytes=VMEM_LIMIT),
+        name=name,
+    )(*operands)
+
+
+def merge(total, near_even, near_odd):
+    spectra = jax.ShapeDtypeStruct((total.shape[0], FB, 2 * FB), jnp.float32)
+    return simple_call(
+        merge_kernel, (spectra,) * 3, total, near_even, near_odd, name="merge"
+    )
+
+
+def edges(grad, grad_even, grad_odd):
+    side = jax.ShapeDtypeStruct((FB, 4 * FB), jnp.float32)
+    return simple_call(edges_kernel, (side,) * 2, grad, grad_even, grad_odd, name="edges")
 
 
 def preparation(own, other):
+    tables = jnp.asarray(TABLES["imaging"])
     shape = jax.ShapeDtypeStruct((2 * own.shape[0], FB, 2 * FB), jnp.float32)
+    vmem = pl.BlockSpec(memory_space=pltpu.VMEM)
     return pl.pallas_call(
         preparation_kernel,
-        out_shape=(shape, shape),
-        in_specs=[pl.BlockSpec(memory_space=pltpu.VMEM)] * 2,
-        out_specs=[pl.BlockSpec(memory_space=pltpu.VMEM)] * 2,
+        out_shape=(shape, shape, jax.ShapeDtypeStruct(tables.shape, tables.dtype)),
+        in_specs=[vmem, vmem, pl.BlockSpec(memory_space=pl.ANY)],
+        out_specs=[vmem] * 3,
+        scratch_shapes=[pltpu.SemaphoreType.DMA],
         compiler_params=pltpu.CompilerParams(vmem_limit_bytes=VMEM_LIMIT),
-        cost_estimate=pl.CostEstimate(flops=400000, bytes_accessed=1600000, transcendentals=0),
+        cost_estimate=pl.CostEstimate(flops=400000, bytes_accessed=4000000, transcendentals=0),
         name="preparation",
-    )(own, other)
-
-
-def analysis(odd, mask, halo_even, halo_odd):
-    tiles = mask.shape[0] // TILE
-    tables = jnp.asarray(TABLES["analysis"])
-    spectra = jax.ShapeDtypeStruct((tiles, FB, 2 * FB), jnp.float32)
-    return pl.pallas_call(
-        analysis_kernel,
-        grid=(tiles,),
-        out_shape=(spectra, spectra, spectra, jax.ShapeDtypeStruct(mask.shape, jnp.float32)),
-        in_specs=[
-            pl.BlockSpec(memory_space=pltpu.SMEM),
-            tile_rows(),
-            whole(halo_even),
-            whole(halo_odd),
-            whole(tables),
-        ],
-        out_specs=[whole(spectra)] * 3 + [tile_rows()],
-        scratch_shapes=[pltpu.VMEM((tiles + 2, FB, 4 * FB), jnp.float32)],
-        compiler_params=params(),
-        name="analysis",
-    )(odd, mask, halo_even, halo_odd, tables)
-
-
-def imaging(share, from_even, from_odd, straight, crossed, target):
+    )(own, other, tables)
+
+
+def imaging(share, from_even, from_odd, straight, crossed, tables, target):
     tiles = share.shape[0]
     kernels = straight.shape[0]
-    tables = jnp.asarray(TABLES["imaging"])
-    spectra = pl.BlockSpec((PAIR, FB, 2 * FB), lambda step: (step, 0, 0))
-    pixels = pl.BlockSpec((PAIR * TILE, TILE), lambda step: (step, 0))
+    spectra = pl.BlockSpec((TILES_AT_ONCE, FB, 2 * FB), lambda step: (step, 0, 0))
+    pixels = pl.BlockSpec((TILES_AT_ONCE * TILE, TILE), lambda step: (step, 0))
     return pl.pallas_call(
         imaging_kernel,
-        grid=(tiles // PAIR,),
+        grid=(tiles // TILES_AT_ONCE,),
         out_shape=(
             jax.ShapeDtypeStruct(target.shape, jnp.float32),
             jax.ShapeDtypeStruct(share.shape, jnp.float32),
@@ -510,65 +528,46 @@
         in_specs=[spectra] * 3 + [whole(straight), whole(crossed), pixels, whole(tables)],
         out_specs=[pixels, spectra],
         scratch_shapes=[
-            pltpu.VMEM((PAIR, kernels, COARSE, 2 * COARSE), jnp.float32),
-            pltpu.VMEM((PAIR, 2, kernels // 2 * COARSE, 2 * FB), jnp.float32),
+            pltpu.VMEM((TILES_AT_ONCE, kernels, COARSE, 2 * COARSE), jnp.float32),
+            pltpu.VMEM((TILES_AT_ONCE, 2, kernels // 2 * COARSE, 2 * FB), jnp.float32),
         ],
         compiler_params=params(),
         name="imaging",
     )(share, from_even, from_odd, straight, crossed, target, tables)
 
 
-def edges(odd, grad, grad_even, grad_odd):
-    side = jax.ShapeDtypeStruct((FB, 4 * FB), jnp.float32)
-    vmem = pl.BlockSpec(memory_space=pltpu.VMEM)
-    return pl.pallas_call(
-        edges_kernel,
-        out_shape=(side, side),
-        in_specs=[pl.BlockSpec(memory_space=pltpu.SMEM)] + [vmem] * 3,
-        out_specs=[vmem] * 2,
-        compiler_params=pltpu.CompilerParams(vmem_limit_bytes=VMEM_LIMIT),
-        name="edges",
-    )(odd, grad, grad_even, grad_odd)
-
-
-def inner_synthesis(odd, own, even_in, odd_in, slope):
-    tiles = own.shape[0]
+def inner_synthesis(own, even_in, odd_in, slope):
     tables = jnp.asarray(TABLES["synthesis"])
-    place = pl.BlockSpec((TILE, TILE), lambda step: (step + 1, 0))
+    place = pl.BlockSpec((PAIR * TILE, TILE), lambda step: (1, 0))
     return pl.pallas_call(
         inner_kernel,
-        grid=(tiles - 2,),
+        grid=(1,),
         out_shape=jax.ShapeDtypeStruct(slope.shape, jnp.float32),
-        in_specs=[pl.BlockSpec(memory_space=pltpu.SMEM)]
-        + [whole(own)] * 3
-        + [place, whole(tables)],
+        in_specs=[whole(own)] * 3 + [place, whole(tables)],
         out_specs=place,
-        scratch_shapes=[pltpu.VMEM((tiles, FB, 4 * FB), jnp.float32)],
         compiler_params=params(),
         cost_estimate=pl.CostEstimate(
             flops=1500000000, bytes_accessed=2500000, transcendentals=0
         ),
         name="inner_synthesis",
-    )(odd, own, even_in, odd_in, slope, tables)
-
-
-def outer_synthesis(odd, own, even_in, odd_in, near_even, near_odd, slope, partial):
-    tiles = own.shape[0]
+    )(own, even_in, odd_in, slope, tables)
+
+
+def outer_synthesis(own, even_in, odd_in, near_even, near_odd, slope, partial):
     tables = jnp.asarray(TABLES["synthesis"])
-    place = pl.BlockSpec((TILE, TILE), lambda step: (step * (tiles - 1), 0))
+    place = pl.BlockSpec((PAIR * TILE, TILE), lambda step: (2 * step, 0))
     return pl.pallas_call(
         outer_kernel,
         grid=(2,),
         out_shape=jax.ShapeDtypeStruct(slope.shape, jnp.float32),
-        in_specs=[pl.BlockSpec(memory_space=pltpu.SMEM)]
-        + [whole(own)] * 3
+        in_specs=[whole(own)] * 3
         + [whole(near_even), whole(near_odd), place, whole(tables)]
         + [pl.BlockSpec(memory_space=pl.ANY)],
         out_specs=place,
-        input_output_aliases={8: 0},
+        input_output_aliases={7: 0},
         compiler_params=params(),
         name="outer_synthesis",
-    )(odd, own, even_in, odd_in, near_even, near_odd, slope, tables, partial)
+    )(own, even_in, odd_in, near_even, near_odd, slope, tables, partial)
 
 
 def swap_pairs(count, first):
@@ -579,14 +578,12 @@
 
 
 def local(mask_param, target, kernels, weights):
-    rows, cols = lax.axis_size("gy"), lax.axis_size("gx")
-    odd_row, odd_col = lax.axis_index("gy") % 2, lax.axis_index("gx") % 2
-    odd = jnp.stack([odd_row, odd_col]).astype(jnp.int32)
+    rows = lax.axis_size("gy")
 
     def swap(value, axis, first):
         return lax.ppermute(value, axis, swap_pairs(lax.axis_size(axis), first))
 
-    edge_even, edge_odd, own = prelude(odd, mask_param, kernels, weights)
+    total, own, edge_even, edge_odd, slope = analysis(mask_param, kernels, weights)
     halo_odd = swap(edge_odd, "gy", 1)
     halo_even = swap(edge_even, "gy", 0)
     inner = rows // 4
@@ -595,19 +592,19 @@
         mirror = (3 - place // inner) * inner + place % inner
         pairs += [(2 * place, 2 * mirror + 1), (2 * place + 1, 2 * mirror)]
     other = lax.ppermute(own, ("gy", "ka"), pairs)
-    share, to_even, to_odd, slope = analysis(odd, mask_param, halo_even, halo_odd)
+    share, to_even, to_odd = merge(total, halo_even, halo_odd)
     from_odd = swap(to_odd, "gx", 1)
     from_even = swap(to_even, "gx", 0)
-    straight, crossed = preparation(own, other)
-    resist, grad = imaging(share, from_even, from_odd, straight, crossed, target)
+    straight, crossed, tables = preparation(own, other)
+    resist, grad = imaging(share, from_even, from_odd, straight, crossed, tables, target)
     grad_odd = swap(grad, "gx", 1)
     grad_even = swap(grad, "gx", 0)
-    side_even, side_odd = edges(odd, grad, grad_even, grad_odd)
+    side_even, side_odd = edges(grad, grad_even, grad_odd)
     near_odd = swap(side_odd, "gy", 1)
     near_even = swap(side_even, "gy", 0)
-    partial = inner_synthesis(odd, grad, grad_even, grad_odd, slope)
+    partial = inner_synthesis(grad, grad_even, grad_odd, slope)
     gradient = outer_synthesis(
-        odd, grad, grad_even, grad_odd, near_even, near_odd, slope, partial
+        grad, grad_even, grad_odd, near_even, near_odd, slope, partial
     )
     return (gradient, resist)
 

time: 63.6 us -> 59.1 us (0.929)
  the two profiles are of different devices: /device:TPU:40 before, /device:TPU:18 now
where the time goes in v3:
time: 59.1 us; the launch traced here: 58.7 us
  Pallas kernels  22.9 us (39%)
  starting transfers between devices  20.3 us (34%)
  waiting for transfers between devices  11.5 us (19%)
  local copies, waits for them, and re-layouts  3.21 us (5%)
  between operations  0.76 us (1%)
    ppermute x8, starting transfers between devices, swap(): return lax.ppermute(value, axis, swap_pairs(lax.axis_size(axis), first))  14.4 us
    pallas_call x1, Pallas kernels, imaging(): pl.pallas_call(imaging_kernel, grid=(tiles // TILES_AT_ONCE,), out_shape=...  13.6 us
    ppermute x8, waiting for transfers between devices, swap(): return lax.ppermute(value, axis, swap_pairs(lax.axis_size(axis), first))  6.37 us
    ppermute x1, starting transfers between devices, local(): other = lax.ppermute(own, ('gy', 'ka'), pairs)  5.94 us
    pallas_call x1, Pallas kernels, analysis(): pl.pallas_call(analysis_kernel, grid=(tiles // PAIR,), out_shape=(total,...  5.18 us
    ppermute x1, waiting for transfers between devices, local(): other = lax.ppermute(own, ('gy', 'ka'), pairs)  5.14 us
    unnamed x12, local copies, waits for them, and re-layouts  3.21 us
    pallas_call x1, Pallas kernels, outer_synthesis(): pl.pallas_call(outer_kernel, grid=(2,), out_shape=jax.ShapeDtypeStruct(sl...  2.13 us
  transfers between devices with their start and end apart: 9, of which 3 were waited for; matrix products, arithmetic and copies ran while one was open for 0% of the time, Pallas kernels for 3%

profile of v3, /device:TPU:18, one launch (start us, length us, event | category | flops | bytes accessed | tf_op | source)
XLA Modules:
  0.0 58.7 jit_solution(2931124627692731290)
XLA Ops:
  0.6 5.2 %analysis.1 = (f32[6,64,256]{2,1,0:T(8,128)}, f32[6,64,128]{2,1,0:T(8,128)}, f32[64,256]{1,0:T(8,128)}, f32[64,256]{1,0:T(8,128)}, f32[1536,256]{1,0:T(8,128)}) custom-call(f32[1536,256]{1,0:T(8,128)} %mask.1, f32[6,2,4096]{2,1,0:T(2,128)} %kernels.1, f32[6]{0:T(128)} %weights.1, bf16[1536,128]{1,0:T(8,128)(2,1)} %constant.6.clone.tables), custom_call_target="tpu_custom_call" | custom-call | tf_op jit(solution)/shard_map/analysis/pallas_call | solution.py:459
  5.8 0.5 collective-permute-start
  6.3 4.0 %collective-permute-start.1 = (f32[64,256]{1,0:T(8,128)}, f32[64,256]{1,0:T(8,128)S(1)}, u32[]{:S(2)}, u32[]{:S(2)}) collective-permute-start(f32[64,256]{1,0:T(8,128)} %get-tuple-element.19), channel_id=1, source_target_pairs={{2,4},{4,2},{6,8},{8,6},{10,12},{12,10},{14,16},{16,14},{18,20},{2... | collective-permute-start | bytes 196616 | tf_op jit(solution)/shard_map/ppermute | solution.py:584
  10.4 5.9 %collective-permute-start.4 = (f32[6,64,128]{2,1,0:T(8,128)}, f32[6,64,128]{2,1,0:T(8,128)S(1)}, u32[]{:S(2)}, u32[]{:S(2)}) collective-permute-start(f32[6,64,128]{2,1,0:T(8,128)} %get-tuple-element.23.own), channel_id=1, source_target_pairs={{0,25},{1,24},{2,27},{3,26},{4,29},{5,28},{6,31},{7,30},{8,17},{9,... | collective-permute-start | bytes 589832 | tf_op jit(solution)/shard_map/ppermute | solution.py:594
  16.3 0.0 collective-permute-done.near_even
  16.3 0.0 collective-permute-done.1.near_odd
  16.4 1.0 %copy-done.4 = f32[6,64,256]{2,1,0:T(8,128)S(1)} copy-done((f32[6,64,256]{2,1,0:T(8,128)S(1)}, f32[6,64,256]{2,1,0:T(8,128)}, u32[]{:S(2)}) %copy-start.4) | copy-done | bytes 393240
  17.3 0.1 merge.1
  17.4 0.1 collective-permute-start.2
  17.5 2.5 %collective-permute-start.3 = (f32[6,64,128]{2,1,0:T(8,128)S(1)}, f32[6,64,128]{2,1,0:T(8,128)S(1)}, u32[]{:S(2)}, u32[]{:S(2)}) collective-permute-start(f32[6,64,128]{2,1,0:T(8,128)S(1)} %get-tuple-element.22), channel_id=1, source_target_pairs={{32,64},{64,32},{96,128},{128,96},{160,192},{192,160},{33,65},{65,... | collective-permute-start | bytes 589832 | tf_op jit(solution)/shard_map/ppermute | solution.py:584
  20.0 5.1 %collective-permute-done.4.other = f32[6,64,128]{2,1,0:T(8,128)S(1)} collective-permute-done((f32[6,64,128]{2,1,0:T(8,128)}, f32[6,64,128]{2,1,0:T(8,128)S(1)}, u32[]{:S(2)}, u32[]{:S(2)}) %collective-permute-start.4) | collective-permute-done | bytes 196640 | tf_op jit(solution)/shard_map/ppermute | solution.py:594
  25.1 1.3 %copy-done.2 = bf16[4608,128]{1,0:T(8,128)(2,1)S(1)} copy-done((bf16[4608,128]{1,0:T(8,128)(2,1)S(1)}, bf16[4608,128]{1,0:T(8,128)(2,1)}, u32[]{:S(2)}) %copy-start.2) | copy-done | bytes 1179672
  26.4 0.9 %copy-done.5 = f32[6,64,128]{2,1,0:T(8,128)S(1)} copy-done((f32[6,64,128]{2,1,0:T(8,128)S(1)}, f32[6,64,128]{2,1,0:T(8,128)}, u32[]{:S(2)}) %copy-start.5) | copy-done | bytes 196632
  27.3 0.4 preparation.1
  27.7 0.0 collective-permute-done.2.from_even
  27.8 0.0 collective-permute-done.3.from_odd
  27.8 0.0 copy-done
  27.8 0.0 copy-start.1
  27.8 0.0 copy-start.3
  27.8 13.6 %imaging.1 = (f32[1536,256]{1,0:T(8,128)}, f32[6,64,128]{2,1,0:T(8,128)S(1)}) custom-call(f32[6,64,128]{2,1,0:T(8,128)S(1)} %get-tuple-element.20.share, f32[6,64,128]{2,1,0:T(8,128)S(1)} %collective-permute-done.2.from_even, f32[6,64,128]{2,1,0:T(8,128)S(1)} %collective-permute-done.3.from_odd, f32[12,64,128]{2,1,0:T(8,128)S(1)} %get-tuple-element.24.straight, ...), custom_call_target="tpu_custom_call" | custom-call | tf_op jit(solution)/shard_map/imaging/pallas_call | solution.py:521
  41.4 1.9 %collective-permute-start.6 = (f32[6,64,128]{2,1,0:T(8,128)S(1)}, f32[6,64,128]{2,1,0:T(8,128)S(1)}, u32[]{:S(2)}, u32[]{:S(2)}) collective-permute-start(f32[6,64,128]{2,1,0:T(8,128)S(1)} %get-tuple-element.27.own), channel_id=1, source_target_pairs={{32,64},{64,32},{96,128},{128,96},{160,192},{192,160},{33,65},{65,... | collective-permute-start | bytes 589832 | tf_op jit(solution)/shard_map/ppermute | solution.py:584
  43.4 1.5 %collective-permute-start.5 = (f32[6,64,128]{2,1,0:T(8,128)S(1)}, f32[6,64,128]{2,1,0:T(8,128)S(1)}, u32[]{:S(2)}, u32[]{:S(2)}) collective-permute-start(f32[6,64,128]{2,1,0:T(8,128)S(1)} %get-tuple-element.27.own), channel_id=1, source_target_pairs={{0,32},{32,0},{64,96},{96,64},{128,160},{160,128},{192,224},{224,1... | collective-permute-start | bytes 589832 | tf_op jit(solution)/shard_map/ppermute | solution.py:584
  44.8 3.6 %collective-permute-done.6.odd_in = f32[6,64,128]{2,1,0:T(8,128)S(1)} collective-permute-done((f32[6,64,128]{2,1,0:T(8,128)S(1)}, f32[6,64,128]{2,1,0:T(8,128)S(1)}, u32[]{:S(2)}, u32[]{:S(2)}) %collective-permute-start.6) | collective-permute-done | bytes 196640 | tf_op jit(solution)/shard_map/ppermute | solution.py:584
  48.4 0.0 collective-permute-done.5.even_in
  48.5 2.0 %collective-permute-start.7 = (f32[64,256]{1,0:T(8,128)S(1)}, f32[64,256]{1,0:T(8,128)S(1)}, u32[]{:S(2)}, u32[]{:S(2)}) collective-permute-start(f32[64,256]{1,0:T(8,128)S(1)} %get-tuple-element.28), channel_id=1, source_target_pairs={{0,2},{2,0},{4,6},{6,4},{8,10},{10,8},{12,14},{14,12},{16,18},{18,... | collective-permute-start | bytes 196616 | tf_op jit(solution)/shard_map/ppermute | solution.py:584
  50.4 1.9 %collective-permute-start.8 = (f32[64,256]{1,0:T(8,128)S(1)}, f32[64,256]{1,0:T(8,128)S(1)}, u32[]{:S(2)}, u32[]{:S(2)}) collective-permute-start(f32[64,256]{1,0:T(8,128)S(1)} %get-tuple-element.29), channel_id=1, source_target_pairs={{2,4},{4,2},{6,8},{8,6},{10,12},{12,10},{14,16},{16,14},{18,20},{2... | collective-permute-start | bytes 196616 | tf_op jit(solution)/shard_map/ppermute | solution.py:584
  52.3 0.0 copy-done.1
  52.4 0.0 copy-done.3
  52.4 1.4 %inner_synthesis.1.partial = f32[1536,256]{1,0:T(8,128)} custom-call(f32[6,64,128]{2,1,0:T(8,128)S(1)} %get-tuple-element.27.own, f32[6,64,128]{2,1,0:T(8,128)S(1)} %collective-permute-done.5.even_in, f32[6,64,128]{2,1,0:T(8,128)S(1)} %collective-permute-done.6.odd_in, f32[1536,256]{1,0:T(8,128)S(1)} %copy-done.1, bf16[1536,128]{1,0:T(8,128)(2,1)S(1)} %copy-done.3), custom_call_target="tpu_custom_call" | custom-call | flops 1500000000 | bytes 2500000 | tf_op jit(solution)/shard_map/inner_synthesis/pallas_call | solution.py:542
  53.8 0.0 collective-permute-done.7.near_even
  53.8 2.8 %collective-permute-done.8.near_odd = f32[64,256]{1,0:T(8,128)S(1)} collective-permute-done((f32[64,256]{1,0:T(8,128)S(1)}, f32[64,256]{1,0:T(8,128)S(1)}, u32[]{:S(2)}, u32[]{:S(2)}) %collective-permute-start.8) | collective-permute-done | bytes 65568 | tf_op jit(solution)/shard_map/ppermute | solution.py:584
  56.6 2.1 %outer_synthesis.1 = f32[1536,256]{1,0:T(8,128)} custom-call(f32[6,64,128]{2,1,0:T(8,128)S(1)} %get-tuple-element.27.own, f32[6,64,128]{2,1,0:T(8,128)S(1)} %collective-permute-done.5.even_in, f32[6,64,128]{2,1,0:T(8,128)S(1)} %collective-permute-done.6.odd_in, f32[64,256]{1,0:T(8,128)S(1)} %collective-permute-done.7.near_even, ...), custom_call_target="tpu_custom_call", output_to_operand_aliasing={{}: (7, {})} | custom-call | tf_op jit(solution)/shard_map/outer_synthesis/pallas_call | solution.py:559
  (5 shorter events, 0.0 us)
Async XLA Ops:
  5.8 22.0 %copy-start = (s32[1536,256]{1,0:T(8,128)S(1)}, s32[1536,256]{1,0:T(8,128)}, u32[]{:S(2)}) copy-start(s32[1536,256]{1,0:T(8,128)} %target.1) | copy-start | bytes 4718596
  5.8 10.5 %collective-permute-start = (f32[64,256]{1,0:T(8,128)}, f32[64,256]{1,0:T(8,128)S(1)}, u32[]{:S(2)}, u32[]{:S(2)}) collective-permute-start(f32[64,256]{1,0:T(8,128)} %get-tuple-element.18), channel_id=1, source_target_pairs={{0,2},{2,0},{4,6},{6,4},{8,10},{10,8},{12,14},{14,12},{16,18},{18,... | collective-permute-start | bytes 196616 | tf_op jit(solution)/shard_map/ppermute | solution.py:584
  6.3 10.0 %collective-permute-start.1 = (f32[64,256]{1,0:T(8,128)}, f32[64,256]{1,0:T(8,128)S(1)}, u32[]{:S(2)}, u32[]{:S(2)}) collective-permute-start(f32[64,256]{1,0:T(8,128)} %get-tuple-element.19), channel_id=1, source_target_pairs={{2,4},{4,2},{6,8},{8,6},{10,12},{12,10},{14,16},{16,14},{18,20},{2... | collective-permute-start | bytes 196616 | tf_op jit(solution)/shard_map/ppermute | solution.py:584
  10.4 14.7 %collective-permute-start.4 = (f32[6,64,128]{2,1,0:T(8,128)}, f32[6,64,128]{2,1,0:T(8,128)S(1)}, u32[]{:S(2)}, u32[]{:S(2)}) collective-permute-start(f32[6,64,128]{2,1,0:T(8,128)} %get-tuple-element.23.own), channel_id=1, source_target_pairs={{0,25},{1,24},{2,27},{3,26},{4,29},{5,28},{6,31},{7,30},{8,17},{9,... | collective-permute-start | bytes 589832 | tf_op jit(solution)/shard_map/ppermute | solution.py:594
  16.3 1.0 %copy-start.4 = (f32[6,64,256]{2,1,0:T(8,128)S(1)}, f32[6,64,256]{2,1,0:T(8,128)}, u32[]{:S(2)}) copy-start(f32[6,64,256]{2,1,0:T(8,128)} %get-tuple-element.17.total) | copy-start | bytes 1179652
  17.4 10.3 %collective-permute-start.2 = (f32[6,64,128]{2,1,0:T(8,128)S(1)}, f32[6,64,128]{2,1,0:T(8,128)S(1)}, u32[]{:S(2)}, u32[]{:S(2)}) collective-permute-start(f32[6,64,128]{2,1,0:T(8,128)S(1)} %get-tuple-element.21), channel_id=1, source_target_pairs={{0,32},{32,0},{64,96},{96,64},{128,160},{160,128},{192,224},{224,1... | collective-permute-start | bytes 589832 | tf_op jit(solution)/shard_map/ppermute | solution.py:584
  17.5 10.2 %collective-permute-start.3 = (f32[6,64,128]{2,1,0:T(8,128)S(1)}, f32[6,64,128]{2,1,0:T(8,128)S(1)}, u32[]{:S(2)}, u32[]{:S(2)}) collective-permute-start(f32[6,64,128]{2,1,0:T(8,128)S(1)} %get-tuple-element.22), channel_id=1, source_target_pairs={{32,64},{64,32},{96,128},{128,96},{160,192},{192,160},{33,65},{65,... | collective-permute-start | bytes 589832 | tf_op jit(solution)/shard_map/ppermute | solution.py:584
  25.1 1.3 %copy-start.2 = (bf16[4608,128]{1,0:T(8,128)(2,1)S(1)}, bf16[4608,128]{1,0:T(8,128)(2,1)}, u32[]{:S(2)}) copy-start(bf16[4608,128]{1,0:T(8,128)(2,1)} %constant.7.clone.tables) | copy-start | bytes 3538948
  26.4 0.9 %copy-start.5 = (f32[6,64,128]{2,1,0:T(8,128)S(1)}, f32[6,64,128]{2,1,0:T(8,128)}, u32[]{:S(2)}) copy-start(f32[6,64,128]{2,1,0:T(8,128)} %get-tuple-element.23.own) | copy-start | bytes 589828
  27.8 24.6 %copy-start.1 = (f32[1536,256]{1,0:T(8,128)S(1)}, f32[1536,256]{1,0:T(8,128)}, u32[]{:S(2)}) copy-start(f32[1536,256]{1,0:T(8,128)} %get-tuple-element.30.slope) | copy-start | bytes 4718596
  27.8 24.6 %copy-start.3 = (bf16[1536,128]{1,0:T(8,128)(2,1)S(1)}, bf16[1536,128]{1,0:T(8,128)(2,1)}, u32[]{:S(2)}) copy-start(bf16[1536,128]{1,0:T(8,128)(2,1)} %constant.8.clone.tables) | copy-start | bytes 1179652
  41.4 7.0 %collective-permute-start.6 = (f32[6,64,128]{2,1,0:T(8,128)S(1)}, f32[6,64,128]{2,1,0:T(8,128)S(1)}, u32[]{:S(2)}, u32[]{:S(2)}) collective-permute-start(f32[6,64,128]{2,1,0:T(8,128)S(1)} %get-tuple-element.27.own), channel_id=1, source_target_pairs={{32,64},{64,32},{96,128},{128,96},{160,192},{192,160},{33,65},{65,... | collective-permute-start | bytes 589832 | tf_op jit(solution)/shard_map/ppermute | solution.py:584
  43.4 5.1 %collective-permute-start.5 = (f32[6,64,128]{2,1,0:T(8,128)S(1)}, f32[6,64,128]{2,1,0:T(8,128)S(1)}, u32[]{:S(2)}, u32[]{:S(2)}) collective-permute-start(f32[6,64,128]{2,1,0:T(8,128)S(1)} %get-tuple-element.27.own), channel_id=1, source_target_pairs={{0,32},{32,0},{64,96},{96,64},{128,160},{160,128},{192,224},{224,1... | collective-permute-start | bytes 589832 | tf_op jit(solution)/shard_map/ppermute | solution.py:584
  48.5 5.3 %collective-permute-start.7 = (f32[64,256]{1,0:T(8,128)S(1)}, f32[64,256]{1,0:T(8,128)S(1)}, u32[]{:S(2)}, u32[]{:S(2)}) collective-permute-start(f32[64,256]{1,0:T(8,128)S(1)} %get-tuple-element.28), channel_id=1, source_target_pairs={{0,2},{2,0},{4,6},{6,4},{8,10},{10,8},{12,14},{14,12},{16,18},{18,... | collective-permute-start | bytes 196616 | tf_op jit(solution)/shard_map/ppermute | solution.py:584
  50.4 6.1 %collective-permute-start.8 = (f32[64,256]{1,0:T(8,128)S(1)}, f32[64,256]{1,0:T(8,128)S(1)}, u32[]{:S(2)}, u32[]{:S(2)}) collective-permute-start(f32[64,256]{1,0:T(8,128)S(1)} %get-tuple-element.29), channel_id=1, source_target_pairs={{2,4},{4,2},{6,8},{8,6},{10,12},{12,10},{14,16},{16,14},{18,20},{2... | collective-permute-start | bytes 196616 | tf_op jit(solution)/shard_map/ppermute | solution.py:584

commit v4 on v3

--- a/solution.py
+++ b/solution.py
@@ -18,7 +18,7 @@
 VMEM_LIMIT = 32 * 1024 * 1024
 PAIR = 2
 TILES_AT_ONCE = 3
-FIRST_LIMIT = 63 * 1024 * 1024
+FIRST_LIMIT = 60 * 1024 * 1024
 
 bf16 = ml_dtypes.bfloat16
 
@@ -195,18 +195,25 @@
     return pltpu.roll(value, FB, 1)
 
 
-def preparation_kernel(own, other, tables, straight, crossed, loaded, semaphore):
-    copy = pltpu.make_async_copy(tables, loaded, semaphore)
-    copy.start()
-    count = own.shape[0]
+def factors(spectrum):
     lanes = low_lanes((FB, 2 * FB))
-    for group, source in enumerate((own, other)):
-        for index in range(count):
-            spectrum = source[index]
-            turned = swapped(spectrum)
-            straight[group * count + index] = jnp.where(lanes, spectrum, turned)
-            crossed[group * count + index] = jnp.where(lanes, -turned, spectrum)
-    copy.wait()
+    turned = swapped(spectrum)
+    return jnp.where(lanes, spectrum, turned), jnp.where(lanes, -turned, spectrum)
+
+
+def own_kernel(own, straight, crossed):
+    for index in range(own.shape[0]):
+        straight[index], crossed[index] = factors(own[index])
+
+
+def other_kernel(mine, partners, straight, crossed):
+    odd_col = is_odd("gx")
+    half = mine.shape[0]
+    for index in range(half):
+        first = jnp.where(odd_col, partners[index], mine[index])
+        second = jnp.where(odd_col, mine[index], partners[index])
+        straight[index], crossed[index] = factors(first)
+        straight[half + index], crossed[half + index] = factors(second)
 
 
 def pack_kernels(kernels, weights, packed, real, imag):
@@ -243,17 +250,40 @@
 
 
 def analysis_kernel(
-    mask, kernels, weights, tables, total, packed, edge_even, edge_odd, slope, real, imag, sums
+    mask_in, kernels_in, weights, tables_in,
+    total, packed, half, edge_even, edge_odd, slope,
+    real, imag, sums, mask, kernels, tables, semaphores,
 ):
     step = pl.program_id(0)
     count = total.shape[0]
 
+    def pixels_copy(step):
+        place = pl.ds(pl.multiple_of(step * PAIR * TILE, TILE), PAIR * TILE)
+        return pltpu.make_async_copy(
+            mask_in.at[place, :], mask.at[place, :], semaphores.at[step]
+        )
+
     @pl.when(step == 0)
     def _():
+        table_copy = pltpu.make_async_copy(tables_in, tables, semaphores.at[count // PAIR])
+        kernel_copy = pltpu.make_async_copy(
+            kernels_in, kernels, semaphores.at[count // PAIR + 1]
+        )
+        kernel_copy.start()
+        pixels_copy(0).start()
+        table_copy.start()
+        for later in range(1, count // PAIR):
+            pixels_copy(later).start()
         sums[...] = jnp.zeros_like(sums)
+        kernel_copy.wait()
         pack_kernels(kernels, weights, packed, real, imag)
-
-    transmit = jnp.tanh(mask[...])
+        size = half.shape[0]
+        for index in range(size):
+            half[index] = jnp.where(is_odd("gx"), packed[size + index], packed[index])
+        table_copy.wait()
+
+    pixels_copy(step).wait()
+    transmit = jnp.tanh(mask[pl.ds(pl.multiple_of(step * PAIR * TILE, TILE), PAIR * TILE), :])
     slope[...] = 1.0 - transmit * transmit
     found = block_spectra(transmit, tables)
     flip = row_parity((FB, 4 * FB))
@@ -273,28 +303,39 @@
         edge_odd[...] = jnp.where(odd_row, down, up)
 
 
-def merge_kernel(total, near_even, near_odd, share, to_even, to_odd):
-    count = share.shape[0]
-    odd_row, odd_col = is_odd("gy"), is_odd("gx")
-    above = jnp.where(odd_row, near_even[...], near_odd[...])
-    below = jnp.where(odd_row, near_odd[...], near_even[...])
-    for index in range(count):
-        both = total[index]
-        if index == 0:
-            both = both + above
-        if index == count - 1:
-            both = both + below
-        left, right = both[:, : 2 * FB], both[:, 2 * FB :]
+def shares_kernel(total, share, to_even, to_odd):
+    odd_col = is_odd("gx")
+    for index in range(share.shape[0]):
+        left, right = total[index, :, : 2 * FB], total[index, :, 2 * FB :]
         share[index] = parity((FB, 2 * FB)) * (left + right)
         to_even[index] = jnp.where(odd_col, left, right)
         to_odd[index] = jnp.where(odd_col, right, left)
 
 
+def merge_kernel(
+    share_in, to_even_in, to_odd_in, near_even, near_odd, share, to_even, to_odd
+):
+    count = share.shape[0]
+    odd_row, odd_col = is_odd("gy"), is_odd("gx")
+    share[...] = share_in[...]
+    to_even[...] = to_even_in[...]
+    to_odd[...] = to_odd_in[...]
+    above = jnp.where(odd_row, near_even[...], near_odd[...])
+    below = jnp.where(odd_row, near_odd[...], near_even[...])
+    for index, near in ((0, above), (count - 1, below)):
+        left, right = near[:, : 2 * FB], near[:, 2 * FB :]
+        share[index] += parity((FB, 2 * FB)) * (left + right)
+        to_even[index] += jnp.where(odd_col, left, right)
+        to_odd[index] += jnp.where(odd_col, right, left)
+
+
 def imaging_kernel(
-    share, from_even, from_odd, straight, crossed, target, wide,
-    resist_ref, grad, fields, sides,
+    share, from_even, from_odd, straight_own, crossed_own, straight_other, crossed_other,
+    target, wide, resist_out, grad, fields, sides, resists, semaphores,
 ):
-    count = straight.shape[0] // 2
+    count = straight_own.shape[0]
+    straights, crosseds = (straight_own, straight_other), (crossed_own, crossed_other)
+    copies = []
     sign = jnp.where(low_lanes((HALF, 2 * FB)), 1.0, -1.0)
     tiles = range(share.shape[0])
     weights = []
@@ -306,7 +347,7 @@
         for group in range(2):
             first = group * count
             products = [
-                straight[first + i] * spectrum + crossed[first + i] * turned
+                straights[group][i] * spectrum + crosseds[group][i] * turned
                 for i in range(count)
             ]
             rows = times_table(jnp.concatenate(products, axis=0), wide_table(wide, SPREAD))
@@ -331,7 +372,15 @@
         fine = stacked_times(wide_table(wide, FINE_LEFT), half_fine)
         resist = jax.nn.sigmoid(4.0 * (fine - 1.0))
         place = slice(tile * TILE, (tile + 1) * TILE)
-        resist_ref[place, :] = resist
+        resists[place, :] = resist
+        start = (pl.program_id(0) * len(tiles) + tile) * TILE
+        copy = pltpu.make_async_copy(
+            resists.at[pl.ds(tile * TILE, TILE), :],
+            resist_out.at[pl.ds(pl.multiple_of(start, TILE), TILE), :],
+            semaphores.at[tile],
+        )
+        copy.start()
+        copies.append(copy)
         misfit = resist - target[place, :].astype(jnp.float32)
         push = 16.0 * misfit * resist * (1.0 - resist)
         high, low = split(push)
@@ -365,10 +414,13 @@
                 for j in (0, 1):
                     part = found[:, j * 2 * FB : (j + 1) * 2 * FB]
                     total = total + (
-                        straight[first + i + j] * part - crossed[first + i + j] * swapped(part)
+                        straights[group][i + j] * part - crosseds[group][i + j] * swapped(part)
                     )
             adjoint.append(total)
         grad[tile] = adjoint[0] + adjoint[1]
+
+    for copy in copies:
+        copy.wait()
 
 
 def sides_of(even_in, odd_in, index):
@@ -455,19 +507,30 @@
     part = pltpu.VMEM((FB // 2, 2 * FB), jnp.float32)
     total = jax.ShapeDtypeStruct((tiles, FB, 4 * FB), jnp.float32)
     packed = jax.ShapeDtypeStruct((kernels.shape[0], FB, 2 * FB), jnp.float32)
+    half = jax.ShapeDtypeStruct((kernels.shape[0] // 2, FB, 2 * FB), jnp.float32)
     edge = jax.ShapeDtypeStruct((FB, 4 * FB), jnp.float32)
     return pl.pallas_call(
         analysis_kernel,
         grid=(tiles // PAIR,),
-        out_shape=(total, packed, edge, edge, jax.ShapeDtypeStruct(mask.shape, jnp.float32)),
+        out_shape=(
+            total, packed, half, edge, edge, jax.ShapeDtypeStruct(mask.shape, jnp.float32)
+        ),
         in_specs=[
-            tile_pair(),
-            whole(kernels),
+            pl.BlockSpec(memory_space=pltpu.HBM),
+            pl.BlockSpec(memory_space=pltpu.HBM),
             pl.BlockSpec(memory_space=pltpu.SMEM),
-            whole(tables),
+            pl.BlockSpec(memory_space=pltpu.HBM),
         ],
-        out_specs=[whole(total), whole(packed), whole(edge), whole(edge), tile_pair()],
-        scratch_shapes=[part, part, pltpu.VMEM((tiles + 2, FB, 4 * FB), jnp.float32)],
+        out_specs=[whole(out) for out in (total, packed, half, edge, edge)] + [tile_pair()],
+        scratch_shapes=[
+            part,
+            part,
+            pltpu.VMEM((tiles + 2, FB, 4 * FB), jnp.float32),
+            pltpu.VMEM(mask.shape, mask.dtype),
+            pltpu.VMEM(kernels.shape, kernels.dtype),
+            pltpu.VMEM(tables.shape, tables.dtype),
+            pltpu.SemaphoreType.DMA((tiles // PAIR + 2,)),
+        ],
         compiler_params=params(FIRST_LIMIT),
         name="analysis",
     )(mask, kernels, weights, tables)
@@ -485,10 +548,15 @@
     )(*operands)
 
 
-def merge(total, near_even, near_odd):
+def shares(total):
     spectra = jax.ShapeDtypeStruct((total.shape[0], FB, 2 * FB), jnp.float32)
+    return simple_call(shares_kernel, (spectra,) * 3, total, name="shares")
+
+
+def merge(share, to_even, to_odd, near_even, near_odd):
+    spectra = jax.ShapeDtypeStruct(share.shape, jnp.float32)
     return simple_call(
-        merge_kernel, (spectra,) * 3, total, near_even, near_odd, name="merge"
+        merge_kernel, (spectra,) * 3, share, to_even, to_odd, near_even, near_odd, name="merge"
     )
 
 
@@ -497,25 +565,20 @@
     return simple_call(edges_kernel, (side,) * 2, grad, grad_even, grad_odd, name="edges")
 
 
-def preparation(own, other):
+def prepare_own(own):
+    shape = jax.ShapeDtypeStruct(own.shape, jnp.float32)
+    return simple_call(own_kernel, (shape, shape), own, name="prepare_own")
+
+
+def prepare_other(mine, partners):
+    shape = jax.ShapeDtypeStruct((2 * mine.shape[0],) + mine.shape[1:], jnp.float32)
+    return simple_call(other_kernel, (shape, shape), mine, partners, name="prepare_other")
+
+
+def imaging(share, from_even, from_odd, own, other, target):
+    tiles = share.shape[0]
+    kernels = 2 * own[0].shape[0]
     tables = jnp.asarray(TABLES["imaging"])
-    shape = jax.ShapeDtypeStruct((2 * own.shape[0], FB, 2 * FB), jnp.float32)
-    vmem = pl.BlockSpec(memory_space=pltpu.VMEM)
-    return pl.pallas_call(
-        preparation_kernel,
-        out_shape=(shape, shape, jax.ShapeDtypeStruct(tables.shape, tables.dtype)),
-        in_specs=[vmem, vmem, pl.BlockSpec(memory_space=pl.ANY)],
-        out_specs=[vmem] * 3,
-        scratch_shapes=[pltpu.SemaphoreType.DMA],
-        compiler_params=pltpu.CompilerParams(vmem_limit_bytes=VMEM_LIMIT),
-        cost_estimate=pl.CostEstimate(flops=400000, bytes_accessed=4000000, transcendentals=0),
-        name="preparation",
-    )(own, other, tables)
-
-
-def imaging(share, from_even, from_odd, straight, crossed, tables, target):
-    tiles = share.shape[0]
-    kernels = straight.shape[0]
     spectra = pl.BlockSpec((TILES_AT_ONCE, FB, 2 * FB), lambda step: (step, 0, 0))
     pixels = pl.BlockSpec((TILES_AT_ONCE * TILE, TILE), lambda step: (step, 0))
     return pl.pallas_call(
@@ -525,15 +588,17 @@
             jax.ShapeDtypeStruct(target.shape, jnp.float32),
             jax.ShapeDtypeStruct(share.shape, jnp.float32),
         ),
-        in_specs=[spectra] * 3 + [whole(straight), whole(crossed), pixels, whole(tables)],
-        out_specs=[pixels, spectra],
+        in_specs=[spectra] * 3 + [whole(own[0])] * 4 + [pixels, whole(tables)],
+        out_specs=[pl.BlockSpec(memory_space=pl.ANY), spectra],
         scratch_shapes=[
             pltpu.VMEM((TILES_AT_ONCE, kernels, COARSE, 2 * COARSE), jnp.float32),
             pltpu.VMEM((TILES_AT_ONCE, 2, kernels // 2 * COARSE, 2 * FB), jnp.float32),
+            pltpu.VMEM((TILES_AT_ONCE * TILE, TILE), jnp.float32),
+            pltpu.SemaphoreType.DMA((TILES_AT_ONCE,)),
         ],
         compiler_params=params(),
         name="imaging",
-    )(share, from_even, from_odd, straight, crossed, target, tables)
+    )(share, from_even, from_odd, *own, *other, target, tables)
 
 
 def inner_synthesis(own, even_in, odd_in, slope):
@@ -583,20 +648,22 @@
     def swap(value, axis, first):
         return lax.ppermute(value, axis, swap_pairs(lax.axis_size(axis), first))
 
-    total, own, edge_even, edge_odd, slope = analysis(mask_param, kernels, weights)
-    halo_odd = swap(edge_odd, "gy", 1)
-    halo_even = swap(edge_even, "gy", 0)
+    total, packed, half, edge_even, edge_odd, slope = analysis(mask_param, kernels, weights)
     inner = rows // 4
     pairs = []
     for place in range(rows):
         mirror = (3 - place // inner) * inner + place % inner
         pairs += [(2 * place, 2 * mirror + 1), (2 * place + 1, 2 * mirror)]
-    other = lax.ppermute(own, ("gy", "ka"), pairs)
-    share, to_even, to_odd = merge(total, halo_even, halo_odd)
+    mine = lax.ppermute(half, ("gy", "ka"), pairs)
+    halo_odd = swap(edge_odd, "gy", 1)
+    halo_even = swap(edge_even, "gy", 0)
+    share, to_even, to_odd = merge(*shares(total), halo_even, halo_odd)
     from_odd = swap(to_odd, "gx", 1)
     from_even = swap(to_even, "gx", 0)
-    straight, crossed, tables = preparation(own, other)
-    resist, grad = imaging(share, from_even, from_odd, straight, crossed, tables, target)
+    own = prepare_own(packed)
+    partners = swap(mine, "gx", 0)
+    other = prepare_other(mine, partners)
+    resist, grad = imaging(share, from_even, from_odd, own, other, target)
     grad_odd = swap(grad, "gx", 1)
     grad_even = swap(grad, "gx", 0)
     side_even, side_odd = edges(grad, grad_even, grad_odd)

time: 59.1 us -> 57.9 us (0.980)
  the two profiles are of different devices: /device:TPU:18 before, /device:TPU:40 now
where the time goes in v4:
time: 57.9 us; the launch traced here: 57.7 us
  Pallas kernels  23 us (40%)
  starting transfers between devices  21.7 us (37%)
  waiting for transfers between devices  10.2 us (18%)
  local copies, waits for them, and re-layouts  1.94 us (3%)
  between operations  0.81 us (1%)
    ppermute x9, starting transfers between devices, swap(): return lax.ppermute(value, axis, swap_pairs(lax.axis_size(axis), first))  14.9 us
    pallas_call x1, Pallas kernels, imaging(): pl.pallas_call(imaging_kernel, grid=(tiles // TILES_AT_ONCE,), out_shape=...  13.6 us
    ppermute x9, waiting for transfers between devices, swap(): return lax.ppermute(value, axis, swap_pairs(lax.axis_size(axis), first))  10.2 us
    ppermute x1, starting transfers between devices, local(): mine = lax.ppermute(half, ('gy', 'ka'), pairs)  6.83 us
    pallas_call x1, Pallas kernels, analysis(): pl.pallas_call(analysis_kernel, grid=(tiles // PAIR,), out_shape=(total,...  5.42 us
    pallas_call x1, Pallas kernels, outer_synthesis(): pl.pallas_call(outer_kernel, grid=(2,), out_shape=jax.ShapeDtypeStruct(sl...  2.12 us
    unnamed x12, local copies, waits for them, and re-layouts  1.94 us
    pallas_call x1, Pallas kernels, inner_synthesis(): pl.pallas_call(inner_kernel, grid=(1,), out_shape=jax.ShapeDtypeStruct(sl...  1.44 us
  transfers between devices with their start and end apart: 10, of which 4 were waited for; matrix products, arithmetic and copies ran while one was open for 0% of the time, Pallas kernels for 3%

profile of v4, /device:TPU:40, one launch (start us, length us, event | category | flops | bytes accessed | tf_op | source)
XLA Modules:
  0.0 57.7 jit_solution(15323616055489595851)
XLA Ops:
  0.6 0.0 copy-start.2
  0.7 5.4 %analysis.1 = (f32[6,64,256]{2,1,0:T(8,128)}, f32[6,64,128]{2,1,0:T(8,128)}, f32[3,64,128]{2,1,0:T(8,128)}, f32[64,256]{1,0:T(8,128)}, f32[64,256]{1,0:T(8,128)}, /*index=5*/f32[1536,256]{1,0:T(8,128)}) custom-call(f32[1536,256]{1,0:T(8,128)} %mask_in.1, f32[6,2,4096]{2,1,0:T(2,128)} %kernels_in.1, f32[6]{0:T(128)} %weights.1, ...), custom_call_target="tpu_custom_call" | custom-call | tf_op jit(solution)/shard_map/analysis/pallas_call | solution.py:512
  6.1 1.6 %collective-permute-start = (f32[64,256]{1,0:T(8,128)}, f32[64,256]{1,0:T(8,128)S(1)}, u32[]{:S(2)}, u32[]{:S(2)}) collective-permute-start(f32[64,256]{1,0:T(8,128)} %get-tuple-element.26), channel_id=1, source_target_pairs={{0,2},{2,0},{4,6},{6,4},{8,10},{10,8},{12,14},{14,12},{16,18},{18,... | collective-permute-start | bytes 196616 | tf_op jit(solution)/shard_map/ppermute | solution.py:649
  7.7 3.5 %collective-permute-start.1 = (f32[64,256]{1,0:T(8,128)}, f32[64,256]{1,0:T(8,128)S(1)}, u32[]{:S(2)}, u32[]{:S(2)}) collective-permute-start(f32[64,256]{1,0:T(8,128)} %get-tuple-element.27), channel_id=1, source_target_pairs={{2,4},{4,2},{6,8},{8,6},{10,12},{12,10},{14,16},{16,14},{18,20},{2... | collective-permute-start | bytes 196616 | tf_op jit(solution)/shard_map/ppermute | solution.py:649
  11.2 6.8 %collective-permute-start.4 = (f32[3,64,128]{2,1,0:T(8,128)}, f32[3,64,128]{2,1,0:T(8,128)S(1)}, u32[]{:S(2)}, u32[]{:S(2)}) collective-permute-start(f32[3,64,128]{2,1,0:T(8,128)} %get-tuple-element.34), channel_id=1, source_target_pairs={{0,25},{1,24},{2,27},{3,26},{4,29},{5,28},{6,31},{7,30},{8,17},{9,... | collective-permute-start | bytes 294920 | tf_op jit(solution)/shard_map/ppermute | solution.py:657
  18.0 1.0 %copy-done.4 = f32[6,64,256]{2,1,0:T(8,128)S(1)} copy-done((f32[6,64,256]{2,1,0:T(8,128)S(1)}, f32[6,64,256]{2,1,0:T(8,128)}, u32[]{:S(2)}) %copy-start.4) | copy-done | bytes 393240
  19.0 0.1 shares.1
  19.1 0.0 collective-permute-done.near_even
  19.1 0.0 collective-permute-done.1.near_odd
  19.1 0.1 merge.1
  19.2 0.1 collective-permute-start.2
  19.3 2.5 %collective-permute-start.3 = (f32[6,64,128]{2,1,0:T(8,128)S(1)}, f32[6,64,128]{2,1,0:T(8,128)S(1)}, u32[]{:S(2)}, u32[]{:S(2)}) collective-permute-start(f32[6,64,128]{2,1,0:T(8,128)S(1)} %get-tuple-element.30), channel_id=1, source_target_pairs={{32,64},{64,32},{96,128},{128,96},{160,192},{192,160},{33,65},{65,... | collective-permute-start | bytes 589832 | tf_op jit(solution)/shard_map/ppermute | solution.py:649
  21.7 0.0 collective-permute-done.4.mine
  21.7 1.2 %collective-permute-start.5 = (f32[3,64,128]{2,1,0:T(8,128)S(1)}, f32[3,64,128]{2,1,0:T(8,128)S(1)}, u32[]{:S(2)}, u32[]{:S(2)}) collective-permute-start(f32[3,64,128]{2,1,0:T(8,128)S(1)} %collective-permute-done.4.mine), channel_id=1, source_target_pairs={{0,32},{32,0},{64,96},{96,64},{128,160},{160,128},{192,224},{224,1... | collective-permute-start | bytes 294920 | tf_op jit(solution)/shard_map/ppermute | solution.py:649
  23.0 0.9 %copy-done.5 = f32[6,64,128]{2,1,0:T(8,128)S(1)} copy-done((f32[6,64,128]{2,1,0:T(8,128)S(1)}, f32[6,64,128]{2,1,0:T(8,128)}, u32[]{:S(2)}) %copy-start.5) | copy-done | bytes 196632
  23.9 0.1 prepare_own.1
  24.0 0.0 collective-permute-done.5.partners
  24.0 0.1 prepare_other.1
  24.2 0.0 collective-permute-done.2.from_even
  24.2 2.1 %collective-permute-done.3.from_odd = f32[6,64,128]{2,1,0:T(8,128)S(1)} collective-permute-done((f32[6,64,128]{2,1,0:T(8,128)S(1)}, f32[6,64,128]{2,1,0:T(8,128)S(1)}, u32[]{:S(2)}, u32[]{:S(2)}) %collective-permute-start.3) | collective-permute-done | bytes 196640 | tf_op jit(solution)/shard_map/ppermute | solution.py:649
  26.3 13.6 %imaging.1 = (f32[1536,256]{1,0:T(8,128)}, f32[6,64,128]{2,1,0:T(8,128)S(1)}) custom-call(f32[6,64,128]{2,1,0:T(8,128)S(1)} %get-tuple-element.28.share, f32[6,64,128]{2,1,0:T(8,128)S(1)} %collective-permute-done.2.from_even, f32[6,64,128]{2,1,0:T(8,128)S(1)} %collective-permute-done.3.from_odd, f32[6,64,128]{2,1,0:T(8,128)S(1)} %get-tuple-element.32.straight_own, ...), custom_call_target="tpu_custom_call" | custom-call | tf_op jit(solution)/shard_map/imaging/pallas_call | solution.py:584
  39.9 2.5 %collective-permute-start.7 = (f32[6,64,128]{2,1,0:T(8,128)S(1)}, f32[6,64,128]{2,1,0:T(8,128)S(1)}, u32[]{:S(2)}, u32[]{:S(2)}) collective-permute-start(f32[6,64,128]{2,1,0:T(8,128)S(1)} %get-tuple-element.37.own), channel_id=1, source_target_pairs={{32,64},{64,32},{96,128},{128,96},{160,192},{192,160},{33,65},{65,... | collective-permute-start | bytes 589832 | tf_op jit(solution)/shard_map/ppermute | solution.py:649
  42.4 1.2 %collective-permute-start.6 = (f32[6,64,128]{2,1,0:T(8,128)S(1)}, f32[6,64,128]{2,1,0:T(8,128)S(1)}, u32[]{:S(2)}, u32[]{:S(2)}) collective-permute-start(f32[6,64,128]{2,1,0:T(8,128)S(1)} %get-tuple-element.37.own), channel_id=1, source_target_pairs={{0,32},{32,0},{64,96},{96,64},{128,160},{160,128},{192,224},{224,1... | collective-permute-start | bytes 589832 | tf_op jit(solution)/shard_map/ppermute | solution.py:649
  43.6 3.3 %collective-permute-done.7.odd_in = f32[6,64,128]{2,1,0:T(8,128)S(1)} collective-permute-done((f32[6,64,128]{2,1,0:T(8,128)S(1)}, f32[6,64,128]{2,1,0:T(8,128)S(1)}, u32[]{:S(2)}, u32[]{:S(2)}) %collective-permute-start.7) | collective-permute-done | bytes 196640 | tf_op jit(solution)/shard_map/ppermute | solution.py:649
  46.9 0.0 collective-permute-done.6.even_in
  46.9 0.2 collective-permute-start.8
  47.2 2.1 %collective-permute-start.9 = (f32[64,256]{1,0:T(8,128)S(1)}, f32[64,256]{1,0:T(8,128)S(1)}, u32[]{:S(2)}, u32[]{:S(2)}) collective-permute-start(f32[64,256]{1,0:T(8,128)S(1)} %get-tuple-element.39), channel_id=1, source_target_pairs={{2,4},{4,2},{6,8},{8,6},{10,12},{12,10},{14,16},{16,14},{18,20},{2... | collective-permute-start | bytes 196616 | tf_op jit(solution)/shard_map/ppermute | solution.py:649
  49.3 0.0 copy-done.1
  49.3 1.4 %inner_synthesis.1.partial = f32[1536,256]{1,0:T(8,128)} custom-call(f32[6,64,128]{2,1,0:T(8,128)S(1)} %get-tuple-element.37.own, f32[6,64,128]{2,1,0:T(8,128)S(1)} %collective-permute-done.6.even_in, f32[6,64,128]{2,1,0:T(8,128)S(1)} %collective-permute-done.7.odd_in, f32[1536,256]{1,0:T(8,128)S(1)} %copy-done.1, bf16[1536,128]{1,0:T(8,128)(2,1)S(1)} %copy-done.3), custom_call_target="tpu_custom_call" | custom-call | flops 1500000000 | bytes 2500000 | tf_op jit(solution)/shard_map/inner_synthesis/pallas_call | solution.py:607
  50.7 0.8 %collective-permute-done.8.near_even = f32[64,256]{1,0:T(8,128)S(1)} collective-permute-done((f32[64,256]{1,0:T(8,128)S(1)}, f32[64,256]{1,0:T(8,128)S(1)}, u32[]{:S(2)}, u32[]{:S(2)}) %collective-permute-start.8) | collective-permute-done | bytes 65568 | tf_op jit(solution)/shard_map/ppermute | solution.py:649
  51.5 4.0 %collective-permute-done.9.near_odd = f32[64,256]{1,0:T(8,128)S(1)} collective-permute-done((f32[64,256]{1,0:T(8,128)S(1)}, f32[64,256]{1,0:T(8,128)S(1)}, u32[]{:S(2)}, u32[]{:S(2)}) %collective-permute-start.9) | collective-permute-done | bytes 65568 | tf_op jit(solution)/shard_map/ppermute | solution.py:649
  55.5 2.1 %outer_synthesis.1 = f32[1536,256]{1,0:T(8,128)} custom-call(f32[6,64,128]{2,1,0:T(8,128)S(1)} %get-tuple-element.37.own, f32[6,64,128]{2,1,0:T(8,128)S(1)} %collective-permute-done.6.even_in, f32[6,64,128]{2,1,0:T(8,128)S(1)} %collective-permute-done.7.odd_in, f32[64,256]{1,0:T(8,128)S(1)} %collective-permute-done.8.near_even, ...), custom_call_target="tpu_custom_call", output_to_operand_aliasing={{}: (7, {})} | custom-call | tf_op jit(solution)/shard_map/outer_synthesis/pallas_call | solution.py:624
  (9 shorter events, 0.0 us)
Async XLA Ops:
  0.6 25.6 %copy-start.2 = (bf16[4608,128]{1,0:T(8,128)(2,1)S(1)}, bf16[4608,128]{1,0:T(8,128)(2,1)}, u32[]{:S(2)}) copy-start(bf16[4608,128]{1,0:T(8,128)(2,1)} %constant.7.clone.wide) | copy-start | bytes 3538948
  0.6 25.6 %copy-start = (s32[1536,256]{1,0:T(8,128)S(1)}, s32[1536,256]{1,0:T(8,128)}, u32[]{:S(2)}) copy-start(s32[1536,256]{1,0:T(8,128)} %target.1) | copy-start | bytes 4718596
  6.1 13.0 %collective-permute-start = (f32[64,256]{1,0:T(8,128)}, f32[64,256]{1,0:T(8,128)S(1)}, u32[]{:S(2)}, u32[]{:S(2)}) collective-permute-start(f32[64,256]{1,0:T(8,128)} %get-tuple-element.26), channel_id=1, source_target_pairs={{0,2},{2,0},{4,6},{6,4},{8,10},{10,8},{12,14},{14,12},{16,18},{18,... | collective-permute-start | bytes 196616 | tf_op jit(solution)/shard_map/ppermute | solution.py:649
  7.7 11.4 %collective-permute-start.1 = (f32[64,256]{1,0:T(8,128)}, f32[64,256]{1,0:T(8,128)S(1)}, u32[]{:S(2)}, u32[]{:S(2)}) collective-permute-start(f32[64,256]{1,0:T(8,128)} %get-tuple-element.27), channel_id=1, source_target_pairs={{2,4},{4,2},{6,8},{8,6},{10,12},{12,10},{14,16},{16,14},{18,20},{2... | collective-permute-start | bytes 196616 | tf_op jit(solution)/shard_map/ppermute | solution.py:649
  11.2 10.5 %collective-permute-start.4 = (f32[3,64,128]{2,1,0:T(8,128)}, f32[3,64,128]{2,1,0:T(8,128)S(1)}, u32[]{:S(2)}, u32[]{:S(2)}) collective-permute-start(f32[3,64,128]{2,1,0:T(8,128)} %get-tuple-element.34), channel_id=1, source_target_pairs={{0,25},{1,24},{2,27},{3,26},{4,29},{5,28},{6,31},{7,30},{8,17},{9,... | collective-permute-start | bytes 294920 | tf_op jit(solution)/shard_map/ppermute | solution.py:657
  18.0 1.0 %copy-start.4 = (f32[6,64,256]{2,1,0:T(8,128)S(1)}, f32[6,64,256]{2,1,0:T(8,128)}, u32[]{:S(2)}) copy-start(f32[6,64,256]{2,1,0:T(8,128)} %get-tuple-element.22.total) | copy-start | bytes 1179652
  19.2 5.0 %collective-permute-start.2 = (f32[6,64,128]{2,1,0:T(8,128)S(1)}, f32[6,64,128]{2,1,0:T(8,128)S(1)}, u32[]{:S(2)}, u32[]{:S(2)}) collective-permute-start(f32[6,64,128]{2,1,0:T(8,128)S(1)} %get-tuple-element.29), channel_id=1, source_target_pairs={{0,32},{32,0},{64,96},{96,64},{128,160},{160,128},{192,224},{224,1... | collective-permute-start | bytes 589832 | tf_op jit(solution)/shard_map/ppermute | solution.py:649
  19.3 7.0 %collective-permute-start.3 = (f32[6,64,128]{2,1,0:T(8,128)S(1)}, f32[6,64,128]{2,1,0:T(8,128)S(1)}, u32[]{:S(2)}, u32[]{:S(2)}) collective-permute-start(f32[6,64,128]{2,1,0:T(8,128)S(1)} %get-tuple-element.30), channel_id=1, source_target_pairs={{32,64},{64,32},{96,128},{128,96},{160,192},{192,160},{33,65},{65,... | collective-permute-start | bytes 589832 | tf_op jit(solution)/shard_map/ppermute | solution.py:649
  21.7 2.3 %collective-permute-start.5 = (f32[3,64,128]{2,1,0:T(8,128)S(1)}, f32[3,64,128]{2,1,0:T(8,128)S(1)}, u32[]{:S(2)}, u32[]{:S(2)}) collective-permute-start(f32[3,64,128]{2,1,0:T(8,128)S(1)} %collective-permute-done.4.mine), channel_id=1, source_target_pairs={{0,32},{32,0},{64,96},{96,64},{128,160},{160,128},{192,224},{224,1... | collective-permute-start | bytes 294920 | tf_op jit(solution)/shard_map/ppermute | solution.py:649
  23.0 0.9 %copy-start.5 = (f32[6,64,128]{2,1,0:T(8,128)S(1)}, f32[6,64,128]{2,1,0:T(8,128)}, u32[]{:S(2)}) copy-start(f32[6,64,128]{2,1,0:T(8,128)} %get-tuple-element.31.own) | copy-start | bytes 589828
  26.3 23.0 %copy-start.1 = (f32[1536,256]{1,0:T(8,128)S(1)}, f32[1536,256]{1,0:T(8,128)}, u32[]{:S(2)}) copy-start(f32[1536,256]{1,0:T(8,128)} %get-tuple-element.40.slope) | copy-start | bytes 4718596
  26.3 23.0 %copy-start.3 = (bf16[1536,128]{1,0:T(8,128)(2,1)S(1)}, bf16[1536,128]{1,0:T(8,128)(2,1)}, u32[]{:S(2)}) copy-start(bf16[1536,128]{1,0:T(8,128)(2,1)} %constant.8.clone.tables) | copy-start | bytes 1179652
  39.9 7.0 %collective-permute-start.7 = (f32[6,64,128]{2,1,0:T(8,128)S(1)}, f32[6,64,128]{2,1,0:T(8,128)S(1)}, u32[]{:S(2)}, u32[]{:S(2)}) collective-permute-start(f32[6,64,128]{2,1,0:T(8,128)S(1)} %get-tuple-element.37.own), channel_id=1, source_target_pairs={{32,64},{64,32},{96,128},{128,96},{160,192},{192,160},{33,65},{65,... | collective-permute-start | bytes 589832 | tf_op jit(solution)/shard_map/ppermute | solution.py:649
  42.4 4.5 %collective-permute-start.6 = (f32[6,64,128]{2,1,0:T(8,128)S(1)}, f32[6,64,128]{2,1,0:T(8,128)S(1)}, u32[]{:S(2)}, u32[]{:S(2)}) collective-permute-start(f32[6,64,128]{2,1,0:T(8,128)S(1)} %get-tuple-element.37.own), channel_id=1, source_target_pairs={{0,32},{32,0},{64,96},{96,64},{128,160},{160,128},{192,224},{224,1... | collective-permute-start | bytes 589832 | tf_op jit(solution)/shard_map/ppermute | solution.py:649
  46.9 4.6 %collective-permute-start.8 = (f32[64,256]{1,0:T(8,128)S(1)}, f32[64,256]{1,0:T(8,128)S(1)}, u32[]{:S(2)}, u32[]{:S(2)}) collective-permute-start(f32[64,256]{1,0:T(8,128)S(1)} %get-tuple-element.38), channel_id=1, source_target_pairs={{0,2},{2,0},{4,6},{6,4},{8,10},{10,8},{12,14},{14,12},{16,18},{18,... | collective-permute-start | bytes 196616 | tf_op jit(solution)/shard_map/ppermute | solution.py:649
  47.2 8.3 %collective-permute-start.9 = (f32[64,256]{1,0:T(8,128)S(1)}, f32[64,256]{1,0:T(8,128)S(1)}, u32[]{:S(2)}, u32[]{:S(2)}) collective-permute-start(f32[64,256]{1,0:T(8,128)S(1)} %get-tuple-element.39), channel_id=1, source_target_pairs={{2,4},{4,2},{6,8},{8,6},{10,12},{12,10},{14,16},{16,14},{18,20},{2... | collective-permute-start | bytes 196616 | tf_op jit(solution)/shard_map/ppermute | solution.py:649

commit v5 on v4

--- a/solution.py
+++ b/solution.py
@@ -15,9 +15,9 @@
 TILE = 256
 COARSE = 128
 HALF = COARSE // 2
-VMEM_LIMIT = 32 * 1024 * 1024
+VMEM_LIMIT = 40 * 1024 * 1024
 PAIR = 2
-TILES_AT_ONCE = 3
+TILES_AT_ONCE = 6
 FIRST_LIMIT = 60 * 1024 * 1024
 
 bf16 = ml_dtypes.bfloat16
@@ -58,11 +58,11 @@
     columns, rows, outs, pixs = [], [], [], []
     for points in (pixels + 3 * HALO, pixels):
         cos, sin = np.cos(angles(points)), np.sin(angles(points))
-        columns.append(as_right(np.concatenate([cos.T, -sin.T], axis=1)))
-        pixs.append(as_right(np.concatenate([cos, -sin], axis=0)))
+        columns += halves(np.concatenate([cos.T, -sin.T], axis=1))
+        pixs += halves(np.concatenate([cos, -sin], axis=0))
         cos, sin = cos[ORDER], sin[ORDER]
-        rows += blocks(as_left(factor * np.concatenate([cos, sin], axis=0)))
-        outs += blocks(as_left(factor * np.concatenate([cos.T, sin.T], axis=1)))
+        rows += halves(factor * np.concatenate([cos, sin], axis=0))
+        outs += halves(factor * np.concatenate([cos.T, sin.T], axis=1))
     plus = 4 * np.arange(HALF) + 2
     samples = np.concatenate([plus, -plus])
     cos, sin = np.cos(angles(samples)), np.sin(angles(samples))
@@ -155,14 +155,37 @@
     return first[:, :width] + (first[:, width:] + dot(low, table[:, :width]))
 
 
-def col_table(packed, index):
-    return packed[index * 384 : (index + 1) * 384, :]
-
-
-def row_table(packed, index):
-    start = 768 + index * 384
+def square(packed, index):
+    return packed[index * 128 : (index + 1) * 128, :]
+
+
+def times_diagonal(value, packed):
+    zeros = jnp.zeros((128, 128), jnp.bfloat16)
+    high_table, low_table = (
+        jnp.concatenate(
+            [
+                jnp.concatenate([square(packed, i), zeros], axis=1),
+                jnp.concatenate([zeros, square(packed, i + 2)], axis=1),
+            ],
+            axis=0,
+        )
+        for i in (0, 1)
+    )
+    high, low = split(value)
+    return dot(
+        jnp.concatenate([high, low, high], axis=1),
+        jnp.concatenate([high_table, high_table, low_table], axis=0),
+    )
+
+
+def stacked_table(packed, part):
+    high, low = square(packed, 4 + 2 * part), square(packed, 5 + 2 * part)
     return jnp.concatenate(
-        [packed[start + i : start + i + 128, :] for i in (0, 128, 256)], axis=1
+        [
+            jnp.concatenate([high, high], axis=1),
+            jnp.concatenate([low, jnp.zeros_like(low)], axis=1),
+        ],
+        axis=0,
     )
 
 
@@ -231,17 +254,11 @@
 
 def block_spectra(transmit, tables):
     sign = jnp.where(low_lanes((FB, 2 * FB)), 1.0, -1.0)
-    high, low = split(transmit)
-    rows = []
-    for side in (0, 1):
-        lanes = slice(side * HALO, (side + 1) * HALO)
-        three = jnp.concatenate([high[:, lanes], low[:, lanes], high[:, lanes]], axis=1)
-        rows.append(dot(three, col_table(tables, side)))
-    rows = jnp.concatenate(rows, axis=1)
+    rows = times_diagonal(transmit, tables)
     found = []
     for block in range(transmit.shape[0] // HALO):
-        both = table_times(
-            row_table(tables, block % 2), rows[block * HALO : (block + 1) * HALO]
+        both = stacked_times(
+            stacked_table(tables, block % 2), rows[block * HALO : (block + 1) * HALO]
         )
         sine = both[FB:]
         turned = [sign * swapped(sine[:, : 2 * FB]), sign * swapped(sine[:, 2 * FB :])]
@@ -441,14 +458,8 @@
             block = base + near
             turned = [sign * swapped(block[:, : 2 * FB]), sign * swapped(block[:, 2 * FB :])]
             stacked = jnp.concatenate([block, jnp.concatenate(turned, axis=1)], axis=0)
-            outer.append(table_times(row_table(tables, part), stacked))
-    high, low = split(jnp.concatenate(outer, axis=0))
-    sides = []
-    for side in (0, 1):
-        lanes = slice(side * 2 * FB, (side + 1) * 2 * FB)
-        three = jnp.concatenate([high[:, lanes], low[:, lanes], high[:, lanes]], axis=1)
-        sides.append(dot(three, col_table(tables, side)))
-    return jnp.concatenate(sides, axis=1) * slope
+            outer.append(stacked_times(stacked_table(tables, part), stacked))
+    return times_diagonal(jnp.concatenate(outer, axis=0), tables) * slope
 
 
 def mixed_row(own, even_in, odd_in, index):
@@ -465,27 +476,41 @@
     side_odd[...] = jnp.where(odd_row, last, first)
 
 
-def inner_kernel(own, even_in, odd_in, slope, tables, result):
-    rows = [mixed_row(own, even_in, odd_in, i) for i in range(PAIR - 1, 2 * PAIR + 1)]
-    result[...] = synthesis_rows(rows, slope[...], tables)
-
-
-def outer_kernel(own, even_in, odd_in, near_even, near_odd, slope, tables, partial, result):
+def write_rows(values, result, first, buffer, semaphore):
+    buffer[...] = values
+    copy = pltpu.make_async_copy(
+        buffer, result.at[pl.ds(first, values.shape[0]), :], semaphore
+    )
+    copy.start()
+    return copy
+
+
+def inner_kernel(own, even_in, odd_in, slope, tables, result, buffer, semaphore):
+    count = own.shape[0]
+    rows = [mixed_row(own, even_in, odd_in, i) for i in range(count)]
+    values = synthesis_rows(rows, slope[TILE : (count - 1) * TILE, :], tables)
+    write_rows(values, result, TILE, buffer, semaphore).wait()
+
+
+def outer_kernel(
+    own, even_in, odd_in, near_even, near_odd, slope, tables, partial, result, buffers,
+    semaphores,
+):
     del partial
     count = own.shape[0]
     odd_row = is_odd("gy")
-
-    @pl.when(pl.program_id(0) == 0)
-    def _():
-        rows = [jnp.where(odd_row, near_even[...], near_odd[...])]
-        rows += [mixed_row(own, even_in, odd_in, i) for i in range(PAIR + 1)]
-        result[...] = synthesis_rows(rows, slope[...], tables)
-
-    @pl.when(pl.program_id(0) == 1)
-    def _():
-        rows = [mixed_row(own, even_in, odd_in, i) for i in range(count - PAIR - 1, count)]
-        rows += [jnp.where(odd_row, near_odd[...], near_even[...])]
-        result[...] = synthesis_rows(rows, slope[...], tables)
+    above = jnp.where(odd_row, near_even[...], near_odd[...])
+    below = jnp.where(odd_row, near_odd[...], near_even[...])
+    rows = [mixed_row(own, even_in, odd_in, i) for i in (0, 1, count - 2, count - 1)]
+    last = (count - 1) * TILE
+    copies = []
+    for index, first, near in ((0, 0, [above] + rows[:2]), (1, last, rows[2:] + [below])):
+        values = synthesis_rows(near, slope[first : first + TILE, :], tables)
+        copies.append(
+            write_rows(values, result, first, buffers.at[index], semaphores.at[index])
+        )
+    for copy in copies:
+        copy.wait()
 
 
 def whole(array):
@@ -603,14 +628,17 @@
 
 def inner_synthesis(own, even_in, odd_in, slope):
     tables = jnp.asarray(TABLES["synthesis"])
-    place = pl.BlockSpec((PAIR * TILE, TILE), lambda step: (1, 0))
+    vmem = pl.BlockSpec(memory_space=pltpu.VMEM)
     return pl.pallas_call(
         inner_kernel,
-        grid=(1,),
         out_shape=jax.ShapeDtypeStruct(slope.shape, jnp.float32),
-        in_specs=[whole(own)] * 3 + [place, whole(tables)],
-        out_specs=place,
-        compiler_params=params(),
+        in_specs=[vmem] * 5,
+        out_specs=pl.BlockSpec(memory_space=pl.ANY),
+        scratch_shapes=[
+            pltpu.VMEM((slope.shape[0] - 2 * TILE, TILE), jnp.float32),
+            pltpu.SemaphoreType.DMA,
+        ],
+        compiler_params=pltpu.CompilerParams(vmem_limit_bytes=VMEM_LIMIT),
         cost_estimate=pl.CostEstimate(
             flops=1500000000, bytes_accessed=2500000, transcendentals=0
         ),
@@ -620,17 +648,18 @@
 
 def outer_synthesis(own, even_in, odd_in, near_even, near_odd, slope, partial):
     tables = jnp.asarray(TABLES["synthesis"])
-    place = pl.BlockSpec((PAIR * TILE, TILE), lambda step: (2 * step, 0))
+    vmem = pl.BlockSpec(memory_space=pltpu.VMEM)
     return pl.pallas_call(
         outer_kernel,
-        grid=(2,),
         out_shape=jax.ShapeDtypeStruct(slope.shape, jnp.float32),
-        in_specs=[whole(own)] * 3
-        + [whole(near_even), whole(near_odd), place, whole(tables)]
-        + [pl.BlockSpec(memory_space=pl.ANY)],
-        out_specs=place,
+        in_specs=[vmem] * 7 + [pl.BlockSpec(memory_space=pl.ANY)],
+        out_specs=pl.BlockSpec(memory_space=pl.ANY),
         input_output_aliases={7: 0},
-        compiler_params=params(),
+        scratch_shapes=[
+            pltpu.VMEM((2, TILE, TILE), jnp.float32),
+            pltpu.SemaphoreType.DMA((2,)),
+        ],
+        compiler_params=pltpu.CompilerParams(vmem_limit_bytes=VMEM_LIMIT),
         name="outer_synthesis",
     )(own, even_in, odd_in, near_even, near_odd, slope, tables, partial)
 

time: 57.9 us -> 58 us (level)
  waiting for transfers between devices: 10.2 us -> 9.5 us
    ppermute x9, waiting for transfers between devices: 10.2 us -> 9.5 us  [swap(): return lax.ppermute(value, axis, swap_pairs(lax.axis_size(axis), first))]
  transfers between devices with their start and end apart: 10 -> 10, of which waited for: 4 -> 4; matrix products, arithmetic and copies ran while one was open for 0% -> 0% of each run, Pallas kernels for 3% -> 4%
where the time goes in v5:
time: 58 us; the launch traced here: 57.7 us
  Pallas kernels  23.4 us (40%)
  starting transfers between devices  21.9 us (38%)
  waiting for transfers between devices  9.5 us (16%)
  local copies, waits for them, and re-layouts  1.94 us (3%)
  between operations  0.98 us (2%)
    ppermute x9, starting transfers between devices, swap(): return lax.ppermute(value, axis, swap_pairs(lax.axis_size(axis), first))  15.1 us
    pallas_call x1, Pallas kernels, imaging(): pl.pallas_call(imaging_kernel, grid=(tiles // TILES_AT_ONCE,), out_shape=...  13.7 us
    ppermute x9, waiting for transfers between devices, swap(): return lax.ppermute(value, axis, swap_pairs(lax.axis_size(axis), first))  9.5 us
    ppermute x1, starting transfers between devices, local(): mine = lax.ppermute(half, ('gy', 'ka'), pairs)  6.83 us
    pallas_call x1, Pallas kernels, analysis(): pl.pallas_call(analysis_kernel, grid=(tiles // PAIR,), out_shape=(total,...  5.88 us
    pallas_call x1, Pallas kernels, inner_synthesis(): pl.pallas_call(inner_kernel, out_shape=jax.ShapeDtypeStruct(slope.shape,...  1.95 us
    unnamed x12, local copies, waits for them, and re-layouts  1.94 us
    pallas_call x1, Pallas kernels, outer_synthesis(): pl.pallas_call(outer_kernel, out_shape=jax.ShapeDtypeStruct(slope.shape,...  1.5 us
  transfers between devices with their start and end apart: 10, of which 4 were waited for; matrix products, arithmetic and copies ran while one was open for 0% of the time, Pallas kernels for 4%

profile of v5, /device:TPU:40, one launch (start us, length us, event | category | flops | bytes accessed | tf_op | source)
XLA Modules:
  0.0 57.7 jit_solution(18129599041506336799)
XLA Ops:
  0.6 0.0 copy-start.2
  0.7 5.9 %analysis.1 = (f32[6,64,256]{2,1,0:T(8,128)}, f32[6,64,128]{2,1,0:T(8,128)}, f32[3,64,128]{2,1,0:T(8,128)}, f32[64,256]{1,0:T(8,128)}, f32[64,256]{1,0:T(8,128)}, /*index=5*/f32[1536,256]{1,0:T(8,128)}) custom-call(f32[1536,256]{1,0:T(8,128)} %mask_in.1, f32[6,2,4096]{2,1,0:T(2,128)} %kernels_in.1, f32[6]{0:T(128)} %weights.1, ...), custom_call_target="tpu_custom_call" | custom-call | tf_op jit(solution)/shard_map/analysis/pallas_call | solution.py:537
  6.5 1.6 %collective-permute-start = (f32[64,256]{1,0:T(8,128)}, f32[64,256]{1,0:T(8,128)S(1)}, u32[]{:S(2)}, u32[]{:S(2)}) collective-permute-start(f32[64,256]{1,0:T(8,128)} %get-tuple-element.26), channel_id=1, source_target_pairs={{0,2},{2,0},{4,6},{6,4},{8,10},{10,8},{12,14},{14,12},{16,18},{18,... | collective-permute-start | bytes 196616 | tf_op jit(solution)/shard_map/ppermute | solution.py:678
  8.1 3.5 %collective-permute-start.1 = (f32[64,256]{1,0:T(8,128)}, f32[64,256]{1,0:T(8,128)S(1)}, u32[]{:S(2)}, u32[]{:S(2)}) collective-permute-start(f32[64,256]{1,0:T(8,128)} %get-tuple-element.27), channel_id=1, source_target_pairs={{2,4},{4,2},{6,8},{8,6},{10,12},{12,10},{14,16},{16,14},{18,20},{2... | collective-permute-start | bytes 196616 | tf_op jit(solution)/shard_map/ppermute | solution.py:678
  11.7 6.8 %collective-permute-start.4 = (f32[3,64,128]{2,1,0:T(8,128)}, f32[3,64,128]{2,1,0:T(8,128)S(1)}, u32[]{:S(2)}, u32[]{:S(2)}) collective-permute-start(f32[3,64,128]{2,1,0:T(8,128)} %get-tuple-element.34), channel_id=1, source_target_pairs={{0,25},{1,24},{2,27},{3,26},{4,29},{5,28},{6,31},{7,30},{8,17},{9,... | collective-permute-start | bytes 294920 | tf_op jit(solution)/shard_map/ppermute | solution.py:686
  18.5 1.0 %copy-done.3 = f32[6,64,256]{2,1,0:T(8,128)S(1)} copy-done((f32[6,64,256]{2,1,0:T(8,128)S(1)}, f32[6,64,256]{2,1,0:T(8,128)}, u32[]{:S(2)}) %copy-start.3) | copy-done | bytes 393240
  19.5 0.1 shares.1
  19.6 0.0 collective-permute-done.near_even
  19.6 0.0 collective-permute-done.1.near_odd
  19.6 0.1 merge.1
  19.6 0.1 collective-permute-start.2
  19.7 2.4 %collective-permute-start.3 = (f32[6,64,128]{2,1,0:T(8,128)S(1)}, f32[6,64,128]{2,1,0:T(8,128)S(1)}, u32[]{:S(2)}, u32[]{:S(2)}) collective-permute-start(f32[6,64,128]{2,1,0:T(8,128)S(1)} %get-tuple-element.30), channel_id=1, source_target_pairs={{32,64},{64,32},{96,128},{128,96},{160,192},{192,160},{33,65},{65,... | collective-permute-start | bytes 589832 | tf_op jit(solution)/shard_map/ppermute | solution.py:678
  22.2 0.0 collective-permute-done.4.mine
  22.2 1.4 %collective-permute-start.5 = (f32[3,64,128]{2,1,0:T(8,128)S(1)}, f32[3,64,128]{2,1,0:T(8,128)S(1)}, u32[]{:S(2)}, u32[]{:S(2)}) collective-permute-start(f32[3,64,128]{2,1,0:T(8,128)S(1)} %collective-permute-done.4.mine), channel_id=1, source_target_pairs={{0,32},{32,0},{64,96},{96,64},{128,160},{160,128},{192,224},{224,1... | collective-permute-start | bytes 294920 | tf_op jit(solution)/shard_map/ppermute | solution.py:678
  23.6 0.9 %copy-done.5 = f32[6,64,128]{2,1,0:T(8,128)S(1)} copy-done((f32[6,64,128]{2,1,0:T(8,128)S(1)}, f32[6,64,128]{2,1,0:T(8,128)}, u32[]{:S(2)}) %copy-start.5) | copy-done | bytes 196632
  24.6 0.1 prepare_own.1
  24.7 0.0 collective-permute-done.5.partners
  24.7 0.1 prepare_other.1
  24.8 0.0 collective-permute-done.2.from_even
  24.8 1.9 %collective-permute-done.3.from_odd = f32[6,64,128]{2,1,0:T(8,128)S(1)} collective-permute-done((f32[6,64,128]{2,1,0:T(8,128)S(1)}, f32[6,64,128]{2,1,0:T(8,128)S(1)}, u32[]{:S(2)}, u32[]{:S(2)}) %collective-permute-start.3) | collective-permute-done | bytes 196640 | tf_op jit(solution)/shard_map/ppermute | solution.py:678
  26.7 0.0 copy-done.2
  26.7 13.7 %imaging.1 = (f32[1536,256]{1,0:T(8,128)}, f32[6,64,128]{2,1,0:T(8,128)S(1)}) custom-call(f32[6,64,128]{2,1,0:T(8,128)S(1)} %get-tuple-element.28.share, f32[6,64,128]{2,1,0:T(8,128)S(1)} %collective-permute-done.2.from_even, f32[6,64,128]{2,1,0:T(8,128)S(1)} %collective-permute-done.3.from_odd, f32[6,64,128]{2,1,0:T(8,128)S(1)} %get-tuple-element.32.straight_own, ...), custom_call_target="tpu_custom_call" | custom-call | tf_op jit(solution)/shard_map/imaging/pallas_call | solution.py:609
  40.4 2.4 %collective-permute-start.7 = (f32[6,64,128]{2,1,0:T(8,128)S(1)}, f32[6,64,128]{2,1,0:T(8,128)S(1)}, u32[]{:S(2)}, u32[]{:S(2)}) collective-permute-start(f32[6,64,128]{2,1,0:T(8,128)S(1)} %get-tuple-element.37.own), channel_id=1, source_target_pairs={{32,64},{64,32},{96,128},{128,96},{160,192},{192,160},{33,65},{65,... | collective-permute-start | bytes 589832 | tf_op jit(solution)/shard_map/ppermute | solution.py:678
  42.9 1.2 %collective-permute-start.6 = (f32[6,64,128]{2,1,0:T(8,128)S(1)}, f32[6,64,128]{2,1,0:T(8,128)S(1)}, u32[]{:S(2)}, u32[]{:S(2)}) collective-permute-start(f32[6,64,128]{2,1,0:T(8,128)S(1)} %get-tuple-element.37.own), channel_id=1, source_target_pairs={{0,32},{32,0},{64,96},{96,64},{128,160},{160,128},{192,224},{224,1... | collective-permute-start | bytes 589832 | tf_op jit(solution)/shard_map/ppermute | solution.py:678
  44.1 3.3 %collective-permute-done.7.odd_in = f32[6,64,128]{2,1,0:T(8,128)S(1)} collective-permute-done((f32[6,64,128]{2,1,0:T(8,128)S(1)}, f32[6,64,128]{2,1,0:T(8,128)S(1)}, u32[]{:S(2)}, u32[]{:S(2)}) %collective-permute-start.7) | collective-permute-done | bytes 196640 | tf_op jit(solution)/shard_map/ppermute | solution.py:678
  47.4 0.0 collective-permute-done.6.even_in
  47.4 0.2 collective-permute-start.8
  47.7 2.1 %collective-permute-start.9 = (f32[64,256]{1,0:T(8,128)S(1)}, f32[64,256]{1,0:T(8,128)S(1)}, u32[]{:S(2)}, u32[]{:S(2)}) collective-permute-start(f32[64,256]{1,0:T(8,128)S(1)} %get-tuple-element.39), channel_id=1, source_target_pairs={{2,4},{4,2},{6,8},{8,6},{10,12},{12,10},{14,16},{16,14},{18,20},{2... | collective-permute-start | bytes 196616 | tf_op jit(solution)/shard_map/ppermute | solution.py:678
  49.8 1.9 %inner_synthesis.1.partial = f32[1536,256]{1,0:T(8,128)} custom-call(f32[6,64,128]{2,1,0:T(8,128)S(1)} %get-tuple-element.37.own, f32[6,64,128]{2,1,0:T(8,128)S(1)} %collective-permute-done.6.even_in, f32[6,64,128]{2,1,0:T(8,128)S(1)} %collective-permute-done.7.odd_in, f32[1536,256]{1,0:T(8,128)S(1)} %copy-done.1, bf16[1024,128]{1,0:T(8,128)(2,1)S(1)} %copy-done.4), custom_call_target="tpu_custom_call" | custom-call | flops 1500000000 | bytes 2500000 | tf_op jit(solution)/shard_map/inner_synthesis/pallas_call | solution.py:632
  51.7 0.3 collective-permute-done.8.near_even
  52.0 4.0 %collective-permute-done.9.near_odd = f32[64,256]{1,0:T(8,128)S(1)} collective-permute-done((f32[64,256]{1,0:T(8,128)S(1)}, f32[64,256]{1,0:T(8,128)S(1)}, u32[]{:S(2)}, u32[]{:S(2)}) %collective-permute-start.9) | collective-permute-done | bytes 65568 | tf_op jit(solution)/shard_map/ppermute | solution.py:678
  56.0 1.5 %outer_synthesis.1 = f32[1536,256]{1,0:T(8,128)} custom-call(f32[6,64,128]{2,1,0:T(8,128)S(1)} %get-tuple-element.37.own, f32[6,64,128]{2,1,0:T(8,128)S(1)} %collective-permute-done.6.even_in, f32[6,64,128]{2,1,0:T(8,128)S(1)} %collective-permute-done.7.odd_in, f32[64,256]{1,0:T(8,128)S(1)} %collective-permute-done.8.near_even, ...), custom_call_target="tpu_custom_call", output_to_operand_aliasing={{}: (7, {})} | custom-call | tf_op jit(solution)/shard_map/outer_synthesis/pallas_call | solution.py:652
  (9 shorter events, 0.0 us)
Async XLA Ops:
  0.6 26.1 %copy-start.2 = (bf16[4608,128]{1,0:T(8,128)(2,1)S(1)}, bf16[4608,128]{1,0:T(8,128)(2,1)}, u32[]{:S(2)}) copy-start(bf16[4608,128]{1,0:T(8,128)(2,1)} %constant.7.clone.wide) | copy-start | bytes 3538948
  0.6 26.1 %copy-start = (s32[1536,256]{1,0:T(8,128)S(1)}, s32[1536,256]{1,0:T(8,128)}, u32[]{:S(2)}) copy-start(s32[1536,256]{1,0:T(8,128)} %target.1) | copy-start | bytes 4718596
  6.5 13.0 %collective-permute-start = (f32[64,256]{1,0:T(8,128)}, f32[64,256]{1,0:T(8,128)S(1)}, u32[]{:S(2)}, u32[]{:S(2)}) collective-permute-start(f32[64,256]{1,0:T(8,128)} %get-tuple-element.26), channel_id=1, source_target_pairs={{0,2},{2,0},{4,6},{6,4},{8,10},{10,8},{12,14},{14,12},{16,18},{18,... | collective-permute-start | bytes 196616 | tf_op jit(solution)/shard_map/ppermute | solution.py:678
  8.1 11.4 %collective-permute-start.1 = (f32[64,256]{1,0:T(8,128)}, f32[64,256]{1,0:T(8,128)S(1)}, u32[]{:S(2)}, u32[]{:S(2)}) collective-permute-start(f32[64,256]{1,0:T(8,128)} %get-tuple-element.27), channel_id=1, source_target_pairs={{2,4},{4,2},{6,8},{8,6},{10,12},{12,10},{14,16},{16,14},{18,20},{2... | collective-permute-start | bytes 196616 | tf_op jit(solution)/shard_map/ppermute | solution.py:678
  11.7 10.5 %collective-permute-start.4 = (f32[3,64,128]{2,1,0:T(8,128)}, f32[3,64,128]{2,1,0:T(8,128)S(1)}, u32[]{:S(2)}, u32[]{:S(2)}) collective-permute-start(f32[3,64,128]{2,1,0:T(8,128)} %get-tuple-element.34), channel_id=1, source_target_pairs={{0,25},{1,24},{2,27},{3,26},{4,29},{5,28},{6,31},{7,30},{8,17},{9,... | collective-permute-start | bytes 294920 | tf_op jit(solution)/shard_map/ppermute | solution.py:686
  18.5 1.0 %copy-start.3 = (f32[6,64,256]{2,1,0:T(8,128)S(1)}, f32[6,64,256]{2,1,0:T(8,128)}, u32[]{:S(2)}) copy-start(f32[6,64,256]{2,1,0:T(8,128)} %get-tuple-element.22.total) | copy-start | bytes 1179652
  19.6 5.2 %collective-permute-start.2 = (f32[6,64,128]{2,1,0:T(8,128)S(1)}, f32[6,64,128]{2,1,0:T(8,128)S(1)}, u32[]{:S(2)}, u32[]{:S(2)}) collective-permute-start(f32[6,64,128]{2,1,0:T(8,128)S(1)} %get-tuple-element.29), channel_id=1, source_target_pairs={{0,32},{32,0},{64,96},{96,64},{128,160},{160,128},{192,224},{224,1... | collective-permute-start | bytes 589832 | tf_op jit(solution)/shard_map/ppermute | solution.py:678
  19.7 7.0 %collective-permute-start.3 = (f32[6,64,128]{2,1,0:T(8,128)S(1)}, f32[6,64,128]{2,1,0:T(8,128)S(1)}, u32[]{:S(2)}, u32[]{:S(2)}) collective-permute-start(f32[6,64,128]{2,1,0:T(8,128)S(1)} %get-tuple-element.30), channel_id=1, source_target_pairs={{32,64},{64,32},{96,128},{128,96},{160,192},{192,160},{33,65},{65,... | collective-permute-start | bytes 589832 | tf_op jit(solution)/shard_map/ppermute | solution.py:678
  22.2 2.5 %collective-permute-start.5 = (f32[3,64,128]{2,1,0:T(8,128)S(1)}, f32[3,64,128]{2,1,0:T(8,128)S(1)}, u32[]{:S(2)}, u32[]{:S(2)}) collective-permute-start(f32[3,64,128]{2,1,0:T(8,128)S(1)} %collective-permute-done.4.mine), channel_id=1, source_target_pairs={{0,32},{32,0},{64,96},{96,64},{128,160},{160,128},{192,224},{224,1... | collective-permute-start | bytes 294920 | tf_op jit(solution)/shard_map/ppermute | solution.py:678
  23.6 0.9 %copy-start.5 = (f32[6,64,128]{2,1,0:T(8,128)S(1)}, f32[6,64,128]{2,1,0:T(8,128)}, u32[]{:S(2)}) copy-start(f32[6,64,128]{2,1,0:T(8,128)} %get-tuple-element.31.own) | copy-start | bytes 589828
  26.7 23.0 %copy-start.1 = (f32[1536,256]{1,0:T(8,128)S(1)}, f32[1536,256]{1,0:T(8,128)}, u32[]{:S(2)}) copy-start(f32[1536,256]{1,0:T(8,128)} %get-tuple-element.40.slope) | copy-start | bytes 4718596
  26.7 23.0 %copy-start.4 = (bf16[1024,128]{1,0:T(8,128)(2,1)S(1)}, bf16[1024,128]{1,0:T(8,128)(2,1)}, u32[]{:S(2)}) copy-start(bf16[1024,128]{1,0:T(8,128)(2,1)} %constant.8.clone.tables) | copy-start | bytes 786436
  40.4 7.0 %collective-permute-start.7 = (f32[6,64,128]{2,1,0:T(8,128)S(1)}, f32[6,64,128]{2,1,0:T(8,128)S(1)}, u32[]{:S(2)}, u32[]{:S(2)}) collective-permute-start(f32[6,64,128]{2,1,0:T(8,128)S(1)} %get-tuple-element.37.own), channel_id=1, source_target_pairs={{32,64},{64,32},{96,128},{128,96},{160,192},{192,160},{33,65},{65,... | collective-permute-start | bytes 589832 | tf_op jit(solution)/shard_map/ppermute | solution.py:678
  42.9 4.5 %collective-permute-start.6 = (f32[6,64,128]{2,1,0:T(8,128)S(1)}, f32[6,64,128]{2,1,0:T(8,128)S(1)}, u32[]{:S(2)}, u32[]{:S(2)}) collective-permute-start(f32[6,64,128]{2,1,0:T(8,128)S(1)} %get-tuple-element.37.own), channel_id=1, source_target_pairs={{0,32},{32,0},{64,96},{96,64},{128,160},{160,128},{192,224},{224,1... | collective-permute-start | bytes 589832 | tf_op jit(solution)/shard_map/ppermute | solution.py:678
  47.4 4.6 %collective-permute-start.8 = (f32[64,256]{1,0:T(8,128)S(1)}, f32[64,256]{1,0:T(8,128)S(1)}, u32[]{:S(2)}, u32[]{:S(2)}) collective-permute-start(f32[64,256]{1,0:T(8,128)S(1)} %get-tuple-element.38), channel_id=1, source_target_pairs={{0,2},{2,0},{4,6},{6,4},{8,10},{10,8},{12,14},{14,12},{16,18},{18,... | collective-permute-start | bytes 196616 | tf_op jit(solution)/shard_map/ppermute | solution.py:678
  47.7 8.3 %collective-permute-start.9 = (f32[64,256]{1,0:T(8,128)S(1)}, f32[64,256]{1,0:T(8,128)S(1)}, u32[]{:S(2)}, u32[]{:S(2)}) collective-permute-start(f32[64,256]{1,0:T(8,128)S(1)} %get-tuple-element.39), channel_id=1, source_target_pairs={{2,4},{4,2},{6,8},{8,6},{10,12},{12,10},{14,16},{16,14},{18,20},{2... | collective-permute-start | bytes 196616 | tf_op jit(solution)/shard_map/ppermute | solution.py:678

commit v6 on v5

--- a/solution.py
+++ b/solution.py
@@ -16,8 +16,8 @@
 COARSE = 128
 HALF = COARSE // 2
 VMEM_LIMIT = 40 * 1024 * 1024
-PAIR = 2
-TILES_AT_ONCE = 6
+PAIR = 3
+TILES_AT_ONCE = 3
 FIRST_LIMIT = 60 * 1024 * 1024
 
 bf16 = ml_dtypes.bfloat16
@@ -159,6 +159,21 @@
     return packed[index * 128 : (index + 1) * 128, :]
 
 
+def times_sides(value, packed):
+    high, low = split(value)
+    found = []
+    for side in (0, 1):
+        lanes = slice(side * 128, (side + 1) * 128)
+        first, second = square(packed, 2 * side), square(packed, 2 * side + 1)
+        found.append(
+            dot(
+                jnp.concatenate([high[:, lanes], low[:, lanes], high[:, lanes]], axis=1),
+                jnp.concatenate([first, first, second], axis=0),
+            )
+        )
+    return jnp.concatenate(found, axis=1)
+
+
 def times_diagonal(value, packed):
     zeros = jnp.zeros((128, 128), jnp.bfloat16)
     high_table, low_table = (
@@ -254,11 +269,14 @@
 
 def block_spectra(transmit, tables):
     sign = jnp.where(low_lanes((FB, 2 * FB)), 1.0, -1.0)
-    rows = times_diagonal(transmit, tables)
+    rows = times_sides(transmit, tables)
     found = []
     for block in range(transmit.shape[0] // HALO):
-        both = stacked_times(
-            stacked_table(tables, block % 2), rows[block * HALO : (block + 1) * HALO]
+        first = square(tables, 4 + 2 * (block % 2))
+        second = square(tables, 5 + 2 * (block % 2))
+        both = table_times(
+            jnp.concatenate([first, second, first], axis=1),
+            rows[block * HALO : (block + 1) * HALO],
         )
         sine = both[FB:]
         turned = [sign * swapped(sine[:, : 2 * FB]), sign * swapped(sine[:, 2 * FB :])]
@@ -355,38 +373,41 @@
     copies = []
     sign = jnp.where(low_lanes((HALF, 2 * FB)), 1.0, -1.0)
     tiles = range(share.shape[0])
-    weights = []
     intensities = [[] for tile in tiles]
 
-    for tile in tiles:
-        spectrum = share[tile] + from_even[tile] + from_odd[tile]
-        turned = swapped(spectrum)
-        for group in range(2):
-            first = group * count
-            products = [
-                straights[group][i] * spectrum + crosseds[group][i] * turned
-                for i in range(count)
-            ]
-            rows = times_table(jnp.concatenate(products, axis=0), wide_table(wide, SPREAD))
+    spectra = [share[tile] + from_even[tile] + from_odd[tile] for tile in tiles]
+    turned = [swapped(spectrum) for spectrum in spectra]
+    for group in range(2):
+        products = [
+            straights[group][i] * spectra[tile] + crosseds[group][i] * turned[tile]
+            for tile in tiles
+            for i in range(count)
+        ]
+        rows = times_table(jnp.concatenate(products, axis=0), wide_table(wide, SPREAD))
+        for tile in tiles:
             total = jnp.zeros((COARSE, COARSE), jnp.float32)
             for i in range(count):
-                both = table_times(
-                    wide_table(wide, LIFT)[:, :192], rows[i * FB : (i + 1) * FB]
-                )
+                place = (tile * count + i) * FB
+                both = table_times(wide_table(wide, LIFT)[:, :192], rows[place : place + FB])
                 cosine, sine = both[:HALF], both[HALF:]
                 sine_re, sine_im = sine[:, :COARSE], sine[:, COARSE:]
                 cosine_re, cosine_im = cosine[:, :COARSE], cosine[:, COARSE:]
                 real = jnp.concatenate([cosine_re - sine_im, cosine_re + sine_im], axis=0)
                 imag = jnp.concatenate([cosine_im + sine_re, cosine_im - sine_re], axis=0)
-                fields[tile, first + i, :, :COARSE] = real
-                fields[tile, first + i, :, COARSE:] = imag
+                fields[tile, group * count + i, :, :COARSE] = real
+                fields[tile, group * count + i, :, COARSE:] = imag
                 total = total + (real * real + imag * imag)
             intensities[tile].append(total)
 
+    half_fine = times_table(
+        jnp.concatenate([first + second for first, second in intensities], axis=0),
+        wide_table(wide, FINE_RIGHT),
+    )
+    half_coarse = []
     for tile in tiles:
-        intensity = intensities[tile][0] + intensities[tile][1]
-        half_fine = times_table(intensity, wide_table(wide, FINE_RIGHT))
-        fine = stacked_times(wide_table(wide, FINE_LEFT), half_fine)
+        fine = stacked_times(
+            wide_table(wide, FINE_LEFT), half_fine[tile * COARSE : (tile + 1) * COARSE]
+        )
         resist = jax.nn.sigmoid(4.0 * (fine - 1.0))
         place = slice(tile * TILE, (tile + 1) * TILE)
         resists[place, :] = resist
@@ -402,26 +423,34 @@
         push = 16.0 * misfit * resist * (1.0 - resist)
         high, low = split(push)
         from_high = dot(wide_table(wide, COARSE_LEFT), high)
-        half_coarse = from_high[:COARSE] + (
-            from_high[COARSE:] + dot(wide_table(wide, COARSE_LEFT)[:COARSE], low)
-        )
-        weights.append(times_paired(half_coarse, wide_table(wide, COARSE_RIGHT)))
-
-    for tile in tiles:
-        scale = jnp.concatenate([weights[tile], weights[tile]], axis=1)
-        adjoint = []
-        for group in range(2):
-            first = group * count
-            scaled = jnp.concatenate(
-                [fields[tile, first + i] * scale for i in range(count)], axis=0
-            )
-            sides[tile, group] = times_paired(scaled, wide_table(wide, GATHER))
+        half_coarse.append(
+            from_high[:COARSE]
+            + (from_high[COARSE:] + dot(wide_table(wide, COARSE_LEFT)[:COARSE], low))
+        )
+    weights = times_paired(jnp.concatenate(half_coarse, axis=0), wide_table(wide, COARSE_RIGHT))
+    scales = [
+        jnp.concatenate([weights[tile * COARSE : (tile + 1) * COARSE]] * 2, axis=1)
+        for tile in tiles
+    ]
+
+    adjoint = [[] for tile in tiles]
+    for group in range(2):
+        scaled = [
+            fields[tile, group * count + i] * scales[tile]
+            for tile in tiles
+            for i in range(count)
+        ]
+        sides[group] = times_paired(
+            jnp.concatenate(scaled, axis=0), wide_table(wide, GATHER)
+        )
+        for tile in tiles:
             total = jnp.zeros((FB, 2 * FB), jnp.float32)
             for i in range(0, count, 2):
                 pair = []
                 for j in (i, i + 1):
-                    plus = sides[tile, group, j * COARSE : j * COARSE + HALF, :]
-                    minus = sides[tile, group, j * COARSE + HALF : (j + 1) * COARSE, :]
+                    place = (tile * count + j) * COARSE
+                    plus = sides[group, place : place + HALF, :]
+                    minus = sides[group, place + HALF : place + COARSE, :]
                     pair.append(
                         jnp.concatenate([plus + minus, sign * swapped(plus - minus)], axis=0)
                     )
@@ -433,8 +462,9 @@
                     total = total + (
                         straights[group][i + j] * part - crosseds[group][i + j] * swapped(part)
                     )
-            adjoint.append(total)
-        grad[tile] = adjoint[0] + adjoint[1]
+            adjoint[tile].append(total)
+    for tile in tiles:
+        grad[tile] = adjoint[tile][0] + adjoint[tile][1]
 
     for copy in copies:
         copy.wait()
@@ -617,7 +647,7 @@
         out_specs=[pl.BlockSpec(memory_space=pl.ANY), spectra],
         scratch_shapes=[
             pltpu.VMEM((TILES_AT_ONCE, kernels, COARSE, 2 * COARSE), jnp.float32),
-            pltpu.VMEM((TILES_AT_ONCE, 2, kernels // 2 * COARSE, 2 * FB), jnp.float32),
+            pltpu.VMEM((2, TILES_AT_ONCE * kernels // 2 * COARSE, 2 * FB), jnp.float32),
             pltpu.VMEM((TILES_AT_ONCE * TILE, TILE), jnp.float32),
             pltpu.SemaphoreType.DMA((TILES_AT_ONCE,)),
         ],

time: 58 us -> 54.1 us (0.933)
  Pallas kernels: 23.4 us -> 19.7 us
    pallas_call x1, Pallas kernels: 13.7 us -> 10.8 us  [imaging(): pl.pallas_call(imaging_kernel, grid=(tiles // TILES_AT_ONCE,), out_shape=...]
    pallas_call x1, Pallas kernels: 5.88 us -> 5.07 us  [analysis(): pl.pallas_call(analysis_kernel, grid=(tiles // PAIR,), out_shape=(total,...]
where the time goes in v6:
time: 54.1 us; the launch traced here: 53.9 us
  starting transfers between devices  21.7 us (40%)
  Pallas kernels  19.7 us (36%)
  waiting for transfers between devices  9.7 us (18%)
  local copies, waits for them, and re-layouts  1.94 us (4%)
  between operations  0.81 us (1%)
    ppermute x9, starting transfers between devices, swap(): return lax.ppermute(value, axis, swap_pairs(lax.axis_size(axis), first))  14.9 us
    pallas_call x1, Pallas kernels, imaging(): pl.pallas_call(imaging_kernel, grid=(tiles // TILES_AT_ONCE,), out_shape=...  10.8 us
    ppermute x9, waiting for transfers between devices, swap(): return lax.ppermute(value, axis, swap_pairs(lax.axis_size(axis), first))  9.7 us
    ppermute x1, starting transfers between devices, local(): mine = lax.ppermute(half, ('gy', 'ka'), pairs)  6.83 us
    pallas_call x1, Pallas kernels, analysis(): pl.pallas_call(analysis_kernel, grid=(tiles // PAIR,), out_shape=(total,...  5.07 us
    pallas_call x1, Pallas kernels, inner_synthesis(): pl.pallas_call(inner_kernel, out_shape=jax.ShapeDtypeStruct(slope.shape,...  1.95 us
    unnamed x12, local copies, waits for them, and re-layouts  1.94 us
    pallas_call x1, Pallas kernels, outer_synthesis(): pl.pallas_call(outer_kernel, out_shape=jax.ShapeDtypeStruct(slope.shape,...  1.5 us
  transfers between devices with their start and end apart: 10, of which 4 were waited for; matrix products, arithmetic and copies ran while one was open for 0% of the time, Pallas kernels for 4%

profile of v6, /device:TPU:40, one launch (start us, length us, event | category | flops | bytes accessed | tf_op | source)
XLA Modules:
  0.0 53.9 jit_solution(401046596886825106)
XLA Ops:
  0.6 0.0 copy-start.2
  0.6 0.0 copy-start
  0.7 5.1 %analysis.1 = (f32[6,64,256]{2,1,0:T(8,128)}, f32[6,64,128]{2,1,0:T(8,128)}, f32[3,64,128]{2,1,0:T(8,128)}, f32[64,256]{1,0:T(8,128)}, f32[64,256]{1,0:T(8,128)}, /*index=5*/f32[1536,256]{1,0:T(8,128)}) custom-call(f32[1536,256]{1,0:T(8,128)} %mask_in.1, f32[6,2,4096]{2,1,0:T(2,128)} %kernels_in.1, f32[6]{0:T(128)} %weights.1, ...), custom_call_target="tpu_custom_call" | custom-call | tf_op jit(solution)/shard_map/analysis/pallas_call | solution.py:567
  5.7 1.6 %collective-permute-start = (f32[64,256]{1,0:T(8,128)}, f32[64,256]{1,0:T(8,128)S(1)}, u32[]{:S(2)}, u32[]{:S(2)}) collective-permute-start(f32[64,256]{1,0:T(8,128)} %get-tuple-element.26), channel_id=1, source_target_pairs={{0,2},{2,0},{4,6},{6,4},{8,10},{10,8},{12,14},{14,12},{16,18},{18,... | collective-permute-start | bytes 196616 | tf_op jit(solution)/shard_map/ppermute | solution.py:708
  7.3 3.5 %collective-permute-start.1 = (f32[64,256]{1,0:T(8,128)}, f32[64,256]{1,0:T(8,128)S(1)}, u32[]{:S(2)}, u32[]{:S(2)}) collective-permute-start(f32[64,256]{1,0:T(8,128)} %get-tuple-element.27), channel_id=1, source_target_pairs={{2,4},{4,2},{6,8},{8,6},{10,12},{12,10},{14,16},{16,14},{18,20},{2... | collective-permute-start | bytes 196616 | tf_op jit(solution)/shard_map/ppermute | solution.py:708
  10.9 6.8 %collective-permute-start.4 = (f32[3,64,128]{2,1,0:T(8,128)}, f32[3,64,128]{2,1,0:T(8,128)S(1)}, u32[]{:S(2)}, u32[]{:S(2)}) collective-permute-start(f32[3,64,128]{2,1,0:T(8,128)} %get-tuple-element.34), channel_id=1, source_target_pairs={{0,25},{1,24},{2,27},{3,26},{4,29},{5,28},{6,31},{7,30},{8,17},{9,... | collective-permute-start | bytes 294920 | tf_op jit(solution)/shard_map/ppermute | solution.py:716
  17.7 1.0 %copy-done.3 = f32[6,64,256]{2,1,0:T(8,128)S(1)} copy-done((f32[6,64,256]{2,1,0:T(8,128)S(1)}, f32[6,64,256]{2,1,0:T(8,128)}, u32[]{:S(2)}) %copy-start.3) | copy-done | bytes 393240
  18.7 0.1 shares.1
  18.7 0.0 collective-permute-done.near_even
  18.8 0.0 collective-permute-done.1.near_odd
  18.8 0.1 merge.1
  18.8 0.1 collective-permute-start.2
  18.9 2.4 %collective-permute-start.3 = (f32[6,64,128]{2,1,0:T(8,128)S(1)}, f32[6,64,128]{2,1,0:T(8,128)S(1)}, u32[]{:S(2)}, u32[]{:S(2)}) collective-permute-start(f32[6,64,128]{2,1,0:T(8,128)S(1)} %get-tuple-element.30), channel_id=1, source_target_pairs={{32,64},{64,32},{96,128},{128,96},{160,192},{192,160},{33,65},{65,... | collective-permute-start | bytes 589832 | tf_op jit(solution)/shard_map/ppermute | solution.py:708
  21.4 0.0 collective-permute-done.4.mine
  21.4 1.2 %collective-permute-start.5 = (f32[3,64,128]{2,1,0:T(8,128)S(1)}, f32[3,64,128]{2,1,0:T(8,128)S(1)}, u32[]{:S(2)}, u32[]{:S(2)}) collective-permute-start(f32[3,64,128]{2,1,0:T(8,128)S(1)} %collective-permute-done.4.mine), channel_id=1, source_target_pairs={{0,32},{32,0},{64,96},{96,64},{128,160},{160,128},{192,224},{224,1... | collective-permute-start | bytes 294920 | tf_op jit(solution)/shard_map/ppermute | solution.py:708
  22.6 0.9 %copy-done.5 = f32[6,64,128]{2,1,0:T(8,128)S(1)} copy-done((f32[6,64,128]{2,1,0:T(8,128)S(1)}, f32[6,64,128]{2,1,0:T(8,128)}, u32[]{:S(2)}) %copy-start.5) | copy-done | bytes 196632
  23.6 0.1 prepare_own.1
  23.7 0.0 collective-permute-done.5.partners
  23.7 0.1 prepare_other.1
  23.8 0.0 collective-permute-done.2.from_even
  23.8 2.1 %collective-permute-done.3.from_odd = f32[6,64,128]{2,1,0:T(8,128)S(1)} collective-permute-done((f32[6,64,128]{2,1,0:T(8,128)S(1)}, f32[6,64,128]{2,1,0:T(8,128)S(1)}, u32[]{:S(2)}, u32[]{:S(2)}) %collective-permute-start.3) | collective-permute-done | bytes 196640 | tf_op jit(solution)/shard_map/ppermute | solution.py:708
  25.9 10.8 %imaging.1 = (f32[1536,256]{1,0:T(8,128)}, f32[6,64,128]{2,1,0:T(8,128)S(1)}) custom-call(f32[6,64,128]{2,1,0:T(8,128)S(1)} %get-tuple-element.28.share, f32[6,64,128]{2,1,0:T(8,128)S(1)} %collective-permute-done.2.from_even, f32[6,64,128]{2,1,0:T(8,128)S(1)} %collective-permute-done.3.from_odd, f32[6,64,128]{2,1,0:T(8,128)S(1)} %get-tuple-element.32.straight_own, ...), custom_call_target="tpu_custom_call" | custom-call | tf_op jit(solution)/shard_map/imaging/pallas_call | solution.py:639
  36.7 2.4 %collective-permute-start.7 = (f32[6,64,128]{2,1,0:T(8,128)S(1)}, f32[6,64,128]{2,1,0:T(8,128)S(1)}, u32[]{:S(2)}, u32[]{:S(2)}) collective-permute-start(f32[6,64,128]{2,1,0:T(8,128)S(1)} %get-tuple-element.37.own), channel_id=1, source_target_pairs={{32,64},{64,32},{96,128},{128,96},{160,192},{192,160},{33,65},{65,... | collective-permute-start | bytes 589832 | tf_op jit(solution)/shard_map/ppermute | solution.py:708
  39.2 1.2 %collective-permute-start.6 = (f32[6,64,128]{2,1,0:T(8,128)S(1)}, f32[6,64,128]{2,1,0:T(8,128)S(1)}, u32[]{:S(2)}, u32[]{:S(2)}) collective-permute-start(f32[6,64,128]{2,1,0:T(8,128)S(1)} %get-tuple-element.37.own), channel_id=1, source_target_pairs={{0,32},{32,0},{64,96},{96,64},{128,160},{160,128},{192,224},{224,1... | collective-permute-start | bytes 589832 | tf_op jit(solution)/shard_map/ppermute | solution.py:708
  40.4 3.3 %collective-permute-done.7.odd_in = f32[6,64,128]{2,1,0:T(8,128)S(1)} collective-permute-done((f32[6,64,128]{2,1,0:T(8,128)S(1)}, f32[6,64,128]{2,1,0:T(8,128)S(1)}, u32[]{:S(2)}, u32[]{:S(2)}) %collective-permute-start.7) | collective-permute-done | bytes 196640 | tf_op jit(solution)/shard_map/ppermute | solution.py:708
  43.7 0.0 collective-permute-done.6.even_in
  43.8 0.2 collective-permute-start.8
  44.0 2.1 %collective-permute-start.9 = (f32[64,256]{1,0:T(8,128)S(1)}, f32[64,256]{1,0:T(8,128)S(1)}, u32[]{:S(2)}, u32[]{:S(2)}) collective-permute-start(f32[64,256]{1,0:T(8,128)S(1)} %get-tuple-element.39), channel_id=1, source_target_pairs={{2,4},{4,2},{6,8},{8,6},{10,12},{12,10},{14,16},{16,14},{18,20},{2... | collective-permute-start | bytes 196616 | tf_op jit(solution)/shard_map/ppermute | solution.py:708
  46.1 1.9 %inner_synthesis.1.partial = f32[1536,256]{1,0:T(8,128)} custom-call(f32[6,64,128]{2,1,0:T(8,128)S(1)} %get-tuple-element.37.own, f32[6,64,128]{2,1,0:T(8,128)S(1)} %collective-permute-done.6.even_in, f32[6,64,128]{2,1,0:T(8,128)S(1)} %collective-permute-done.7.odd_in, f32[1536,256]{1,0:T(8,128)S(1)} %copy-done.1, bf16[1024,128]{1,0:T(8,128)(2,1)S(1)} %copy-done.4), custom_call_target="tpu_custom_call" | custom-call | flops 1500000000 | bytes 2500000 | tf_op jit(solution)/shard_map/inner_synthesis/pallas_call | solution.py:662
  48.1 0.3 collective-permute-done.8.near_even
  48.3 4.0 %collective-permute-done.9.near_odd = f32[64,256]{1,0:T(8,128)S(1)} collective-permute-done((f32[64,256]{1,0:T(8,128)S(1)}, f32[64,256]{1,0:T(8,128)S(1)}, u32[]{:S(2)}, u32[]{:S(2)}) %collective-permute-start.9) | collective-permute-done | bytes 65568 | tf_op jit(solution)/shard_map/ppermute | solution.py:708
  52.4 1.5 %outer_synthesis.1 = f32[1536,256]{1,0:T(8,128)} custom-call(f32[6,64,128]{2,1,0:T(8,128)S(1)} %get-tuple-element.37.own, f32[6,64,128]{2,1,0:T(8,128)S(1)} %collective-permute-done.6.even_in, f32[6,64,128]{2,1,0:T(8,128)S(1)} %collective-permute-done.7.odd_in, f32[64,256]{1,0:T(8,128)S(1)} %collective-permute-done.8.near_even, ...), custom_call_target="tpu_custom_call", output_to_operand_aliasing={{}: (7, {})} | custom-call | tf_op jit(solution)/shard_map/outer_synthesis/pallas_call | solution.py:682
  (9 shorter events, 0.0 us)
Async XLA Ops:
  0.6 25.3 %copy-start.2 = (bf16[4608,128]{1,0:T(8,128)(2,1)S(1)}, bf16[4608,128]{1,0:T(8,128)(2,1)}, u32[]{:S(2)}) copy-start(bf16[4608,128]{1,0:T(8,128)(2,1)} %constant.7.clone.wide) | copy-start | bytes 3538948
  0.6 25.3 %copy-start = (s32[1536,256]{1,0:T(8,128)S(1)}, s32[1536,256]{1,0:T(8,128)}, u32[]{:S(2)}) copy-start(s32[1536,256]{1,0:T(8,128)} %target.1) | copy-start | bytes 4718596
  5.7 13.0 %collective-permute-start = (f32[64,256]{1,0:T(8,128)}, f32[64,256]{1,0:T(8,128)S(1)}, u32[]{:S(2)}, u32[]{:S(2)}) collective-permute-start(f32[64,256]{1,0:T(8,128)} %get-tuple-element.26), channel_id=1, source_target_pairs={{0,2},{2,0},{4,6},{6,4},{8,10},{10,8},{12,14},{14,12},{16,18},{18,... | collective-permute-start | bytes 196616 | tf_op jit(solution)/shard_map/ppermute | solution.py:708
  7.3 11.5 %collective-permute-start.1 = (f32[64,256]{1,0:T(8,128)}, f32[64,256]{1,0:T(8,128)S(1)}, u32[]{:S(2)}, u32[]{:S(2)}) collective-permute-start(f32[64,256]{1,0:T(8,128)} %get-tuple-element.27), channel_id=1, source_target_pairs={{2,4},{4,2},{6,8},{8,6},{10,12},{12,10},{14,16},{16,14},{18,20},{2... | collective-permute-start | bytes 196616 | tf_op jit(solution)/shard_map/ppermute | solution.py:708
  10.9 10.5 %collective-permute-start.4 = (f32[3,64,128]{2,1,0:T(8,128)}, f32[3,64,128]{2,1,0:T(8,128)S(1)}, u32[]{:S(2)}, u32[]{:S(2)}) collective-permute-start(f32[3,64,128]{2,1,0:T(8,128)} %get-tuple-element.34), channel_id=1, source_target_pairs={{0,25},{1,24},{2,27},{3,26},{4,29},{5,28},{6,31},{7,30},{8,17},{9,... | collective-permute-start | bytes 294920 | tf_op jit(solution)/shard_map/ppermute | solution.py:716
  17.7 1.0 %copy-start.3 = (f32[6,64,256]{2,1,0:T(8,128)S(1)}, f32[6,64,256]{2,1,0:T(8,128)}, u32[]{:S(2)}) copy-start(f32[6,64,256]{2,1,0:T(8,128)} %get-tuple-element.22.total) | copy-start | bytes 1179652
  18.8 5.0 %collective-permute-start.2 = (f32[6,64,128]{2,1,0:T(8,128)S(1)}, f32[6,64,128]{2,1,0:T(8,128)S(1)}, u32[]{:S(2)}, u32[]{:S(2)}) collective-permute-start(f32[6,64,128]{2,1,0:T(8,128)S(1)} %get-tuple-element.29), channel_id=1, source_target_pairs={{0,32},{32,0},{64,96},{96,64},{128,160},{160,128},{192,224},{224,1... | collective-permute-start | bytes 589832 | tf_op jit(solution)/shard_map/ppermute | solution.py:708
  18.9 7.0 %collective-permute-start.3 = (f32[6,64,128]{2,1,0:T(8,128)S(1)}, f32[6,64,128]{2,1,0:T(8,128)S(1)}, u32[]{:S(2)}, u32[]{:S(2)}) collective-permute-start(f32[6,64,128]{2,1,0:T(8,128)S(1)} %get-tuple-element.30), channel_id=1, source_target_pairs={{32,64},{64,32},{96,128},{128,96},{160,192},{192,160},{33,65},{65,... | collective-permute-start | bytes 589832 | tf_op jit(solution)/shard_map/ppermute | solution.py:708
  21.4 2.3 %collective-permute-start.5 = (f32[3,64,128]{2,1,0:T(8,128)S(1)}, f32[3,64,128]{2,1,0:T(8,128)S(1)}, u32[]{:S(2)}, u32[]{:S(2)}) collective-permute-start(f32[3,64,128]{2,1,0:T(8,128)S(1)} %collective-permute-done.4.mine), channel_id=1, source_target_pairs={{0,32},{32,0},{64,96},{96,64},{128,160},{160,128},{192,224},{224,1... | collective-permute-start | bytes 294920 | tf_op jit(solution)/shard_map/ppermute | solution.py:708
  22.6 0.9 %copy-start.5 = (f32[6,64,128]{2,1,0:T(8,128)S(1)}, f32[6,64,128]{2,1,0:T(8,128)}, u32[]{:S(2)}) copy-start(f32[6,64,128]{2,1,0:T(8,128)} %get-tuple-element.31.own) | copy-start | bytes 589828
  25.9 20.2 %copy-start.1 = (f32[1536,256]{1,0:T(8,128)S(1)}, f32[1536,256]{1,0:T(8,128)}, u32[]{:S(2)}) copy-start(f32[1536,256]{1,0:T(8,128)} %get-tuple-element.40.slope) | copy-start | bytes 4718596
  25.9 20.2 %copy-start.4 = (bf16[1024,128]{1,0:T(8,128)(2,1)S(1)}, bf16[1024,128]{1,0:T(8,128)(2,1)}, u32[]{:S(2)}) copy-start(bf16[1024,128]{1,0:T(8,128)(2,1)} %constant.8.clone.tables) | copy-start | bytes 786436
  36.7 7.0 %collective-permute-start.7 = (f32[6,64,128]{2,1,0:T(8,128)S(1)}, f32[6,64,128]{2,1,0:T(8,128)S(1)}, u32[]{:S(2)}, u32[]{:S(2)}) collective-permute-start(f32[6,64,128]{2,1,0:T(8,128)S(1)} %get-tuple-element.37.own), channel_id=1, source_target_pairs={{32,64},{64,32},{96,128},{128,96},{160,192},{192,160},{33,65},{65,... | collective-permute-start | bytes 589832 | tf_op jit(solution)/shard_map/ppermute | solution.py:708
  39.2 4.5 %collective-permute-start.6 = (f32[6,64,128]{2,1,0:T(8,128)S(1)}, f32[6,64,128]{2,1,0:T(8,128)S(1)}, u32[]{:S(2)}, u32[]{:S(2)}) collective-permute-start(f32[6,64,128]{2,1,0:T(8,128)S(1)} %get-tuple-element.37.own), channel_id=1, source_target_pairs={{0,32},{32,0},{64,96},{96,64},{128,160},{160,128},{192,224},{224,1... | collective-permute-start | bytes 589832 | tf_op jit(solution)/shard_map/ppermute | solution.py:708
  43.8 4.6 %collective-permute-start.8 = (f32[64,256]{1,0:T(8,128)S(1)}, f32[64,256]{1,0:T(8,128)S(1)}, u32[]{:S(2)}, u32[]{:S(2)}) collective-permute-start(f32[64,256]{1,0:T(8,128)S(1)} %get-tuple-element.38), channel_id=1, source_target_pairs={{0,2},{2,0},{4,6},{6,4},{8,10},{10,8},{12,14},{14,12},{16,18},{18,... | collective-permute-start | bytes 196616 | tf_op jit(solution)/shard_map/ppermute | solution.py:708
  44.0 8.3 %collective-permute-start.9 = (f32[64,256]{1,0:T(8,128)S(1)}, f32[64,256]{1,0:T(8,128)S(1)}, u32[]{:S(2)}, u32[]{:S(2)}) collective-permute-start(f32[64,256]{1,0:T(8,128)S(1)} %get-tuple-element.39), channel_id=1, source_target_pairs={{2,4},{4,2},{6,8},{8,6},{10,12},{12,10},{14,16},{16,14},{18,20},{2... | collective-permute-start | bytes 196616 | tf_op jit(solution)/shard_map/ppermute | solution.py:708

commit v7 on v6

--- a/solution.py
+++ b/solution.py
@@ -66,57 +66,35 @@
     plus = 4 * np.arange(HALF) + 2
     samples = np.concatenate([plus, -plus])
     cos, sin = np.cos(angles(samples)), np.sin(angles(samples))
-    spread = as_right(
-        np.concatenate(
-            [np.concatenate([cos, sin], axis=1), np.concatenate([-sin, cos], axis=1)], axis=0
-        )
-    )
-    gather = np.concatenate(
-        [np.concatenate([cos.T, -sin.T], axis=1), np.concatenate([sin.T, cos.T], axis=1)], axis=0
-    )
-    gather = np.concatenate(halves(gather), axis=1)
-    cos, sin = np.cos(angles(plus))[ORDER], np.sin(angles(plus))[ORDER]
-    lift = as_left(np.concatenate([cos.T, sin.T], axis=0))
-    lift = np.concatenate([lift, np.zeros((COARSE, 64), bf16)], axis=1)
-    high, low = halves(np.concatenate([cos, sin], axis=1))
-    fold = np.concatenate(
-        [np.concatenate([high, high], axis=1), np.concatenate([low, 0 * low], axis=1)], axis=0
-    )
+    spread = np.concatenate(
+        [np.concatenate([cos, sin], axis=1), np.concatenate([-sin, cos], axis=1)], axis=0
+    )
+    gather = spread.T
+    order = np.concatenate([ORDER, FB + ORDER])
     offset = (np.arange(TILE) + HALO)[:, None] - samples[None, :]
     orders = np.arange(1, COARSE // 2)
     turns = np.mod(offset[..., None] * orders, WIN) * (2.0 * math.pi / WIN)
     interp = (1.0 + 2.0 * np.cos(turns).sum(-1)) / COARSE
-    high, low = halves(interp)
-    fine_left = np.concatenate(
-        [np.concatenate([high, high], axis=1), np.concatenate([low, 0 * low], axis=1)], axis=0
-    )
-    coarse_left = np.concatenate(halves(interp.T), axis=0)
-    coarse_right = np.concatenate(halves(interp), axis=1)
+    imaging = (
+        as_right(spread),
+        as_right(spread[order]),
+        np.concatenate(halves(gather), axis=1),
+        np.concatenate(halves(gather[:, order]), axis=1),
+        as_right(interp.T),
+        np.concatenate(halves(interp), axis=1),
+    )
     return {
         "analysis": np.concatenate(columns + rows, axis=0),
         "synthesis": np.concatenate(pixs + outs, axis=0),
-        "imaging": np.concatenate(
-            sum(
-                map(
-                    blocks,
-                    (
-                        spread, gather, lift, fold, as_right(interp.T), fine_left, coarse_left,
-                        coarse_right,
-                    ),
-                ),
-                [],
-            ),
-            axis=0,
-        ),
+        "imaging": np.concatenate(sum(map(blocks, imaging), []), axis=0),
     }
 
 
 TABLES = make_tables()
-SPREAD, GATHER, LIFT, FOLD, FINE_RIGHT, FINE_LEFT, COARSE_LEFT, COARSE_RIGHT = (
+SPREAD, SPREAD_ROWS, GATHER, GATHER_ROWS, FINE, COARSEN = (
     (2 * a, b - a)
     for a, b in (
-        (0, 384), (384, 640), (640, 768), (768, 896), (896, 1280), (1280, 1792), (1792, 2048),
-        (2048, 2304),
+        (0, 384), (384, 768), (768, 1024), (1024, 1280), (1280, 1664), (1664, 1920),
     )
 )
 
@@ -364,15 +342,19 @@
         to_odd[index] += jnp.where(odd_col, right, left)
 
 
+def parts(value, count):
+    size = value.shape[0] // count
+    return [value[index * size : (index + 1) * size] for index in range(count)]
+
+
 def imaging_kernel(
     share, from_even, from_odd, straight_own, crossed_own, straight_other, crossed_other,
     target, wide, resist_out, grad, fields, sides, resists, semaphores,
 ):
     count = straight_own.shape[0]
     straights, crosseds = (straight_own, straight_other), (crossed_own, crossed_other)
-    copies = []
-    sign = jnp.where(low_lanes((HALF, 2 * FB)), 1.0, -1.0)
     tiles = range(share.shape[0])
+    size = len(tiles) * count
     intensities = [[] for tile in tiles]
 
     spectra = [share[tile] + from_even[tile] + from_odd[tile] for tile in tiles]
@@ -384,30 +366,30 @@
             for i in range(count)
         ]
         rows = times_table(jnp.concatenate(products, axis=0), wide_table(wide, SPREAD))
+        columns = [
+            jnp.concatenate([part[:, :COARSE], part[:, COARSE:]], axis=0).T
+            for part in parts(rows, size)
+        ]
+        found = times_table(jnp.concatenate(columns, axis=0), wide_table(wide, SPREAD_ROWS))
+        fields[group] = found
+        powers = [
+            part[:, :COARSE] * part[:, :COARSE] + part[:, COARSE:] * part[:, COARSE:]
+            for part in parts(found, size)
+        ]
         for tile in tiles:
-            total = jnp.zeros((COARSE, COARSE), jnp.float32)
-            for i in range(count):
-                place = (tile * count + i) * FB
-                both = table_times(wide_table(wide, LIFT)[:, :192], rows[place : place + FB])
-                cosine, sine = both[:HALF], both[HALF:]
-                sine_re, sine_im = sine[:, :COARSE], sine[:, COARSE:]
-                cosine_re, cosine_im = cosine[:, :COARSE], cosine[:, COARSE:]
-                real = jnp.concatenate([cosine_re - sine_im, cosine_re + sine_im], axis=0)
-                imag = jnp.concatenate([cosine_im + sine_re, cosine_im - sine_re], axis=0)
-                fields[tile, group * count + i, :, :COARSE] = real
-                fields[tile, group * count + i, :, COARSE:] = imag
-                total = total + (real * real + imag * imag)
-            intensities[tile].append(total)
+            intensities[tile].append(sum(powers[tile * count : (tile + 1) * count]))
 
     half_fine = times_table(
         jnp.concatenate([first + second for first, second in intensities], axis=0),
-        wide_table(wide, FINE_RIGHT),
-    )
-    half_coarse = []
-    for tile in tiles:
-        fine = stacked_times(
-            wide_table(wide, FINE_LEFT), half_fine[tile * COARSE : (tile + 1) * COARSE]
-        )
+        wide_table(wide, FINE),
+    )
+    fines = times_table(
+        jnp.concatenate([part.T for part in parts(half_fine, len(tiles))], axis=0),
+        wide_table(wide, FINE),
+    )
+    pushes = []
+    copies = []
+    for tile, fine in enumerate(parts(fines, len(tiles))):
         resist = jax.nn.sigmoid(4.0 * (fine - 1.0))
         place = slice(tile * TILE, (tile + 1) * TILE)
         resists[place, :] = resist
@@ -420,48 +402,40 @@
         copy.start()
         copies.append(copy)
         misfit = resist - target[place, :].astype(jnp.float32)
-        push = 16.0 * misfit * resist * (1.0 - resist)
-        high, low = split(push)
-        from_high = dot(wide_table(wide, COARSE_LEFT), high)
-        half_coarse.append(
-            from_high[:COARSE]
-            + (from_high[COARSE:] + dot(wide_table(wide, COARSE_LEFT)[:COARSE], low))
-        )
-    weights = times_paired(jnp.concatenate(half_coarse, axis=0), wide_table(wide, COARSE_RIGHT))
+        pushes.append(16.0 * misfit * resist * (1.0 - resist))
+    half_coarse = times_paired(jnp.concatenate(pushes, axis=0), wide_table(wide, COARSEN))
+    weights = times_paired(
+        jnp.concatenate([part.T for part in parts(half_coarse, len(tiles))], axis=0),
+        wide_table(wide, COARSEN),
+    )
     scales = [
-        jnp.concatenate([weights[tile * COARSE : (tile + 1) * COARSE]] * 2, axis=1)
-        for tile in tiles
+        jnp.concatenate([weight, weight], axis=1) for weight in parts(weights, len(tiles))
     ]
 
     adjoint = [[] for tile in tiles]
     for group in range(2):
         scaled = [
-            fields[tile, group * count + i] * scales[tile]
+            fields[group, (tile * count + i) * COARSE : (tile * count + i + 1) * COARSE, :]
+            * scales[tile]
             for tile in tiles
             for i in range(count)
         ]
         sides[group] = times_paired(
-            jnp.concatenate(scaled, axis=0), wide_table(wide, GATHER)
+            jnp.concatenate(scaled, axis=0), wide_table(wide, GATHER_ROWS)
         )
+        columns = []
+        for index in range(size):
+            column = sides[group, index * COARSE : (index + 1) * COARSE, :].T
+            columns.append(jnp.concatenate([column[:FB], column[FB:]], axis=1))
+        found = times_paired(jnp.concatenate(columns, axis=0), wide_table(wide, GATHER))
         for tile in tiles:
             total = jnp.zeros((FB, 2 * FB), jnp.float32)
-            for i in range(0, count, 2):
-                pair = []
-                for j in (i, i + 1):
-                    place = (tile * count + j) * COARSE
-                    plus = sides[group, place : place + HALF, :]
-                    minus = sides[group, place + HALF : place + COARSE, :]
-                    pair.append(
-                        jnp.concatenate([plus + minus, sign * swapped(plus - minus)], axis=0)
-                    )
-                found = stacked_times(
-                    wide_table(wide, FOLD), jnp.concatenate(pair, axis=1)
+            for i in range(count):
+                place = (tile * count + i) * FB
+                part = found[place : place + FB]
+                total = total + (
+                    straights[group][i] * part - crosseds[group][i] * swapped(part)
                 )
-                for j in (0, 1):
-                    part = found[:, j * 2 * FB : (j + 1) * 2 * FB]
-                    total = total + (
-                        straights[group][i + j] * part - crosseds[group][i + j] * swapped(part)
-                    )
             adjoint[tile].append(total)
     for tile in tiles:
         grad[tile] = adjoint[tile][0] + adjoint[tile][1]
@@ -646,7 +620,7 @@
         in_specs=[spectra] * 3 + [whole(own[0])] * 4 + [pixels, whole(tables)],
         out_specs=[pl.BlockSpec(memory_space=pl.ANY), spectra],
         scratch_shapes=[
-            pltpu.VMEM((TILES_AT_ONCE, kernels, COARSE, 2 * COARSE), jnp.float32),
+            pltpu.VMEM((2, TILES_AT_ONCE * kernels // 2 * COARSE, 2 * COARSE), jnp.float32),
             pltpu.VMEM((2, TILES_AT_ONCE * kernels // 2 * COARSE, 2 * FB), jnp.float32),
             pltpu.VMEM((TILES_AT_ONCE * TILE, TILE), jnp.float32),
             pltpu.SemaphoreType.DMA((TILES_AT_ONCE,)),

time: 54.1 us -> 55.8 us (1.031)
  Pallas kernels: 19.7 us -> 21.3 us
    pallas_call x1, Pallas kernels: 10.8 us -> 12.4 us  [imaging(): pl.pallas_call(imaging_kernel, grid=(tiles // TILES_AT_ONCE,), out_shape=...]
where the time goes in v7:
time: 55.8 us; the launch traced here: 55.5 us
  starting transfers between devices  21.7 us (39%)
  Pallas kernels  21.3 us (38%)
  waiting for transfers between devices  9.7 us (17%)
  local copies, waits for them, and re-layouts  1.94 us (3%)
  between operations  0.81 us (1%)
    ppermute x9, starting transfers between devices, swap(): return lax.ppermute(value, axis, swap_pairs(lax.axis_size(axis), first))  14.9 us
    pallas_call x1, Pallas kernels, imaging(): pl.pallas_call(imaging_kernel, grid=(tiles // TILES_AT_ONCE,), out_shape=...  12.4 us
    ppermute x9, waiting for transfers between devices, swap(): return lax.ppermute(value, axis, swap_pairs(lax.axis_size(axis), first))  9.7 us
    ppermute x1, starting transfers between devices, local(): mine = lax.ppermute(half, ('gy', 'ka'), pairs)  6.83 us
    pallas_call x1, Pallas kernels, analysis(): pl.pallas_call(analysis_kernel, grid=(tiles // PAIR,), out_shape=(total,...  5.07 us
    pallas_call x1, Pallas kernels, inner_synthesis(): pl.pallas_call(inner_kernel, out_shape=jax.ShapeDtypeStruct(slope.shape,...  1.95 us
    unnamed x12, local copies, waits for them, and re-layouts  1.94 us
    pallas_call x1, Pallas kernels, outer_synthesis(): pl.pallas_call(outer_kernel, out_shape=jax.ShapeDtypeStruct(slope.shape,...  1.5 us
  transfers between devices with their start and end apart: 10, of which 4 were waited for; matrix products, arithmetic and copies ran while one was open for 0% of the time, Pallas kernels for 4%

profile of v7, /device:TPU:40, one launch (start us, length us, event | category | flops | bytes accessed | tf_op | source)
XLA Modules:
  0.0 55.5 jit_solution(9421044638901844067)
XLA Ops:
  0.6 0.0 copy-start.2
  0.7 5.1 %analysis.1 = (f32[6,64,256]{2,1,0:T(8,128)}, f32[6,64,128]{2,1,0:T(8,128)}, f32[3,64,128]{2,1,0:T(8,128)}, f32[64,256]{1,0:T(8,128)}, f32[64,256]{1,0:T(8,128)}, /*index=5*/f32[1536,256]{1,0:T(8,128)}) custom-call(f32[1536,256]{1,0:T(8,128)} %mask_in.1, f32[6,2,4096]{2,1,0:T(2,128)} %kernels_in.1, f32[6]{0:T(128)} %weights.1, ...), custom_call_target="tpu_custom_call" | custom-call | tf_op jit(solution)/shard_map/analysis/pallas_call | solution.py:541
  5.7 1.6 %collective-permute-start = (f32[64,256]{1,0:T(8,128)}, f32[64,256]{1,0:T(8,128)S(1)}, u32[]{:S(2)}, u32[]{:S(2)}) collective-permute-start(f32[64,256]{1,0:T(8,128)} %get-tuple-element.26), channel_id=1, source_target_pairs={{0,2},{2,0},{4,6},{6,4},{8,10},{10,8},{12,14},{14,12},{16,18},{18,... | collective-permute-start | bytes 196616 | tf_op jit(solution)/shard_map/ppermute | solution.py:682
  7.3 3.5 %collective-permute-start.1 = (f32[64,256]{1,0:T(8,128)}, f32[64,256]{1,0:T(8,128)S(1)}, u32[]{:S(2)}, u32[]{:S(2)}) collective-permute-start(f32[64,256]{1,0:T(8,128)} %get-tuple-element.27), channel_id=1, source_target_pairs={{2,4},{4,2},{6,8},{8,6},{10,12},{12,10},{14,16},{16,14},{18,20},{2... | collective-permute-start | bytes 196616 | tf_op jit(solution)/shard_map/ppermute | solution.py:682
  10.9 6.8 %collective-permute-start.4 = (f32[3,64,128]{2,1,0:T(8,128)}, f32[3,64,128]{2,1,0:T(8,128)S(1)}, u32[]{:S(2)}, u32[]{:S(2)}) collective-permute-start(f32[3,64,128]{2,1,0:T(8,128)} %get-tuple-element.34), channel_id=1, source_target_pairs={{0,25},{1,24},{2,27},{3,26},{4,29},{5,28},{6,31},{7,30},{8,17},{9,... | collective-permute-start | bytes 294920 | tf_op jit(solution)/shard_map/ppermute | solution.py:690
  17.7 1.0 %copy-done.3 = f32[6,64,256]{2,1,0:T(8,128)S(1)} copy-done((f32[6,64,256]{2,1,0:T(8,128)S(1)}, f32[6,64,256]{2,1,0:T(8,128)}, u32[]{:S(2)}) %copy-start.3) | copy-done | bytes 393240
  18.7 0.1 shares.1
  18.7 0.0 collective-permute-done.near_even
  18.8 0.0 collective-permute-done.1.near_odd
  18.8 0.1 merge.1
  18.8 0.1 collective-permute-start.2
  18.9 2.4 %collective-permute-start.3 = (f32[6,64,128]{2,1,0:T(8,128)S(1)}, f32[6,64,128]{2,1,0:T(8,128)S(1)}, u32[]{:S(2)}, u32[]{:S(2)}) collective-permute-start(f32[6,64,128]{2,1,0:T(8,128)S(1)} %get-tuple-element.30), channel_id=1, source_target_pairs={{32,64},{64,32},{96,128},{128,96},{160,192},{192,160},{33,65},{65,... | collective-permute-start | bytes 589832 | tf_op jit(solution)/shard_map/ppermute | solution.py:682
  21.4 0.0 collective-permute-done.4.mine
  21.4 1.2 %collective-permute-start.5 = (f32[3,64,128]{2,1,0:T(8,128)S(1)}, f32[3,64,128]{2,1,0:T(8,128)S(1)}, u32[]{:S(2)}, u32[]{:S(2)}) collective-permute-start(f32[3,64,128]{2,1,0:T(8,128)S(1)} %collective-permute-done.4.mine), channel_id=1, source_target_pairs={{0,32},{32,0},{64,96},{96,64},{128,160},{160,128},{192,224},{224,1... | collective-permute-start | bytes 294920 | tf_op jit(solution)/shard_map/ppermute | solution.py:682
  22.6 0.9 %copy-done.5 = f32[6,64,128]{2,1,0:T(8,128)S(1)} copy-done((f32[6,64,128]{2,1,0:T(8,128)S(1)}, f32[6,64,128]{2,1,0:T(8,128)}, u32[]{:S(2)}) %copy-start.5) | copy-done | bytes 196632
  23.6 0.1 prepare_own.1
  23.7 0.0 collective-permute-done.5.partners
  23.7 0.1 prepare_other.1
  23.8 0.0 collective-permute-done.2.from_even
  23.8 2.1 %collective-permute-done.3.from_odd = f32[6,64,128]{2,1,0:T(8,128)S(1)} collective-permute-done((f32[6,64,128]{2,1,0:T(8,128)S(1)}, f32[6,64,128]{2,1,0:T(8,128)S(1)}, u32[]{:S(2)}, u32[]{:S(2)}) %collective-permute-start.3) | collective-permute-done | bytes 196640 | tf_op jit(solution)/shard_map/ppermute | solution.py:682
  25.9 0.0 copy-done.2
  25.9 12.4 %imaging.1 = (f32[1536,256]{1,0:T(8,128)}, f32[6,64,128]{2,1,0:T(8,128)S(1)}) custom-call(f32[6,64,128]{2,1,0:T(8,128)S(1)} %get-tuple-element.28.share, f32[6,64,128]{2,1,0:T(8,128)S(1)} %collective-permute-done.2.from_even, f32[6,64,128]{2,1,0:T(8,128)S(1)} %collective-permute-done.3.from_odd, f32[6,64,128]{2,1,0:T(8,128)S(1)} %get-tuple-element.32.straight_own, ...), custom_call_target="tpu_custom_call" | custom-call | tf_op jit(solution)/shard_map/imaging/pallas_call | solution.py:613
  38.4 2.4 %collective-permute-start.7 = (f32[6,64,128]{2,1,0:T(8,128)S(1)}, f32[6,64,128]{2,1,0:T(8,128)S(1)}, u32[]{:S(2)}, u32[]{:S(2)}) collective-permute-start(f32[6,64,128]{2,1,0:T(8,128)S(1)} %get-tuple-element.37.own), channel_id=1, source_target_pairs={{32,64},{64,32},{96,128},{128,96},{160,192},{192,160},{33,65},{65,... | collective-permute-start | bytes 589832 | tf_op jit(solution)/shard_map/ppermute | solution.py:682
  40.8 1.2 %collective-permute-start.6 = (f32[6,64,128]{2,1,0:T(8,128)S(1)}, f32[6,64,128]{2,1,0:T(8,128)S(1)}, u32[]{:S(2)}, u32[]{:S(2)}) collective-permute-start(f32[6,64,128]{2,1,0:T(8,128)S(1)} %get-tuple-element.37.own), channel_id=1, source_target_pairs={{0,32},{32,0},{64,96},{96,64},{128,160},{160,128},{192,224},{224,1... | collective-permute-start | bytes 589832 | tf_op jit(solution)/shard_map/ppermute | solution.py:682
  42.1 3.3 %collective-permute-done.7.odd_in = f32[6,64,128]{2,1,0:T(8,128)S(1)} collective-permute-done((f32[6,64,128]{2,1,0:T(8,128)S(1)}, f32[6,64,128]{2,1,0:T(8,128)S(1)}, u32[]{:S(2)}, u32[]{:S(2)}) %collective-permute-start.7) | collective-permute-done | bytes 196640 | tf_op jit(solution)/shard_map/ppermute | solution.py:682
  45.4 0.0 collective-permute-done.6.even_in
  45.4 0.2 collective-permute-start.8
  45.6 2.1 %collective-permute-start.9 = (f32[64,256]{1,0:T(8,128)S(1)}, f32[64,256]{1,0:T(8,128)S(1)}, u32[]{:S(2)}, u32[]{:S(2)}) collective-permute-start(f32[64,256]{1,0:T(8,128)S(1)} %get-tuple-element.39), channel_id=1, source_target_pairs={{2,4},{4,2},{6,8},{8,6},{10,12},{12,10},{14,16},{16,14},{18,20},{2... | collective-permute-start | bytes 196616 | tf_op jit(solution)/shard_map/ppermute | solution.py:682
  47.7 1.9 %inner_synthesis.1.partial = f32[1536,256]{1,0:T(8,128)} custom-call(f32[6,64,128]{2,1,0:T(8,128)S(1)} %get-tuple-element.37.own, f32[6,64,128]{2,1,0:T(8,128)S(1)} %collective-permute-done.6.even_in, f32[6,64,128]{2,1,0:T(8,128)S(1)} %collective-permute-done.7.odd_in, f32[1536,256]{1,0:T(8,128)S(1)} %copy-done.1, bf16[1024,128]{1,0:T(8,128)(2,1)S(1)} %copy-done.4), custom_call_target="tpu_custom_call" | custom-call | flops 1500000000 | bytes 2500000 | tf_op jit(solution)/shard_map/inner_synthesis/pallas_call | solution.py:636
  49.7 0.3 collective-permute-done.8.near_even
  50.0 4.0 %collective-permute-done.9.near_odd = f32[64,256]{1,0:T(8,128)S(1)} collective-permute-done((f32[64,256]{1,0:T(8,128)S(1)}, f32[64,256]{1,0:T(8,128)S(1)}, u32[]{:S(2)}, u32[]{:S(2)}) %collective-permute-start.9) | collective-permute-done | bytes 65568 | tf_op jit(solution)/shard_map/ppermute | solution.py:682
  54.0 1.5 %outer_synthesis.1 = f32[1536,256]{1,0:T(8,128)} custom-call(f32[6,64,128]{2,1,0:T(8,128)S(1)} %get-tuple-element.37.own, f32[6,64,128]{2,1,0:T(8,128)S(1)} %collective-permute-done.6.even_in, f32[6,64,128]{2,1,0:T(8,128)S(1)} %collective-permute-done.7.odd_in, f32[64,256]{1,0:T(8,128)S(1)} %collective-permute-done.8.near_even, ...), custom_call_target="tpu_custom_call", output_to_operand_aliasing={{}: (7, {})} | custom-call | tf_op jit(solution)/shard_map/outer_synthesis/pallas_call | solution.py:656
  (9 shorter events, 0.0 us)
Async XLA Ops:
  0.6 25.3 %copy-start.2 = (bf16[3840,128]{1,0:T(8,128)(2,1)S(1)}, bf16[3840,128]{1,0:T(8,128)(2,1)}, u32[]{:S(2)}) copy-start(bf16[3840,128]{1,0:T(8,128)(2,1)} %constant.7.clone.wide) | copy-start | bytes 2949124
  0.6 25.3 %copy-start = (s32[1536,256]{1,0:T(8,128)S(1)}, s32[1536,256]{1,0:T(8,128)}, u32[]{:S(2)}) copy-start(s32[1536,256]{1,0:T(8,128)} %target.1) | copy-start | bytes 4718596
  5.7 13.0 %collective-permute-start = (f32[64,256]{1,0:T(8,128)}, f32[64,256]{1,0:T(8,128)S(1)}, u32[]{:S(2)}, u32[]{:S(2)}) collective-permute-start(f32[64,256]{1,0:T(8,128)} %get-tuple-element.26), channel_id=1, source_target_pairs={{0,2},{2,0},{4,6},{6,4},{8,10},{10,8},{12,14},{14,12},{16,18},{18,... | collective-permute-start | bytes 196616 | tf_op jit(solution)/shard_map/ppermute | solution.py:682
  7.3 11.5 %collective-permute-start.1 = (f32[64,256]{1,0:T(8,128)}, f32[64,256]{1,0:T(8,128)S(1)}, u32[]{:S(2)}, u32[]{:S(2)}) collective-permute-start(f32[64,256]{1,0:T(8,128)} %get-tuple-element.27), channel_id=1, source_target_pairs={{2,4},{4,2},{6,8},{8,6},{10,12},{12,10},{14,16},{16,14},{18,20},{2... | collective-permute-start | bytes 196616 | tf_op jit(solution)/shard_map/ppermute | solution.py:682
  10.9 10.5 %collective-permute-start.4 = (f32[3,64,128]{2,1,0:T(8,128)}, f32[3,64,128]{2,1,0:T(8,128)S(1)}, u32[]{:S(2)}, u32[]{:S(2)}) collective-permute-start(f32[3,64,128]{2,1,0:T(8,128)} %get-tuple-element.34), channel_id=1, source_target_pairs={{0,25},{1,24},{2,27},{3,26},{4,29},{5,28},{6,31},{7,30},{8,17},{9,... | collective-permute-start | bytes 294920 | tf_op jit(solution)/shard_map/ppermute | solution.py:690
  17.7 1.0 %copy-start.3 = (f32[6,64,256]{2,1,0:T(8,128)S(1)}, f32[6,64,256]{2,1,0:T(8,128)}, u32[]{:S(2)}) copy-start(f32[6,64,256]{2,1,0:T(8,128)} %get-tuple-element.22.total) | copy-start | bytes 1179652
  18.8 5.0 %collective-permute-start.2 = (f32[6,64,128]{2,1,0:T(8,128)S(1)}, f32[6,64,128]{2,1,0:T(8,128)S(1)}, u32[]{:S(2)}, u32[]{:S(2)}) collective-permute-start(f32[6,64,128]{2,1,0:T(8,128)S(1)} %get-tuple-element.29), channel_id=1, source_target_pairs={{0,32},{32,0},{64,96},{96,64},{128,160},{160,128},{192,224},{224,1... | collective-permute-start | bytes 589832 | tf_op jit(solution)/shard_map/ppermute | solution.py:682
  18.9 7.0 %collective-permute-start.3 = (f32[6,64,128]{2,1,0:T(8,128)S(1)}, f32[6,64,128]{2,1,0:T(8,128)S(1)}, u32[]{:S(2)}, u32[]{:S(2)}) collective-permute-start(f32[6,64,128]{2,1,0:T(8,128)S(1)} %get-tuple-element.30), channel_id=1, source_target_pairs={{32,64},{64,32},{96,128},{128,96},{160,192},{192,160},{33,65},{65,... | collective-permute-start | bytes 589832 | tf_op jit(solution)/shard_map/ppermute | solution.py:682
  21.4 2.3 %collective-permute-start.5 = (f32[3,64,128]{2,1,0:T(8,128)S(1)}, f32[3,64,128]{2,1,0:T(8,128)S(1)}, u32[]{:S(2)}, u32[]{:S(2)}) collective-permute-start(f32[3,64,128]{2,1,0:T(8,128)S(1)} %collective-permute-done.4.mine), channel_id=1, source_target_pairs={{0,32},{32,0},{64,96},{96,64},{128,160},{160,128},{192,224},{224,1... | collective-permute-start | bytes 294920 | tf_op jit(solution)/shard_map/ppermute | solution.py:682
  22.6 0.9 %copy-start.5 = (f32[6,64,128]{2,1,0:T(8,128)S(1)}, f32[6,64,128]{2,1,0:T(8,128)}, u32[]{:S(2)}) copy-start(f32[6,64,128]{2,1,0:T(8,128)} %get-tuple-element.31.own) | copy-start | bytes 589828
  25.9 21.8 %copy-start.1 = (f32[1536,256]{1,0:T(8,128)S(1)}, f32[1536,256]{1,0:T(8,128)}, u32[]{:S(2)}) copy-start(f32[1536,256]{1,0:T(8,128)} %get-tuple-element.40.slope) | copy-start | bytes 4718596
  25.9 21.8 %copy-start.4 = (bf16[1024,128]{1,0:T(8,128)(2,1)S(1)}, bf16[1024,128]{1,0:T(8,128)(2,1)}, u32[]{:S(2)}) copy-start(bf16[1024,128]{1,0:T(8,128)(2,1)} %constant.8.clone.tables) | copy-start | bytes 786436
  38.4 7.0 %collective-permute-start.7 = (f32[6,64,128]{2,1,0:T(8,128)S(1)}, f32[6,64,128]{2,1,0:T(8,128)S(1)}, u32[]{:S(2)}, u32[]{:S(2)}) collective-permute-start(f32[6,64,128]{2,1,0:T(8,128)S(1)} %get-tuple-element.37.own), channel_id=1, source_target_pairs={{32,64},{64,32},{96,128},{128,96},{160,192},{192,160},{33,65},{65,... | collective-permute-start | bytes 589832 | tf_op jit(solution)/shard_map/ppermute | solution.py:682
  40.8 4.5 %collective-permute-start.6 = (f32[6,64,128]{2,1,0:T(8,128)S(1)}, f32[6,64,128]{2,1,0:T(8,128)S(1)}, u32[]{:S(2)}, u32[]{:S(2)}) collective-permute-start(f32[6,64,128]{2,1,0:T(8,128)S(1)} %get-tuple-element.37.own), channel_id=1, source_target_pairs={{0,32},{32,0},{64,96},{96,64},{128,160},{160,128},{192,224},{224,1... | collective-permute-start | bytes 589832 | tf_op jit(solution)/shard_map/ppermute | solution.py:682
  45.4 4.6 %collective-permute-start.8 = (f32[64,256]{1,0:T(8,128)S(1)}, f32[64,256]{1,0:T(8,128)S(1)}, u32[]{:S(2)}, u32[]{:S(2)}) collective-permute-start(f32[64,256]{1,0:T(8,128)S(1)} %get-tuple-element.38), channel_id=1, source_target_pairs={{0,2},{2,0},{4,6},{6,4},{8,10},{10,8},{12,14},{14,12},{16,18},{18,... | collective-permute-start | bytes 196616 | tf_op jit(solution)/shard_map/ppermute | solution.py:682
  45.6 8.3 %collective-permute-start.9 = (f32[64,256]{1,0:T(8,128)S(1)}, f32[64,256]{1,0:T(8,128)S(1)}, u32[]{:S(2)}, u32[]{:S(2)}) collective-permute-start(f32[64,256]{1,0:T(8,128)S(1)} %get-tuple-element.39), channel_id=1, source_target_pairs={{2,4},{4,2},{6,8},{8,6},{10,12},{12,10},{14,16},{16,14},{18,20},{2... | collective-permute-start | bytes 196616 | tf_op jit(solution)/shard_map/ppermute | solution.py:682

commit v8 on v6

--- a/solution.py
+++ b/solution.py
@@ -383,19 +383,23 @@
             for tile in tiles
             for i in range(count)
         ]
-        rows = times_table(jnp.concatenate(products, axis=0), wide_table(wide, SPREAD))
+        halves_of = []
+        for i in range(0, len(products), 2):
+            both = table_times(
+                wide_table(wide, LIFT)[:, :192], jnp.concatenate(products[i : i + 2], axis=1)
+            )
+            for j in (0, 1):
+                part = both[:, j * 2 * FB : (j + 1) * 2 * FB]
+                cosine, sine = part[:HALF], sign * swapped(part[HALF:])
+                halves_of += [cosine - sine, cosine + sine]
+        found = times_table(jnp.concatenate(halves_of, axis=0), wide_table(wide, SPREAD))
+        fields[group] = found
         for tile in tiles:
             total = jnp.zeros((COARSE, COARSE), jnp.float32)
             for i in range(count):
-                place = (tile * count + i) * FB
-                both = table_times(wide_table(wide, LIFT)[:, :192], rows[place : place + FB])
-                cosine, sine = both[:HALF], both[HALF:]
-                sine_re, sine_im = sine[:, :COARSE], sine[:, COARSE:]
-                cosine_re, cosine_im = cosine[:, :COARSE], cosine[:, COARSE:]
-                real = jnp.concatenate([cosine_re - sine_im, cosine_re + sine_im], axis=0)
-                imag = jnp.concatenate([cosine_im + sine_re, cosine_im - sine_re], axis=0)
-                fields[tile, group * count + i, :, :COARSE] = real
-                fields[tile, group * count + i, :, COARSE:] = imag
+                place = (tile * count + i) * COARSE
+                real = found[place : place + COARSE, :COARSE]
+                imag = found[place : place + COARSE, COARSE:]
                 total = total + (real * real + imag * imag)
             intensities[tile].append(total)
 
@@ -436,7 +440,8 @@
     adjoint = [[] for tile in tiles]
     for group in range(2):
         scaled = [
-            fields[tile, group * count + i] * scales[tile]
+            fields[group, (tile * count + i) * COARSE : (tile * count + i + 1) * COARSE, :]
+            * scales[tile]
             for tile in tiles
             for i in range(count)
         ]
@@ -646,7 +651,7 @@
         in_specs=[spectra] * 3 + [whole(own[0])] * 4 + [pixels, whole(tables)],
         out_specs=[pl.BlockSpec(memory_space=pl.ANY), spectra],
         scratch_shapes=[
-            pltpu.VMEM((TILES_AT_ONCE, kernels, COARSE, 2 * COARSE), jnp.float32),
+            pltpu.VMEM((2, TILES_AT_ONCE * kernels // 2 * COARSE, 2 * COARSE), jnp.float32),
             pltpu.VMEM((2, TILES_AT_ONCE * kernels // 2 * COARSE, 2 * FB), jnp.float32),
             pltpu.VMEM((TILES_AT_ONCE * TILE, TILE), jnp.float32),
             pltpu.SemaphoreType.DMA((TILES_AT_ONCE,)),

time: 54.1 us -> 53.7 us (level)
  no operation moved by 1% of the time
where the time goes in v8:
time: 53.7 us; the launch traced here: 53.4 us
  starting transfers between devices  21.7 us (40%)
  Pallas kernels  19.2 us (36%)
  waiting for transfers between devices  9.71 us (18%)
  local copies, waits for them, and re-layouts  1.94 us (4%)
  between operations  0.81 us (2%)
    ppermute x9, starting transfers between devices, swap(): return lax.ppermute(value, axis, swap_pairs(lax.axis_size(axis), first))  14.9 us
    pallas_call x1, Pallas kernels, imaging(): pl.pallas_call(imaging_kernel, grid=(tiles // TILES_AT_ONCE,), out_shape=...  10.3 us
    ppermute x9, waiting for transfers between devices, swap(): return lax.ppermute(value, axis, swap_pairs(lax.axis_size(axis), first))  9.7 us
    ppermute x1, starting transfers between devices, local(): mine = lax.ppermute(half, ('gy', 'ka'), pairs)  6.83 us
    pallas_call x1, Pallas kernels, analysis(): pl.pallas_call(analysis_kernel, grid=(tiles // PAIR,), out_shape=(total,...  5.07 us
    pallas_call x1, Pallas kernels, inner_synthesis(): pl.pallas_call(inner_kernel, out_shape=jax.ShapeDtypeStruct(slope.shape,...  1.95 us
    unnamed x12, local copies, waits for them, and re-layouts  1.94 us
    pallas_call x1, Pallas kernels, outer_synthesis(): pl.pallas_call(outer_kernel, out_shape=jax.ShapeDtypeStruct(slope.shape,...  1.51 us
  transfers between devices with their start and end apart: 10, of which 4 were waited for; matrix products, arithmetic and copies ran while one was open for 0% of the time, Pallas kernels for 4%

profile of v8, /device:TPU:40, one launch (start us, length us, event | category | flops | bytes accessed | tf_op | source)
XLA Modules:
  0.0 53.4 jit_solution(13170403568981771349)
XLA Ops:
  0.6 0.0 copy-start.2
  0.7 5.1 %analysis.1 = (f32[6,64,256]{2,1,0:T(8,128)}, f32[6,64,128]{2,1,0:T(8,128)}, f32[3,64,128]{2,1,0:T(8,128)}, f32[64,256]{1,0:T(8,128)}, f32[64,256]{1,0:T(8,128)}, /*index=5*/f32[1536,256]{1,0:T(8,128)}) custom-call(f32[1536,256]{1,0:T(8,128)} %mask_in.1, f32[6,2,4096]{2,1,0:T(2,128)} %kernels_in.1, f32[6]{0:T(128)} %weights.1, ...), custom_call_target="tpu_custom_call" | custom-call | tf_op jit(solution)/shard_map/analysis/pallas_call | solution.py:572
  5.7 1.6 %collective-permute-start = (f32[64,256]{1,0:T(8,128)}, f32[64,256]{1,0:T(8,128)S(1)}, u32[]{:S(2)}, u32[]{:S(2)}) collective-permute-start(f32[64,256]{1,0:T(8,128)} %get-tuple-element.26), channel_id=1, source_target_pairs={{0,2},{2,0},{4,6},{6,4},{8,10},{10,8},{12,14},{14,12},{16,18},{18,... | collective-permute-start | bytes 196616 | tf_op jit(solution)/shard_map/ppermute | solution.py:713
  7.3 3.5 %collective-permute-start.1 = (f32[64,256]{1,0:T(8,128)}, f32[64,256]{1,0:T(8,128)S(1)}, u32[]{:S(2)}, u32[]{:S(2)}) collective-permute-start(f32[64,256]{1,0:T(8,128)} %get-tuple-element.27), channel_id=1, source_target_pairs={{2,4},{4,2},{6,8},{8,6},{10,12},{12,10},{14,16},{16,14},{18,20},{2... | collective-permute-start | bytes 196616 | tf_op jit(solution)/shard_map/ppermute | solution.py:713
  10.9 6.8 %collective-permute-start.4 = (f32[3,64,128]{2,1,0:T(8,128)}, f32[3,64,128]{2,1,0:T(8,128)S(1)}, u32[]{:S(2)}, u32[]{:S(2)}) collective-permute-start(f32[3,64,128]{2,1,0:T(8,128)} %get-tuple-element.34), channel_id=1, source_target_pairs={{0,25},{1,24},{2,27},{3,26},{4,29},{5,28},{6,31},{7,30},{8,17},{9,... | collective-permute-start | bytes 294920 | tf_op jit(solution)/shard_map/ppermute | solution.py:721
  17.7 1.0 %copy-done.3 = f32[6,64,256]{2,1,0:T(8,128)S(1)} copy-done((f32[6,64,256]{2,1,0:T(8,128)S(1)}, f32[6,64,256]{2,1,0:T(8,128)}, u32[]{:S(2)}) %copy-start.3) | copy-done | bytes 393240
  18.7 0.1 shares.1
  18.7 0.0 collective-permute-done.near_even
  18.8 0.0 collective-permute-done.1.near_odd
  18.8 0.1 merge.1
  18.8 0.1 collective-permute-start.2
  18.9 2.4 %collective-permute-start.3 = (f32[6,64,128]{2,1,0:T(8,128)S(1)}, f32[6,64,128]{2,1,0:T(8,128)S(1)}, u32[]{:S(2)}, u32[]{:S(2)}) collective-permute-start(f32[6,64,128]{2,1,0:T(8,128)S(1)} %get-tuple-element.30), channel_id=1, source_target_pairs={{32,64},{64,32},{96,128},{128,96},{160,192},{192,160},{33,65},{65,... | collective-permute-start | bytes 589832 | tf_op jit(solution)/shard_map/ppermute | solution.py:713
  21.4 0.0 collective-permute-done.4.mine
  21.4 1.2 %collective-permute-start.5 = (f32[3,64,128]{2,1,0:T(8,128)S(1)}, f32[3,64,128]{2,1,0:T(8,128)S(1)}, u32[]{:S(2)}, u32[]{:S(2)}) collective-permute-start(f32[3,64,128]{2,1,0:T(8,128)S(1)} %collective-permute-done.4.mine), channel_id=1, source_target_pairs={{0,32},{32,0},{64,96},{96,64},{128,160},{160,128},{192,224},{224,1... | collective-permute-start | bytes 294920 | tf_op jit(solution)/shard_map/ppermute | solution.py:713
  22.6 0.9 %copy-done.5 = f32[6,64,128]{2,1,0:T(8,128)S(1)} copy-done((f32[6,64,128]{2,1,0:T(8,128)S(1)}, f32[6,64,128]{2,1,0:T(8,128)}, u32[]{:S(2)}) %copy-start.5) | copy-done | bytes 196632
  23.6 0.1 prepare_own.1
  23.7 0.0 collective-permute-done.5.partners
  23.7 0.1 prepare_other.1
  23.8 0.0 collective-permute-done.2.from_even
  23.8 2.1 %collective-permute-done.3.from_odd = f32[6,64,128]{2,1,0:T(8,128)S(1)} collective-permute-done((f32[6,64,128]{2,1,0:T(8,128)S(1)}, f32[6,64,128]{2,1,0:T(8,128)S(1)}, u32[]{:S(2)}, u32[]{:S(2)}) %collective-permute-start.3) | collective-permute-done | bytes 196640 | tf_op jit(solution)/shard_map/ppermute | solution.py:713
  25.9 10.3 %imaging.1 = (f32[1536,256]{1,0:T(8,128)}, f32[6,64,128]{2,1,0:T(8,128)S(1)}) custom-call(f32[6,64,128]{2,1,0:T(8,128)S(1)} %get-tuple-element.28.share, f32[6,64,128]{2,1,0:T(8,128)S(1)} %collective-permute-done.2.from_even, f32[6,64,128]{2,1,0:T(8,128)S(1)} %collective-permute-done.3.from_odd, f32[6,64,128]{2,1,0:T(8,128)S(1)} %get-tuple-element.32.straight_own, ...), custom_call_target="tpu_custom_call" | custom-call | tf_op jit(solution)/shard_map/imaging/pallas_call | solution.py:644
  36.3 2.4 %collective-permute-start.7 = (f32[6,64,128]{2,1,0:T(8,128)S(1)}, f32[6,64,128]{2,1,0:T(8,128)S(1)}, u32[]{:S(2)}, u32[]{:S(2)}) collective-permute-start(f32[6,64,128]{2,1,0:T(8,128)S(1)} %get-tuple-element.37.own), channel_id=1, source_target_pairs={{32,64},{64,32},{96,128},{128,96},{160,192},{192,160},{33,65},{65,... | collective-permute-start | bytes 589832 | tf_op jit(solution)/shard_map/ppermute | solution.py:713
  38.7 1.2 %collective-permute-start.6 = (f32[6,64,128]{2,1,0:T(8,128)S(1)}, f32[6,64,128]{2,1,0:T(8,128)S(1)}, u32[]{:S(2)}, u32[]{:S(2)}) collective-permute-start(f32[6,64,128]{2,1,0:T(8,128)S(1)} %get-tuple-element.37.own), channel_id=1, source_target_pairs={{0,32},{32,0},{64,96},{96,64},{128,160},{160,128},{192,224},{224,1... | collective-permute-start | bytes 589832 | tf_op jit(solution)/shard_map/ppermute | solution.py:713
  39.9 3.3 %collective-permute-done.7.odd_in = f32[6,64,128]{2,1,0:T(8,128)S(1)} collective-permute-done((f32[6,64,128]{2,1,0:T(8,128)S(1)}, f32[6,64,128]{2,1,0:T(8,128)S(1)}, u32[]{:S(2)}, u32[]{:S(2)}) %collective-permute-start.7) | collective-permute-done | bytes 196640 | tf_op jit(solution)/shard_map/ppermute | solution.py:713
  43.2 0.0 collective-permute-done.6.even_in
  43.3 0.2 collective-permute-start.8
  43.5 2.1 %collective-permute-start.9 = (f32[64,256]{1,0:T(8,128)S(1)}, f32[64,256]{1,0:T(8,128)S(1)}, u32[]{:S(2)}, u32[]{:S(2)}) collective-permute-start(f32[64,256]{1,0:T(8,128)S(1)} %get-tuple-element.39), channel_id=1, source_target_pairs={{2,4},{4,2},{6,8},{8,6},{10,12},{12,10},{14,16},{16,14},{18,20},{2... | collective-permute-start | bytes 196616 | tf_op jit(solution)/shard_map/ppermute | solution.py:713
  45.6 0.0 copy-done.1
  45.6 1.9 %inner_synthesis.1.partial = f32[1536,256]{1,0:T(8,128)} custom-call(f32[6,64,128]{2,1,0:T(8,128)S(1)} %get-tuple-element.37.own, f32[6,64,128]{2,1,0:T(8,128)S(1)} %collective-permute-done.6.even_in, f32[6,64,128]{2,1,0:T(8,128)S(1)} %collective-permute-done.7.odd_in, f32[1536,256]{1,0:T(8,128)S(1)} %copy-done.1, bf16[1024,128]{1,0:T(8,128)(2,1)S(1)} %copy-done.4), custom_call_target="tpu_custom_call" | custom-call | flops 1500000000 | bytes 2500000 | tf_op jit(solution)/shard_map/inner_synthesis/pallas_call | solution.py:667
  47.6 0.3 collective-permute-done.8.near_even
  47.9 4.0 %collective-permute-done.9.near_odd = f32[64,256]{1,0:T(8,128)S(1)} collective-permute-done((f32[64,256]{1,0:T(8,128)S(1)}, f32[64,256]{1,0:T(8,128)S(1)}, u32[]{:S(2)}, u32[]{:S(2)}) %collective-permute-start.9) | collective-permute-done | bytes 65568 | tf_op jit(solution)/shard_map/ppermute | solution.py:713
  51.9 1.5 %outer_synthesis.1 = f32[1536,256]{1,0:T(8,128)} custom-call(f32[6,64,128]{2,1,0:T(8,128)S(1)} %get-tuple-element.37.own, f32[6,64,128]{2,1,0:T(8,128)S(1)} %collective-permute-done.6.even_in, f32[6,64,128]{2,1,0:T(8,128)S(1)} %collective-permute-done.7.odd_in, f32[64,256]{1,0:T(8,128)S(1)} %collective-permute-done.8.near_even, ...), custom_call_target="tpu_custom_call", output_to_operand_aliasing={{}: (7, {})} | custom-call | tf_op jit(solution)/shard_map/outer_synthesis/pallas_call | solution.py:687
  (9 shorter events, 0.0 us)
Async XLA Ops:
  0.6 25.3 %copy-start.2 = (bf16[4608,128]{1,0:T(8,128)(2,1)S(1)}, bf16[4608,128]{1,0:T(8,128)(2,1)}, u32[]{:S(2)}) copy-start(bf16[4608,128]{1,0:T(8,128)(2,1)} %constant.7.clone.wide) | copy-start | bytes 3538948
  0.6 25.3 %copy-start = (s32[1536,256]{1,0:T(8,128)S(1)}, s32[1536,256]{1,0:T(8,128)}, u32[]{:S(2)}) copy-start(s32[1536,256]{1,0:T(8,128)} %target.1) | copy-start | bytes 4718596
  5.7 13.0 %collective-permute-start = (f32[64,256]{1,0:T(8,128)}, f32[64,256]{1,0:T(8,128)S(1)}, u32[]{:S(2)}, u32[]{:S(2)}) collective-permute-start(f32[64,256]{1,0:T(8,128)} %get-tuple-element.26), channel_id=1, source_target_pairs={{0,2},{2,0},{4,6},{6,4},{8,10},{10,8},{12,14},{14,12},{16,18},{18,... | collective-permute-start | bytes 196616 | tf_op jit(solution)/shard_map/ppermute | solution.py:713
  7.3 11.5 %collective-permute-start.1 = (f32[64,256]{1,0:T(8,128)}, f32[64,256]{1,0:T(8,128)S(1)}, u32[]{:S(2)}, u32[]{:S(2)}) collective-permute-start(f32[64,256]{1,0:T(8,128)} %get-tuple-element.27), channel_id=1, source_target_pairs={{2,4},{4,2},{6,8},{8,6},{10,12},{12,10},{14,16},{16,14},{18,20},{2... | collective-permute-start | bytes 196616 | tf_op jit(solution)/shard_map/ppermute | solution.py:713
  10.9 10.5 %collective-permute-start.4 = (f32[3,64,128]{2,1,0:T(8,128)}, f32[3,64,128]{2,1,0:T(8,128)S(1)}, u32[]{:S(2)}, u32[]{:S(2)}) collective-permute-start(f32[3,64,128]{2,1,0:T(8,128)} %get-tuple-element.34), channel_id=1, source_target_pairs={{0,25},{1,24},{2,27},{3,26},{4,29},{5,28},{6,31},{7,30},{8,17},{9,... | collective-permute-start | bytes 294920 | tf_op jit(solution)/shard_map/ppermute | solution.py:721
  17.7 1.0 %copy-start.3 = (f32[6,64,256]{2,1,0:T(8,128)S(1)}, f32[6,64,256]{2,1,0:T(8,128)}, u32[]{:S(2)}) copy-start(f32[6,64,256]{2,1,0:T(8,128)} %get-tuple-element.22.total) | copy-start | bytes 1179652
  18.8 5.0 %collective-permute-start.2 = (f32[6,64,128]{2,1,0:T(8,128)S(1)}, f32[6,64,128]{2,1,0:T(8,128)S(1)}, u32[]{:S(2)}, u32[]{:S(2)}) collective-permute-start(f32[6,64,128]{2,1,0:T(8,128)S(1)} %get-tuple-element.29), channel_id=1, source_target_pairs={{0,32},{32,0},{64,96},{96,64},{128,160},{160,128},{192,224},{224,1... | collective-permute-start | bytes 589832 | tf_op jit(solution)/shard_map/ppermute | solution.py:713
  18.9 7.0 %collective-permute-start.3 = (f32[6,64,128]{2,1,0:T(8,128)S(1)}, f32[6,64,128]{2,1,0:T(8,128)S(1)}, u32[]{:S(2)}, u32[]{:S(2)}) collective-permute-start(f32[6,64,128]{2,1,0:T(8,128)S(1)} %get-tuple-element.30), channel_id=1, source_target_pairs={{32,64},{64,32},{96,128},{128,96},{160,192},{192,160},{33,65},{65,... | collective-permute-start | bytes 589832 | tf_op jit(solution)/shard_map/ppermute | solution.py:713
  21.4 2.3 %collective-permute-start.5 = (f32[3,64,128]{2,1,0:T(8,128)S(1)}, f32[3,64,128]{2,1,0:T(8,128)S(1)}, u32[]{:S(2)}, u32[]{:S(2)}) collective-permute-start(f32[3,64,128]{2,1,0:T(8,128)S(1)} %collective-permute-done.4.mine), channel_id=1, source_target_pairs={{0,32},{32,0},{64,96},{96,64},{128,160},{160,128},{192,224},{224,1... | collective-permute-start | bytes 294920 | tf_op jit(solution)/shard_map/ppermute | solution.py:713
  22.6 0.9 %copy-start.5 = (f32[6,64,128]{2,1,0:T(8,128)S(1)}, f32[6,64,128]{2,1,0:T(8,128)}, u32[]{:S(2)}) copy-start(f32[6,64,128]{2,1,0:T(8,128)} %get-tuple-element.31.own) | copy-start | bytes 589828
  25.9 19.7 %copy-start.1 = (f32[1536,256]{1,0:T(8,128)S(1)}, f32[1536,256]{1,0:T(8,128)}, u32[]{:S(2)}) copy-start(f32[1536,256]{1,0:T(8,128)} %get-tuple-element.40.slope) | copy-start | bytes 4718596
  25.9 19.7 %copy-start.4 = (bf16[1024,128]{1,0:T(8,128)(2,1)S(1)}, bf16[1024,128]{1,0:T(8,128)(2,1)}, u32[]{:S(2)}) copy-start(bf16[1024,128]{1,0:T(8,128)(2,1)} %constant.8.clone.tables) | copy-start | bytes 786436
  36.3 7.0 %collective-permute-start.7 = (f32[6,64,128]{2,1,0:T(8,128)S(1)}, f32[6,64,128]{2,1,0:T(8,128)S(1)}, u32[]{:S(2)}, u32[]{:S(2)}) collective-permute-start(f32[6,64,128]{2,1,0:T(8,128)S(1)} %get-tuple-element.37.own), channel_id=1, source_target_pairs={{32,64},{64,32},{96,128},{128,96},{160,192},{192,160},{33,65},{65,... | collective-permute-start | bytes 589832 | tf_op jit(solution)/shard_map/ppermute | solution.py:713
  38.7 4.5 %collective-permute-start.6 = (f32[6,64,128]{2,1,0:T(8,128)S(1)}, f32[6,64,128]{2,1,0:T(8,128)S(1)}, u32[]{:S(2)}, u32[]{:S(2)}) collective-permute-start(f32[6,64,128]{2,1,0:T(8,128)S(1)} %get-tuple-element.37.own), channel_id=1, source_target_pairs={{0,32},{32,0},{64,96},{96,64},{128,160},{160,128},{192,224},{224,1... | collective-permute-start | bytes 589832 | tf_op jit(solution)/shard_map/ppermute | solution.py:713
  43.3 4.6 %collective-permute-start.8 = (f32[64,256]{1,0:T(8,128)S(1)}, f32[64,256]{1,0:T(8,128)S(1)}, u32[]{:S(2)}, u32[]{:S(2)}) collective-permute-start(f32[64,256]{1,0:T(8,128)S(1)} %get-tuple-element.38), channel_id=1, source_target_pairs={{0,2},{2,0},{4,6},{6,4},{8,10},{10,8},{12,14},{14,12},{16,18},{18,... | collective-permute-start | bytes 196616 | tf_op jit(solution)/shard_map/ppermute | solution.py:713
  43.5 8.3 %collective-permute-start.9 = (f32[64,256]{1,0:T(8,128)S(1)}, f32[64,256]{1,0:T(8,128)S(1)}, u32[]{:S(2)}, u32[]{:S(2)}) collective-permute-start(f32[64,256]{1,0:T(8,128)S(1)} %get-tuple-element.39), channel_id=1, source_target_pairs={{2,4},{4,2},{6,8},{8,6},{10,12},{12,10},{14,16},{16,14},{18,20},{2... | collective-permute-start | bytes 196616 | tf_op jit(solution)/shard_map/ppermute | solution.py:713

commit v9 on v6

--- a/solution.py
+++ b/solution.py
@@ -286,11 +286,11 @@
 
 def analysis_kernel(
     mask_in, kernels_in, weights, tables_in,
-    total, packed, half, edge_even, edge_odd, slope,
+    total, packed, half, edge_odd, slope,
     real, imag, sums, mask, kernels, tables, semaphores,
 ):
     step = pl.program_id(0)
-    count = total.shape[0]
+    count = total.shape[0] - 2
 
     def pixels_copy(step):
         place = pl.ds(pl.multiple_of(step * PAIR * TILE, TILE), PAIR * TILE)
@@ -331,17 +331,15 @@
 
     @pl.when(step == pl.num_programs(0) - 1)
     def _():
-        total[...] = sums[1 : count + 1]
-        up, down = sums[0], sums[count + 1]
-        odd_row = is_odd("gy")
-        edge_even[...] = jnp.where(odd_row, up, down)
-        edge_odd[...] = jnp.where(odd_row, down, up)
-
-
-def shares_kernel(total, share, to_even, to_odd):
+        total[...] = sums[...]
+        edge_odd[...] = jnp.where(is_odd("gy"), sums[count + 1], sums[0])
+
+
+def shares_kernel(total, share, to_even, to_odd, edge):
     odd_col = is_odd("gx")
+    edge[...] = jnp.where(is_odd("gy"), total[0], total[share.shape[0] + 1])
     for index in range(share.shape[0]):
-        left, right = total[index, :, : 2 * FB], total[index, :, 2 * FB :]
+        left, right = total[index + 1, :, : 2 * FB], total[index + 1, :, 2 * FB :]
         share[index] = parity((FB, 2 * FB)) * (left + right)
         to_even[index] = jnp.where(odd_col, left, right)
         to_odd[index] = jnp.where(odd_col, right, left)
@@ -373,34 +371,34 @@
     copies = []
     sign = jnp.where(low_lanes((HALF, 2 * FB)), 1.0, -1.0)
     tiles = range(share.shape[0])
-    intensities = [[] for tile in tiles]
 
     spectra = [share[tile] + from_even[tile] + from_odd[tile] for tile in tiles]
     turned = [swapped(spectrum) for spectrum in spectra]
-    for group in range(2):
-        products = [
-            straights[group][i] * spectra[tile] + crosseds[group][i] * turned[tile]
-            for tile in tiles
-            for i in range(count)
-        ]
-        rows = times_table(jnp.concatenate(products, axis=0), wide_table(wide, SPREAD))
-        for tile in tiles:
-            total = jnp.zeros((COARSE, COARSE), jnp.float32)
-            for i in range(count):
-                place = (tile * count + i) * FB
-                both = table_times(wide_table(wide, LIFT)[:, :192], rows[place : place + FB])
-                cosine, sine = both[:HALF], both[HALF:]
-                sine_re, sine_im = sine[:, :COARSE], sine[:, COARSE:]
-                cosine_re, cosine_im = cosine[:, :COARSE], cosine[:, COARSE:]
-                real = jnp.concatenate([cosine_re - sine_im, cosine_re + sine_im], axis=0)
-                imag = jnp.concatenate([cosine_im + sine_re, cosine_im - sine_re], axis=0)
-                fields[tile, group * count + i, :, :COARSE] = real
-                fields[tile, group * count + i, :, COARSE:] = imag
-                total = total + (real * real + imag * imag)
-            intensities[tile].append(total)
+    order = [(group, tile, i) for group in range(2) for tile in tiles for i in range(count)]
+    products = [
+        straights[group][i] * spectra[tile] + crosseds[group][i] * turned[tile]
+        for group, tile, i in order
+    ]
+    halves_of = []
+    for i in range(0, len(products), 2):
+        both = table_times(
+            wide_table(wide, LIFT)[:, :192], jnp.concatenate(products[i : i + 2], axis=1)
+        )
+        for j in (0, 1):
+            part = both[:, j * 2 * FB : (j + 1) * 2 * FB]
+            cosine, sine = part[:HALF], sign * swapped(part[HALF:])
+            halves_of += [cosine - sine, cosine + sine]
+    found = times_table(jnp.concatenate(halves_of, axis=0), wide_table(wide, SPREAD))
+    fields[...] = found
+    totals = {}
+    for place, (group, tile, i) in enumerate(order):
+        real = found[place * COARSE : (place + 1) * COARSE, :COARSE]
+        imag = found[place * COARSE : (place + 1) * COARSE, COARSE:]
+        power = real * real + imag * imag
+        totals[group, tile] = power if i == 0 else totals[group, tile] + power
 
     half_fine = times_table(
-        jnp.concatenate([first + second for first, second in intensities], axis=0),
+        jnp.concatenate([totals[0, tile] + totals[1, tile] for tile in tiles], axis=0),
         wide_table(wide, FINE_RIGHT),
     )
     half_coarse = []
@@ -433,38 +431,26 @@
         for tile in tiles
     ]
 
-    adjoint = [[] for tile in tiles]
-    for group in range(2):
-        scaled = [
-            fields[tile, group * count + i] * scales[tile]
-            for tile in tiles
-            for i in range(count)
-        ]
-        sides[group] = times_paired(
-            jnp.concatenate(scaled, axis=0), wide_table(wide, GATHER)
-        )
-        for tile in tiles:
-            total = jnp.zeros((FB, 2 * FB), jnp.float32)
-            for i in range(0, count, 2):
-                pair = []
-                for j in (i, i + 1):
-                    place = (tile * count + j) * COARSE
-                    plus = sides[group, place : place + HALF, :]
-                    minus = sides[group, place + HALF : place + COARSE, :]
-                    pair.append(
-                        jnp.concatenate([plus + minus, sign * swapped(plus - minus)], axis=0)
-                    )
-                found = stacked_times(
-                    wide_table(wide, FOLD), jnp.concatenate(pair, axis=1)
-                )
-                for j in (0, 1):
-                    part = found[:, j * 2 * FB : (j + 1) * 2 * FB]
-                    total = total + (
-                        straights[group][i + j] * part - crosseds[group][i + j] * swapped(part)
-                    )
-            adjoint[tile].append(total)
+    scaled = [
+        fields[place * COARSE : (place + 1) * COARSE, :] * scales[tile]
+        for place, (group, tile, i) in enumerate(order)
+    ]
+    sides[...] = times_paired(jnp.concatenate(scaled, axis=0), wide_table(wide, GATHER))
+    adjoint = {}
+    for place in range(0, len(order), 2):
+        pair = []
+        for j in (place, place + 1):
+            plus = sides[j * COARSE : j * COARSE + HALF, :]
+            minus = sides[j * COARSE + HALF : (j + 1) * COARSE, :]
+            pair.append(jnp.concatenate([plus + minus, sign * swapped(plus - minus)], axis=0))
+        found = stacked_times(wide_table(wide, FOLD), jnp.concatenate(pair, axis=1))
+        for j in (0, 1):
+            group, tile, i = order[place + j]
+            part = found[:, j * 2 * FB : (j + 1) * 2 * FB]
+            term = straights[group][i] * part - crosseds[group][i] * swapped(part)
+            adjoint[group, tile] = term if i == 0 else adjoint[group, tile] + term
     for tile in tiles:
-        grad[tile] = adjoint[tile][0] + adjoint[tile][1]
+        grad[tile] = adjoint[0, tile] + adjoint[1, tile]
 
     for copy in copies:
         copy.wait()
@@ -498,12 +484,17 @@
     return jnp.concatenate([base + from_left, base + from_right], axis=1)
 
 
-def edges_kernel(own, even_in, odd_in, side_even, side_odd):
+def odd_edge_kernel(own, even_in, odd_in, side):
     first = mixed_row(own, even_in, odd_in, 0)
     last = mixed_row(own, even_in, odd_in, own.shape[0] - 1)
-    odd_row = is_odd("gy")
-    side_even[...] = jnp.where(odd_row, first, last)
-    side_odd[...] = jnp.where(odd_row, last, first)
+    side[...] = jnp.where(is_odd("gy"), last, first)
+
+
+def even_edge_kernel(own, even_in, odd_in, before, side):
+    del before
+    first = mixed_row(own, even_in, odd_in, 0)
+    last = mixed_row(own, even_in, odd_in, own.shape[0] - 1)
+    side[...] = jnp.where(is_odd("gy"), first, last)
 
 
 def write_rows(values, result, first, buffer, semaphore):
@@ -560,7 +551,7 @@
     tiles = mask.shape[0] // TILE
     tables = jnp.asarray(TABLES["analysis"])
     part = pltpu.VMEM((FB // 2, 2 * FB), jnp.float32)
-    total = jax.ShapeDtypeStruct((tiles, FB, 4 * FB), jnp.float32)
+    total = jax.ShapeDtypeStruct((tiles + 2, FB, 4 * FB), jnp.float32)
     packed = jax.ShapeDtypeStruct((kernels.shape[0], FB, 2 * FB), jnp.float32)
     half = jax.ShapeDtypeStruct((kernels.shape[0] // 2, FB, 2 * FB), jnp.float32)
     edge = jax.ShapeDtypeStruct((FB, 4 * FB), jnp.float32)
@@ -568,7 +559,7 @@
         analysis_kernel,
         grid=(tiles // PAIR,),
         out_shape=(
-            total, packed, half, edge, edge, jax.ShapeDtypeStruct(mask.shape, jnp.float32)
+            total, packed, half, edge, jax.ShapeDtypeStruct(mask.shape, jnp.float32)
         ),
         in_specs=[
             pl.BlockSpec(memory_space=pltpu.HBM),
@@ -576,7 +567,7 @@
             pl.BlockSpec(memory_space=pltpu.SMEM),
             pl.BlockSpec(memory_space=pltpu.HBM),
         ],
-        out_specs=[whole(out) for out in (total, packed, half, edge, edge)] + [tile_pair()],
+        out_specs=[whole(out) for out in (total, packed, half, edge)] + [tile_pair()],
         scratch_shapes=[
             part,
             part,
@@ -604,8 +595,9 @@
 
 
 def shares(total):
-    spectra = jax.ShapeDtypeStruct((total.shape[0], FB, 2 * FB), jnp.float32)
-    return simple_call(shares_kernel, (spectra,) * 3, total, name="shares")
+    spectra = jax.ShapeDtypeStruct((total.shape[0] - 2, FB, 2 * FB), jnp.float32)
+    side = jax.ShapeDtypeStruct((FB, 4 * FB), jnp.float32)
+    return simple_call(shares_kernel, (spectra,) * 3 + (side,), total, name="shares")
 
 
 def merge(share, to_even, to_odd, near_even, near_odd):
@@ -615,9 +607,16 @@
     )
 
 
-def edges(grad, grad_even, grad_odd):
+def odd_edge(grad, grad_even, grad_odd):
     side = jax.ShapeDtypeStruct((FB, 4 * FB), jnp.float32)
-    return simple_call(edges_kernel, (side,) * 2, grad, grad_even, grad_odd, name="edges")
+    return simple_call(odd_edge_kernel, (side,), grad, grad_even, grad_odd, name="odd_edge")[0]
+
+
+def even_edge(grad, grad_even, grad_odd, before):
+    side = jax.ShapeDtypeStruct((FB, 4 * FB), jnp.float32)
+    return simple_call(
+        even_edge_kernel, (side,), grad, grad_even, grad_odd, before, name="even_edge"
+    )[0]
 
 
 def prepare_own(own):
@@ -646,8 +645,8 @@
         in_specs=[spectra] * 3 + [whole(own[0])] * 4 + [pixels, whole(tables)],
         out_specs=[pl.BlockSpec(memory_space=pl.ANY), spectra],
         scratch_shapes=[
-            pltpu.VMEM((TILES_AT_ONCE, kernels, COARSE, 2 * COARSE), jnp.float32),
-            pltpu.VMEM((2, TILES_AT_ONCE * kernels // 2 * COARSE, 2 * FB), jnp.float32),
+            pltpu.VMEM((TILES_AT_ONCE * kernels * COARSE, 2 * COARSE), jnp.float32),
+            pltpu.VMEM((TILES_AT_ONCE * kernels * COARSE, 2 * FB), jnp.float32),
             pltpu.VMEM((TILES_AT_ONCE * TILE, TILE), jnp.float32),
             pltpu.SemaphoreType.DMA((TILES_AT_ONCE,)),
         ],
@@ -707,7 +706,7 @@
     def swap(value, axis, first):
         return lax.ppermute(value, axis, swap_pairs(lax.axis_size(axis), first))
 
-    total, packed, half, edge_even, edge_odd, slope = analysis(mask_param, kernels, weights)
+    total, packed, half, edge_odd, slope = analysis(mask_param, kernels, weights)
     inner = rows // 4
     pairs = []
     for place in range(rows):
@@ -715,8 +714,9 @@
         pairs += [(2 * place, 2 * mirror + 1), (2 * place + 1, 2 * mirror)]
     mine = lax.ppermute(half, ("gy", "ka"), pairs)
     halo_odd = swap(edge_odd, "gy", 1)
+    *sums, edge_even = shares(total)
     halo_even = swap(edge_even, "gy", 0)
-    share, to_even, to_odd = merge(*shares(total), halo_even, halo_odd)
+    share, to_even, to_odd = merge(*sums, halo_even, halo_odd)
     from_odd = swap(to_odd, "gx", 1)
     from_even = swap(to_even, "gx", 0)
     own = prepare_own(packed)
@@ -725,8 +725,9 @@
     resist, grad = imaging(share, from_even, from_odd, own, other, target)
     grad_odd = swap(grad, "gx", 1)
     grad_even = swap(grad, "gx", 0)
-    side_even, side_odd = edges(grad, grad_even, grad_odd)
+    side_odd = odd_edge(grad, grad_even, grad_odd)
     near_odd = swap(side_odd, "gy", 1)
+    side_even = even_edge(grad, grad_even, grad_odd, side_odd)
     near_even = swap(side_even, "gy", 0)
     partial = inner_synthesis(grad, grad_even, grad_odd, slope)
     gradient = outer_synthesis(

time: 54.1 us -> 57.6 us (1.065)
  Pallas kernels: 19.7 us -> 24.1 us
  waiting for transfers between devices: 9.7 us -> 8.18 us
  starting transfers between devices: 21.7 us -> 22.3 us
    pallas_call x1, Pallas kernels: 10.8 us -> 15.2 us  [imaging(): pl.pallas_call(imaging_kernel, grid=(tiles // TILES_AT_ONCE,), out_shape=...]
    ppermute x9, waiting for transfers between devices: 9.7 us -> 7.93 us  [swap(): return lax.ppermute(value, axis, swap_pairs(lax.axis_size(axis), first))]
    ppermute x9, starting transfers between devices: 14.9 us -> 16.1 us  [swap(): return lax.ppermute(value, axis, swap_pairs(lax.axis_size(axis), first))]
    ppermute x1, starting transfers between devices: 6.83 us -> 6.17 us  [local(): mine = lax.ppermute(half, ('gy', 'ka'), pairs)]
  transfers between devices with their start and end apart: 10 -> 10, of which waited for: 4 -> 5; matrix products, arithmetic and copies ran while one was open for 0% -> 0% of each run, Pallas kernels for 4% -> 4%
where the time goes in v9:
time: 57.6 us; the launch traced here: 57.4 us
  Pallas kernels  24.1 us (42%)
  starting transfers between devices  22.3 us (39%)
  waiting for transfers between devices  8.18 us (14%)
  local copies, waits for them, and re-layouts  1.98 us (3%)
  between operations  0.79 us (1%)
    ppermute x9, starting transfers between devices, swap(): return lax.ppermute(value, axis, swap_pairs(lax.axis_size(axis), first))  16.1 us
    pallas_call x1, Pallas kernels, imaging(): pl.pallas_call(imaging_kernel, grid=(tiles // TILES_AT_ONCE,), out_shape=...  15.2 us
    ppermute x9, waiting for transfers between devices, swap(): return lax.ppermute(value, axis, swap_pairs(lax.axis_size(axis), first))  7.93 us
    ppermute x1, starting transfers between devices, local(): mine = lax.ppermute(half, ('gy', 'ka'), pairs)  6.17 us
    pallas_call x1, Pallas kernels, analysis(): pl.pallas_call(analysis_kernel, grid=(tiles // PAIR,), out_shape=(total,...  5.09 us
    unnamed x12, local copies, waits for them, and re-layouts  1.98 us
    pallas_call x1, Pallas kernels, inner_synthesis(): pl.pallas_call(inner_kernel, out_shape=jax.ShapeDtypeStruct(slope.shape,...  1.94 us
    pallas_call x1, Pallas kernels, outer_synthesis(): pl.pallas_call(outer_kernel, out_shape=jax.ShapeDtypeStruct(slope.shape,...  1.5 us
  transfers between devices with their start and end apart: 10, of which 5 were waited for; matrix products, arithmetic and copies ran while one was open for 0% of the time, Pallas kernels for 4%

profile of v9, /device:TPU:40, one launch (start us, length us, event | category | flops | bytes accessed | tf_op | source)
XLA Modules:
  0.0 57.4 jit_solution(10671519777570724941)
XLA Ops:
  0.6 0.0 copy-start.2
  0.7 5.1 %analysis.1 = (f32[8,64,256]{2,1,0:T(8,128)}, f32[6,64,128]{2,1,0:T(8,128)}, f32[3,64,128]{2,1,0:T(8,128)}, f32[64,256]{1,0:T(8,128)}, f32[1536,256]{1,0:T(8,128)}) custom-call(f32[1536,256]{1,0:T(8,128)} %mask_in.1, f32[6,2,4096]{2,1,0:T(2,128)} %kernels_in.1, f32[6]{0:T(128)} %weights.1, bf16[1024,128]{1,0:T(8,128)(2,1)} %constant.6.clone.tables_in), custom_call_target="tpu_custom_call" | custom-call | tf_op jit(solution)/shard_map/analysis/pallas_call | solution.py:558
  5.7 4.2 %collective-permute-start.1 = (f32[64,256]{1,0:T(8,128)}, f32[64,256]{1,0:T(8,128)S(1)}, u32[]{:S(2)}, u32[]{:S(2)}) collective-permute-start(f32[64,256]{1,0:T(8,128)} %get-tuple-element.25), channel_id=1, source_target_pairs={{2,4},{4,2},{6,8},{8,6},{10,12},{12,10},{14,16},{16,14},{18,20},{2... | collective-permute-start | bytes 196616 | tf_op jit(solution)/shard_map/ppermute | solution.py:707
  10.0 0.0 copy-start.3
  10.0 1.0 %copy-done.3 = f32[8,64,256]{2,1,0:T(8,128)S(1)} copy-done((f32[8,64,256]{2,1,0:T(8,128)S(1)}, f32[8,64,256]{2,1,0:T(8,128)}, u32[]{:S(2)}) %copy-start.3) | copy-done | bytes 524312
  11.0 0.1 shares.1
  11.1 0.8 %collective-permute-start = (f32[64,256]{1,0:T(8,128)S(1)}, f32[64,256]{1,0:T(8,128)S(1)}, u32[]{:S(2)}, u32[]{:S(2)}) collective-permute-start(f32[64,256]{1,0:T(8,128)S(1)} %get-tuple-element.24), channel_id=1, source_target_pairs={{0,2},{2,0},{4,6},{6,4},{8,10},{10,8},{12,14},{14,12},{16,18},{18,... | collective-permute-start | bytes 196616 | tf_op jit(solution)/shard_map/ppermute | solution.py:707
  11.8 6.2 %collective-permute-start.4 = (f32[3,64,128]{2,1,0:T(8,128)}, f32[3,64,128]{2,1,0:T(8,128)S(1)}, u32[]{:S(2)}, u32[]{:S(2)}) collective-permute-start(f32[3,64,128]{2,1,0:T(8,128)} %get-tuple-element.32), channel_id=1, source_target_pairs={{0,25},{1,24},{2,27},{3,26},{4,29},{5,28},{6,31},{7,30},{8,17},{9,... | collective-permute-start | bytes 294920 | tf_op jit(solution)/shard_map/ppermute | solution.py:715
  18.0 0.0 collective-permute-done.1.near_odd
  18.0 0.0 collective-permute-done.near_even
  18.0 0.1 merge.1
  18.1 0.1 collective-permute-start.2
  18.2 2.4 %collective-permute-start.3 = (f32[6,64,128]{2,1,0:T(8,128)S(1)}, f32[6,64,128]{2,1,0:T(8,128)S(1)}, u32[]{:S(2)}, u32[]{:S(2)}) collective-permute-start(f32[6,64,128]{2,1,0:T(8,128)S(1)} %get-tuple-element.28), channel_id=1, source_target_pairs={{32,64},{64,32},{96,128},{128,96},{160,192},{192,160},{33,65},{65,... | collective-permute-start | bytes 589832 | tf_op jit(solution)/shard_map/ppermute | solution.py:707
  20.6 0.3 collective-permute-done.4.mine
  20.9 1.0 %collective-permute-start.5 = (f32[3,64,128]{2,1,0:T(8,128)S(1)}, f32[3,64,128]{2,1,0:T(8,128)S(1)}, u32[]{:S(2)}, u32[]{:S(2)}) collective-permute-start(f32[3,64,128]{2,1,0:T(8,128)S(1)} %collective-permute-done.4.mine), channel_id=1, source_target_pairs={{0,32},{32,0},{64,96},{96,64},{128,160},{160,128},{192,224},{224,1... | collective-permute-start | bytes 294920 | tf_op jit(solution)/shard_map/ppermute | solution.py:707
  21.9 0.9 %copy-done.5 = f32[6,64,128]{2,1,0:T(8,128)S(1)} copy-done((f32[6,64,128]{2,1,0:T(8,128)S(1)}, f32[6,64,128]{2,1,0:T(8,128)}, u32[]{:S(2)}) %copy-start.5) | copy-done | bytes 196632
  22.8 0.1 prepare_own.1
  22.9 0.0 collective-permute-done.5.partners
  22.9 0.1 prepare_other.1
  23.1 0.0 collective-permute-done.2.from_even
  23.1 2.1 %collective-permute-done.3.from_odd = f32[6,64,128]{2,1,0:T(8,128)S(1)} collective-permute-done((f32[6,64,128]{2,1,0:T(8,128)S(1)}, f32[6,64,128]{2,1,0:T(8,128)S(1)}, u32[]{:S(2)}, u32[]{:S(2)}) %collective-permute-start.3) | collective-permute-done | bytes 196640 | tf_op jit(solution)/shard_map/ppermute | solution.py:707
  25.2 15.2 %imaging.1 = (f32[1536,256]{1,0:T(8,128)}, f32[6,64,128]{2,1,0:T(8,128)S(1)}) custom-call(f32[6,64,128]{2,1,0:T(8,128)S(1)} %get-tuple-element.26.share, f32[6,64,128]{2,1,0:T(8,128)S(1)} %collective-permute-done.2.from_even, f32[6,64,128]{2,1,0:T(8,128)S(1)} %collective-permute-done.3.from_odd, f32[6,64,128]{2,1,0:T(8,128)S(1)} %get-tuple-element.30.straight_own, ...), custom_call_target="tpu_custom_call" | custom-call | tf_op jit(solution)/shard_map/imaging/pallas_call | solution.py:638
  40.3 2.4 %collective-permute-start.7 = (f32[6,64,128]{2,1,0:T(8,128)S(1)}, f32[6,64,128]{2,1,0:T(8,128)S(1)}, u32[]{:S(2)}, u32[]{:S(2)}) collective-permute-start(f32[6,64,128]{2,1,0:T(8,128)S(1)} %get-tuple-element.35.own), channel_id=1, source_target_pairs={{32,64},{64,32},{96,128},{128,96},{160,192},{192,160},{33,65},{65,... | collective-permute-start | bytes 589832 | tf_op jit(solution)/shard_map/ppermute | solution.py:707
  42.8 1.2 %collective-permute-start.6 = (f32[6,64,128]{2,1,0:T(8,128)S(1)}, f32[6,64,128]{2,1,0:T(8,128)S(1)}, u32[]{:S(2)}, u32[]{:S(2)}) collective-permute-start(f32[6,64,128]{2,1,0:T(8,128)S(1)} %get-tuple-element.35.own), channel_id=1, source_target_pairs={{0,32},{32,0},{64,96},{96,64},{128,160},{160,128},{192,224},{224,1... | collective-permute-start | bytes 589832 | tf_op jit(solution)/shard_map/ppermute | solution.py:707
  44.0 3.3 %collective-permute-done.7.odd_in = f32[6,64,128]{2,1,0:T(8,128)S(1)} collective-permute-done((f32[6,64,128]{2,1,0:T(8,128)S(1)}, f32[6,64,128]{2,1,0:T(8,128)S(1)}, u32[]{:S(2)}, u32[]{:S(2)}) %collective-permute-start.7) | collective-permute-done | bytes 196640 | tf_op jit(solution)/shard_map/ppermute | solution.py:707
  47.3 0.0 collective-permute-done.6.even_in
  47.4 2.3 %collective-permute-start.9 = (f32[64,256]{1,0:T(8,128)S(1)}, f32[64,256]{1,0:T(8,128)S(1)}, u32[]{:S(2)}, u32[]{:S(2)}) collective-permute-start(f32[64,256]{1,0:T(8,128)S(1)} %odd_edge.1.before), channel_id=1, source_target_pairs={{2,4},{4,2},{6,8},{8,6},{10,12},{12,10},{14,16},{16,14},{18,20},{2... | collective-permute-start | bytes 196616 | tf_op jit(solution)/shard_map/ppermute | solution.py:707
  49.7 1.7 %collective-permute-start.8 = (f32[64,256]{1,0:T(8,128)S(1)}, f32[64,256]{1,0:T(8,128)S(1)}, u32[]{:S(2)}, u32[]{:S(2)}) collective-permute-start(f32[64,256]{1,0:T(8,128)S(1)} %even_edge.1), channel_id=1, source_target_pairs={{0,2},{2,0},{4,6},{6,4},{8,10},{10,8},{12,14},{14,12},{16,18},{18,... | collective-permute-start | bytes 196616 | tf_op jit(solution)/shard_map/ppermute | solution.py:707
  51.4 1.9 %inner_synthesis.1.partial = f32[1536,256]{1,0:T(8,128)} custom-call(f32[6,64,128]{2,1,0:T(8,128)S(1)} %get-tuple-element.35.own, f32[6,64,128]{2,1,0:T(8,128)S(1)} %collective-permute-done.6.even_in, f32[6,64,128]{2,1,0:T(8,128)S(1)} %collective-permute-done.7.odd_in, f32[1536,256]{1,0:T(8,128)S(1)} %copy-done.1, bf16[1024,128]{1,0:T(8,128)(2,1)S(1)} %copy-done.4), custom_call_target="tpu_custom_call" | custom-call | flops 1500000000 | bytes 2500000 | tf_op jit(solution)/shard_map/inner_synthesis/pallas_call | solution.py:661
  53.3 0.8 %collective-permute-done.8.near_even = f32[64,256]{1,0:T(8,128)S(1)} collective-permute-done((f32[64,256]{1,0:T(8,128)S(1)}, f32[64,256]{1,0:T(8,128)S(1)}, u32[]{:S(2)}, u32[]{:S(2)}) %collective-permute-start.8) | collective-permute-done | bytes 65568 | tf_op jit(solution)/shard_map/ppermute | solution.py:707
  54.1 1.8 %collective-permute-done.9.near_odd = f32[64,256]{1,0:T(8,128)S(1)} collective-permute-done((f32[64,256]{1,0:T(8,128)S(1)}, f32[64,256]{1,0:T(8,128)S(1)}, u32[]{:S(2)}, u32[]{:S(2)}) %collective-permute-start.9) | collective-permute-done | bytes 65568 | tf_op jit(solution)/shard_map/ppermute | solution.py:707
  55.9 1.5 %outer_synthesis.1 = f32[1536,256]{1,0:T(8,128)} custom-call(f32[6,64,128]{2,1,0:T(8,128)S(1)} %get-tuple-element.35.own, f32[6,64,128]{2,1,0:T(8,128)S(1)} %collective-permute-done.6.even_in, f32[6,64,128]{2,1,0:T(8,128)S(1)} %collective-permute-done.7.odd_in, f32[64,256]{1,0:T(8,128)S(1)} %collective-permute-done.8.near_even, ...), custom_call_target="tpu_custom_call", output_to_operand_aliasing={{}: (7, {})} | custom-call | tf_op jit(solution)/shard_map/outer_synthesis/pallas_call | solution.py:681
  (10 shorter events, 0.1 us)
Async XLA Ops:
  0.6 24.5 %copy-start.2 = (bf16[4608,128]{1,0:T(8,128)(2,1)S(1)}, bf16[4608,128]{1,0:T(8,128)(2,1)}, u32[]{:S(2)}) copy-start(bf16[4608,128]{1,0:T(8,128)(2,1)} %constant.7.clone.wide) | copy-start | bytes 3538948
  0.6 24.5 %copy-start = (s32[1536,256]{1,0:T(8,128)S(1)}, s32[1536,256]{1,0:T(8,128)}, u32[]{:S(2)}) copy-start(s32[1536,256]{1,0:T(8,128)} %target.1) | copy-start | bytes 4718596
  5.7 12.3 %collective-permute-start.1 = (f32[64,256]{1,0:T(8,128)}, f32[64,256]{1,0:T(8,128)S(1)}, u32[]{:S(2)}, u32[]{:S(2)}) collective-permute-start(f32[64,256]{1,0:T(8,128)} %get-tuple-element.25), channel_id=1, source_target_pairs={{2,4},{4,2},{6,8},{8,6},{10,12},{12,10},{14,16},{16,14},{18,20},{2... | collective-permute-start | bytes 196616 | tf_op jit(solution)/shard_map/ppermute | solution.py:707
  10.0 1.0 %copy-start.3 = (f32[8,64,256]{2,1,0:T(8,128)S(1)}, f32[8,64,256]{2,1,0:T(8,128)}, u32[]{:S(2)}) copy-start(f32[8,64,256]{2,1,0:T(8,128)} %get-tuple-element.20.total) | copy-start | bytes 1572868
  11.1 6.9 %collective-permute-start = (f32[64,256]{1,0:T(8,128)S(1)}, f32[64,256]{1,0:T(8,128)S(1)}, u32[]{:S(2)}, u32[]{:S(2)}) collective-permute-start(f32[64,256]{1,0:T(8,128)S(1)} %get-tuple-element.24), channel_id=1, source_target_pairs={{0,2},{2,0},{4,6},{6,4},{8,10},{10,8},{12,14},{14,12},{16,18},{18,... | collective-permute-start | bytes 196616 | tf_op jit(solution)/shard_map/ppermute | solution.py:707
  11.8 9.0 %collective-permute-start.4 = (f32[3,64,128]{2,1,0:T(8,128)}, f32[3,64,128]{2,1,0:T(8,128)S(1)}, u32[]{:S(2)}, u32[]{:S(2)}) collective-permute-start(f32[3,64,128]{2,1,0:T(8,128)} %get-tuple-element.32), channel_id=1, source_target_pairs={{0,25},{1,24},{2,27},{3,26},{4,29},{5,28},{6,31},{7,30},{8,17},{9,... | collective-permute-start | bytes 294920 | tf_op jit(solution)/shard_map/ppermute | solution.py:715
  18.1 5.0 %collective-permute-start.2 = (f32[6,64,128]{2,1,0:T(8,128)S(1)}, f32[6,64,128]{2,1,0:T(8,128)S(1)}, u32[]{:S(2)}, u32[]{:S(2)}) collective-permute-start(f32[6,64,128]{2,1,0:T(8,128)S(1)} %get-tuple-element.27), channel_id=1, source_target_pairs={{0,32},{32,0},{64,96},{96,64},{128,160},{160,128},{192,224},{224,1... | collective-permute-start | bytes 589832 | tf_op jit(solution)/shard_map/ppermute | solution.py:707
  18.2 7.0 %collective-permute-start.3 = (f32[6,64,128]{2,1,0:T(8,128)S(1)}, f32[6,64,128]{2,1,0:T(8,128)S(1)}, u32[]{:S(2)}, u32[]{:S(2)}) collective-permute-start(f32[6,64,128]{2,1,0:T(8,128)S(1)} %get-tuple-element.28), channel_id=1, source_target_pairs={{32,64},{64,32},{96,128},{128,96},{160,192},{192,160},{33,65},{65,... | collective-permute-start | bytes 589832 | tf_op jit(solution)/shard_map/ppermute | solution.py:707
  20.9 2.1 %collective-permute-start.5 = (f32[3,64,128]{2,1,0:T(8,128)S(1)}, f32[3,64,128]{2,1,0:T(8,128)S(1)}, u32[]{:S(2)}, u32[]{:S(2)}) collective-permute-start(f32[3,64,128]{2,1,0:T(8,128)S(1)} %collective-permute-done.4.mine), channel_id=1, source_target_pairs={{0,32},{32,0},{64,96},{96,64},{128,160},{160,128},{192,224},{224,1... | collective-permute-start | bytes 294920 | tf_op jit(solution)/shard_map/ppermute | solution.py:707
  21.9 0.9 %copy-start.5 = (f32[6,64,128]{2,1,0:T(8,128)S(1)}, f32[6,64,128]{2,1,0:T(8,128)}, u32[]{:S(2)}) copy-start(f32[6,64,128]{2,1,0:T(8,128)} %get-tuple-element.29.own) | copy-start | bytes 589828
  25.2 26.2 %copy-start.1 = (f32[1536,256]{1,0:T(8,128)S(1)}, f32[1536,256]{1,0:T(8,128)}, u32[]{:S(2)}) copy-start(f32[1536,256]{1,0:T(8,128)} %get-tuple-element.36.slope) | copy-start | bytes 4718596
  25.2 26.2 %copy-start.4 = (bf16[1024,128]{1,0:T(8,128)(2,1)S(1)}, bf16[1024,128]{1,0:T(8,128)(2,1)}, u32[]{:S(2)}) copy-start(bf16[1024,128]{1,0:T(8,128)(2,1)} %constant.8.clone.tables) | copy-start | bytes 786436
  40.3 7.0 %collective-permute-start.7 = (f32[6,64,128]{2,1,0:T(8,128)S(1)}, f32[6,64,128]{2,1,0:T(8,128)S(1)}, u32[]{:S(2)}, u32[]{:S(2)}) collective-permute-start(f32[6,64,128]{2,1,0:T(8,128)S(1)} %get-tuple-element.35.own), channel_id=1, source_target_pairs={{32,64},{64,32},{96,128},{128,96},{160,192},{192,160},{33,65},{65,... | collective-permute-start | bytes 589832 | tf_op jit(solution)/shard_map/ppermute | solution.py:707
  42.8 4.5 %collective-permute-start.6 = (f32[6,64,128]{2,1,0:T(8,128)S(1)}, f32[6,64,128]{2,1,0:T(8,128)S(1)}, u32[]{:S(2)}, u32[]{:S(2)}) collective-permute-start(f32[6,64,128]{2,1,0:T(8,128)S(1)} %get-tuple-element.35.own), channel_id=1, source_target_pairs={{0,32},{32,0},{64,96},{96,64},{128,160},{160,128},{192,224},{224,1... | collective-permute-start | bytes 589832 | tf_op jit(solution)/shard_map/ppermute | solution.py:707
  47.4 8.5 %collective-permute-start.9 = (f32[64,256]{1,0:T(8,128)S(1)}, f32[64,256]{1,0:T(8,128)S(1)}, u32[]{:S(2)}, u32[]{:S(2)}) collective-permute-start(f32[64,256]{1,0:T(8,128)S(1)} %odd_edge.1.before), channel_id=1, source_target_pairs={{2,4},{4,2},{6,8},{8,6},{10,12},{12,10},{14,16},{16,14},{18,20},{2... | collective-permute-start | bytes 196616 | tf_op jit(solution)/shard_map/ppermute | solution.py:707
  49.7 4.4 %collective-permute-start.8 = (f32[64,256]{1,0:T(8,128)S(1)}, f32[64,256]{1,0:T(8,128)S(1)}, u32[]{:S(2)}, u32[]{:S(2)}) collective-permute-start(f32[64,256]{1,0:T(8,128)S(1)} %even_edge.1), channel_id=1, source_target_pairs={{0,2},{2,0},{4,6},{6,4},{8,10},{10,8},{12,14},{14,12},{16,18},{18,... | collective-permute-start | bytes 196616 | tf_op jit(solution)/shard_map/ppermute | solution.py:707

commit v10 on v8

--- a/solution.py
+++ b/solution.py
@@ -286,11 +286,11 @@
 
 def analysis_kernel(
     mask_in, kernels_in, weights, tables_in,
-    total, packed, half, edge_even, edge_odd, slope,
+    total, packed, half, edge_odd, slope,
     real, imag, sums, mask, kernels, tables, semaphores,
 ):
     step = pl.program_id(0)
-    count = total.shape[0]
+    count = total.shape[0] - 2
 
     def pixels_copy(step):
         place = pl.ds(pl.multiple_of(step * PAIR * TILE, TILE), PAIR * TILE)
@@ -331,17 +331,15 @@
 
     @pl.when(step == pl.num_programs(0) - 1)
     def _():
-        total[...] = sums[1 : count + 1]
-        up, down = sums[0], sums[count + 1]
-        odd_row = is_odd("gy")
-        edge_even[...] = jnp.where(odd_row, up, down)
-        edge_odd[...] = jnp.where(odd_row, down, up)
-
-
-def shares_kernel(total, share, to_even, to_odd):
+        total[...] = sums[...]
+        edge_odd[...] = jnp.where(is_odd("gy"), sums[count + 1], sums[0])
+
+
+def shares_kernel(total, share, to_even, to_odd, edge):
     odd_col = is_odd("gx")
+    edge[...] = jnp.where(is_odd("gy"), total[0], total[share.shape[0] + 1])
     for index in range(share.shape[0]):
-        left, right = total[index, :, : 2 * FB], total[index, :, 2 * FB :]
+        left, right = total[index + 1, :, : 2 * FB], total[index + 1, :, 2 * FB :]
         share[index] = parity((FB, 2 * FB)) * (left + right)
         to_even[index] = jnp.where(odd_col, left, right)
         to_odd[index] = jnp.where(odd_col, right, left)
@@ -392,15 +390,20 @@
                 part = both[:, j * 2 * FB : (j + 1) * 2 * FB]
                 cosine, sine = part[:HALF], sign * swapped(part[HALF:])
                 halves_of += [cosine - sine, cosine + sine]
-        found = times_table(jnp.concatenate(halves_of, axis=0), wide_table(wide, SPREAD))
-        fields[group] = found
+        powers = []
+        for first in range(0, len(halves_of), len(halves_of) // 2):
+            chunk = halves_of[first : first + len(halves_of) // 2]
+            found = times_table(jnp.concatenate(chunk, axis=0), wide_table(wide, SPREAD))
+            place = first * HALF
+            fields[group, place : place + found.shape[0], :] = found
+            for start in range(0, found.shape[0], COARSE):
+                real = found[start : start + COARSE, :COARSE]
+                imag = found[start : start + COARSE, COARSE:]
+                powers.append(real * real + imag * imag)
         for tile in tiles:
-            total = jnp.zeros((COARSE, COARSE), jnp.float32)
-            for i in range(count):
-                place = (tile * count + i) * COARSE
-                real = found[place : place + COARSE, :COARSE]
-                imag = found[place : place + COARSE, COARSE:]
-                total = total + (real * real + imag * imag)
+            total = powers[tile * count]
+            for power in powers[tile * count + 1 : (tile + 1) * count]:
+                total = total + power
             intensities[tile].append(total)
 
     half_fine = times_table(
@@ -565,7 +568,7 @@
     tiles = mask.shape[0] // TILE
     tables = jnp.asarray(TABLES["analysis"])
     part = pltpu.VMEM((FB // 2, 2 * FB), jnp.float32)
-    total = jax.ShapeDtypeStruct((tiles, FB, 4 * FB), jnp.float32)
+    total = jax.ShapeDtypeStruct((tiles + 2, FB, 4 * FB), jnp.float32)
     packed = jax.ShapeDtypeStruct((kernels.shape[0], FB, 2 * FB), jnp.float32)
     half = jax.ShapeDtypeStruct((kernels.shape[0] // 2, FB, 2 * FB), jnp.float32)
     edge = jax.ShapeDtypeStruct((FB, 4 * FB), jnp.float32)
@@ -573,7 +576,7 @@
         analysis_kernel,
         grid=(tiles // PAIR,),
         out_shape=(
-            total, packed, half, edge, edge, jax.ShapeDtypeStruct(mask.shape, jnp.float32)
+            total, packed, half, edge, jax.ShapeDtypeStruct(mask.shape, jnp.float32)
         ),
         in_specs=[
             pl.BlockSpec(memory_space=pltpu.HBM),
@@ -581,7 +584,7 @@
             pl.BlockSpec(memory_space=pltpu.SMEM),
             pl.BlockSpec(memory_space=pltpu.HBM),
         ],
-        out_specs=[whole(out) for out in (total, packed, half, edge, edge)] + [tile_pair()],
+        out_specs=[whole(out) for out in (total, packed, half, edge)] + [tile_pair()],
         scratch_shapes=[
             part,
             part,
@@ -609,8 +612,9 @@
 
 
 def shares(total):
-    spectra = jax.ShapeDtypeStruct((total.shape[0], FB, 2 * FB), jnp.float32)
-    return simple_call(shares_kernel, (spectra,) * 3, total, name="shares")
+    spectra = jax.ShapeDtypeStruct((total.shape[0] - 2, FB, 2 * FB), jnp.float32)
+    side = jax.ShapeDtypeStruct((FB, 4 * FB), jnp.float32)
+    return simple_call(shares_kernel, (spectra,) * 3 + (side,), total, name="shares")
 
 
 def merge(share, to_even, to_odd, near_even, near_odd):
@@ -712,7 +716,7 @@
     def swap(value, axis, first):
         return lax.ppermute(value, axis, swap_pairs(lax.axis_size(axis), first))
 
-    total, packed, half, edge_even, edge_odd, slope = analysis(mask_param, kernels, weights)
+    total, packed, half, edge_odd, slope = analysis(mask_param, kernels, weights)
     inner = rows // 4
     pairs = []
     for place in range(rows):
@@ -720,8 +724,9 @@
         pairs += [(2 * place, 2 * mirror + 1), (2 * place + 1, 2 * mirror)]
     mine = lax.ppermute(half, ("gy", "ka"), pairs)
     halo_odd = swap(edge_odd, "gy", 1)
+    *sums, edge_even = shares(total)
     halo_even = swap(edge_even, "gy", 0)
-    share, to_even, to_odd = merge(*shares(total), halo_even, halo_odd)
+    share, to_even, to_odd = merge(*sums, halo_even, halo_odd)
     from_odd = swap(to_odd, "gx", 1)
     from_even = swap(to_even, "gx", 0)
     own = prepare_own(packed)

time: 53.7 us -> 54.4 us (1.013)
  starting transfers between devices: 21.7 us -> 22.3 us
    ppermute x9, starting transfers between devices: 14.9 us -> 16.1 us  [swap(): return lax.ppermute(value, axis, swap_pairs(lax.axis_size(axis), first))]
    ppermute x1, starting transfers between devices: 6.83 us -> 6.17 us  [local(): mine = lax.ppermute(half, ('gy', 'ka'), pairs)]
where the time goes in v10:
time: 54.4 us; the launch traced here: 54.1 us
  starting transfers between devices  22.3 us (41%)
  Pallas kernels  19.1 us (35%)
  waiting for transfers between devices  10 us (18%)
  local copies, waits for them, and re-layouts  1.98 us (4%)
  between operations  0.8 us (1%)
    ppermute x9, starting transfers between devices, swap(): return lax.ppermute(value, axis, swap_pairs(lax.axis_size(axis), first))  16.1 us
    pallas_call x1, Pallas kernels, imaging(): pl.pallas_call(imaging_kernel, grid=(tiles // TILES_AT_ONCE,), out_shape=...  10.2 us
    ppermute x9, waiting for transfers between devices, swap(): return lax.ppermute(value, axis, swap_pairs(lax.axis_size(axis), first))  9.75 us
    ppermute x1, starting transfers between devices, local(): mine = lax.ppermute(half, ('gy', 'ka'), pairs)  6.17 us
    pallas_call x1, Pallas kernels, analysis(): pl.pallas_call(analysis_kernel, grid=(tiles // PAIR,), out_shape=(total,...  5.09 us
    unnamed x12, local copies, waits for them, and re-layouts  1.98 us
    pallas_call x1, Pallas kernels, inner_synthesis(): pl.pallas_call(inner_kernel, out_shape=jax.ShapeDtypeStruct(slope.shape,...  1.95 us
    pallas_call x1, Pallas kernels, outer_synthesis(): pl.pallas_call(outer_kernel, out_shape=jax.ShapeDtypeStruct(slope.shape,...  1.5 us
  transfers between devices with their start and end apart: 10, of which 4 were waited for; matrix products, arithmetic and copies ran while one was open for 0% of the time, Pallas kernels for 4%

profile of v10, /device:TPU:40, one launch (start us, length us, event | category | flops | bytes accessed | tf_op | source)
XLA Modules:
  0.0 54.1 jit_solution(15373613009282734960)
XLA Ops:
  0.6 0.0 copy-start.2
  0.7 5.1 %analysis.1 = (f32[8,64,256]{2,1,0:T(8,128)}, f32[6,64,128]{2,1,0:T(8,128)}, f32[3,64,128]{2,1,0:T(8,128)}, f32[64,256]{1,0:T(8,128)}, f32[1536,256]{1,0:T(8,128)}) custom-call(f32[1536,256]{1,0:T(8,128)} %mask_in.1, f32[6,2,4096]{2,1,0:T(2,128)} %kernels_in.1, f32[6]{0:T(128)} %weights.1, bf16[1024,128]{1,0:T(8,128)(2,1)} %constant.6.clone.tables_in), custom_call_target="tpu_custom_call" | custom-call | tf_op jit(solution)/shard_map/analysis/pallas_call | solution.py:575
  5.7 4.2 %collective-permute-start.1 = (f32[64,256]{1,0:T(8,128)}, f32[64,256]{1,0:T(8,128)S(1)}, u32[]{:S(2)}, u32[]{:S(2)}) collective-permute-start(f32[64,256]{1,0:T(8,128)} %get-tuple-element.27), channel_id=1, source_target_pairs={{2,4},{4,2},{6,8},{8,6},{10,12},{12,10},{14,16},{16,14},{18,20},{2... | collective-permute-start | bytes 196616 | tf_op jit(solution)/shard_map/ppermute | solution.py:717
  10.0 0.0 copy-start.3
  10.0 1.0 %copy-done.3 = f32[8,64,256]{2,1,0:T(8,128)S(1)} copy-done((f32[8,64,256]{2,1,0:T(8,128)S(1)}, f32[8,64,256]{2,1,0:T(8,128)}, u32[]{:S(2)}) %copy-start.3) | copy-done | bytes 524312
  11.0 0.1 shares.1
  11.1 0.8 %collective-permute-start = (f32[64,256]{1,0:T(8,128)S(1)}, f32[64,256]{1,0:T(8,128)S(1)}, u32[]{:S(2)}, u32[]{:S(2)}) collective-permute-start(f32[64,256]{1,0:T(8,128)S(1)} %get-tuple-element.26), channel_id=1, source_target_pairs={{0,2},{2,0},{4,6},{6,4},{8,10},{10,8},{12,14},{14,12},{16,18},{18,... | collective-permute-start | bytes 196616 | tf_op jit(solution)/shard_map/ppermute | solution.py:717
  11.8 6.2 %collective-permute-start.4 = (f32[3,64,128]{2,1,0:T(8,128)}, f32[3,64,128]{2,1,0:T(8,128)S(1)}, u32[]{:S(2)}, u32[]{:S(2)}) collective-permute-start(f32[3,64,128]{2,1,0:T(8,128)} %get-tuple-element.34), channel_id=1, source_target_pairs={{0,25},{1,24},{2,27},{3,26},{4,29},{5,28},{6,31},{7,30},{8,17},{9,... | collective-permute-start | bytes 294920 | tf_op jit(solution)/shard_map/ppermute | solution.py:725
  18.0 0.0 collective-permute-done.1.near_odd
  18.0 0.0 collective-permute-done.near_even
  18.0 0.1 merge.1
  18.1 0.1 collective-permute-start.2
  18.2 2.4 %collective-permute-start.3 = (f32[6,64,128]{2,1,0:T(8,128)S(1)}, f32[6,64,128]{2,1,0:T(8,128)S(1)}, u32[]{:S(2)}, u32[]{:S(2)}) collective-permute-start(f32[6,64,128]{2,1,0:T(8,128)S(1)} %get-tuple-element.30), channel_id=1, source_target_pairs={{32,64},{64,32},{96,128},{128,96},{160,192},{192,160},{33,65},{65,... | collective-permute-start | bytes 589832 | tf_op jit(solution)/shard_map/ppermute | solution.py:717
  20.6 0.3 collective-permute-done.4.mine
  20.9 1.0 %collective-permute-start.5 = (f32[3,64,128]{2,1,0:T(8,128)S(1)}, f32[3,64,128]{2,1,0:T(8,128)S(1)}, u32[]{:S(2)}, u32[]{:S(2)}) collective-permute-start(f32[3,64,128]{2,1,0:T(8,128)S(1)} %collective-permute-done.4.mine), channel_id=1, source_target_pairs={{0,32},{32,0},{64,96},{96,64},{128,160},{160,128},{192,224},{224,1... | collective-permute-start | bytes 294920 | tf_op jit(solution)/shard_map/ppermute | solution.py:717
  21.9 0.9 %copy-done.5 = f32[6,64,128]{2,1,0:T(8,128)S(1)} copy-done((f32[6,64,128]{2,1,0:T(8,128)S(1)}, f32[6,64,128]{2,1,0:T(8,128)}, u32[]{:S(2)}) %copy-start.5) | copy-done | bytes 196632
  22.8 0.1 prepare_own.1
  22.9 0.0 collective-permute-done.5.partners
  22.9 0.1 prepare_other.1
  23.1 0.0 collective-permute-done.2.from_even
  23.1 2.1 %collective-permute-done.3.from_odd = f32[6,64,128]{2,1,0:T(8,128)S(1)} collective-permute-done((f32[6,64,128]{2,1,0:T(8,128)S(1)}, f32[6,64,128]{2,1,0:T(8,128)S(1)}, u32[]{:S(2)}, u32[]{:S(2)}) %collective-permute-start.3) | collective-permute-done | bytes 196640 | tf_op jit(solution)/shard_map/ppermute | solution.py:717
  25.2 10.2 %imaging.1 = (f32[1536,256]{1,0:T(8,128)}, f32[6,64,128]{2,1,0:T(8,128)S(1)}) custom-call(f32[6,64,128]{2,1,0:T(8,128)S(1)} %get-tuple-element.28.share, f32[6,64,128]{2,1,0:T(8,128)S(1)} %collective-permute-done.2.from_even, f32[6,64,128]{2,1,0:T(8,128)S(1)} %collective-permute-done.3.from_odd, f32[6,64,128]{2,1,0:T(8,128)S(1)} %get-tuple-element.32.straight_own, ...), custom_call_target="tpu_custom_call" | custom-call | tf_op jit(solution)/shard_map/imaging/pallas_call | solution.py:648
  35.3 2.4 %collective-permute-start.7 = (f32[6,64,128]{2,1,0:T(8,128)S(1)}, f32[6,64,128]{2,1,0:T(8,128)S(1)}, u32[]{:S(2)}, u32[]{:S(2)}) collective-permute-start(f32[6,64,128]{2,1,0:T(8,128)S(1)} %get-tuple-element.37.own), channel_id=1, source_target_pairs={{32,64},{64,32},{96,128},{128,96},{160,192},{192,160},{33,65},{65,... | collective-permute-start | bytes 589832 | tf_op jit(solution)/shard_map/ppermute | solution.py:717
  37.8 1.2 %collective-permute-start.6 = (f32[6,64,128]{2,1,0:T(8,128)S(1)}, f32[6,64,128]{2,1,0:T(8,128)S(1)}, u32[]{:S(2)}, u32[]{:S(2)}) collective-permute-start(f32[6,64,128]{2,1,0:T(8,128)S(1)} %get-tuple-element.37.own), channel_id=1, source_target_pairs={{0,32},{32,0},{64,96},{96,64},{128,160},{160,128},{192,224},{224,1... | collective-permute-start | bytes 589832 | tf_op jit(solution)/shard_map/ppermute | solution.py:717
  39.0 3.3 %collective-permute-done.7.odd_in = f32[6,64,128]{2,1,0:T(8,128)S(1)} collective-permute-done((f32[6,64,128]{2,1,0:T(8,128)S(1)}, f32[6,64,128]{2,1,0:T(8,128)S(1)}, u32[]{:S(2)}, u32[]{:S(2)}) %collective-permute-start.7) | collective-permute-done | bytes 196640 | tf_op jit(solution)/shard_map/ppermute | solution.py:717
  42.3 0.0 collective-permute-done.6.even_in
  42.4 2.0 %collective-permute-start.8 = (f32[64,256]{1,0:T(8,128)S(1)}, f32[64,256]{1,0:T(8,128)S(1)}, u32[]{:S(2)}, u32[]{:S(2)}) collective-permute-start(f32[64,256]{1,0:T(8,128)S(1)} %get-tuple-element.38), channel_id=1, source_target_pairs={{0,2},{2,0},{4,6},{6,4},{8,10},{10,8},{12,14},{14,12},{16,18},{18,... | collective-permute-start | bytes 196616 | tf_op jit(solution)/shard_map/ppermute | solution.py:717
  44.4 1.9 %collective-permute-start.9 = (f32[64,256]{1,0:T(8,128)S(1)}, f32[64,256]{1,0:T(8,128)S(1)}, u32[]{:S(2)}, u32[]{:S(2)}) collective-permute-start(f32[64,256]{1,0:T(8,128)S(1)} %get-tuple-element.39), channel_id=1, source_target_pairs={{2,4},{4,2},{6,8},{8,6},{10,12},{12,10},{14,16},{16,14},{18,20},{2... | collective-permute-start | bytes 196616 | tf_op jit(solution)/shard_map/ppermute | solution.py:717
  46.3 1.9 %inner_synthesis.1.partial = f32[1536,256]{1,0:T(8,128)} custom-call(f32[6,64,128]{2,1,0:T(8,128)S(1)} %get-tuple-element.37.own, f32[6,64,128]{2,1,0:T(8,128)S(1)} %collective-permute-done.6.even_in, f32[6,64,128]{2,1,0:T(8,128)S(1)} %collective-permute-done.7.odd_in, f32[1536,256]{1,0:T(8,128)S(1)} %copy-done.1, bf16[1024,128]{1,0:T(8,128)(2,1)S(1)} %copy-done.4), custom_call_target="tpu_custom_call" | custom-call | flops 1500000000 | bytes 2500000 | tf_op jit(solution)/shard_map/inner_synthesis/pallas_call | solution.py:671
  48.3 0.0 collective-permute-done.8.near_even
  48.3 4.4 %collective-permute-done.9.near_odd = f32[64,256]{1,0:T(8,128)S(1)} collective-permute-done((f32[64,256]{1,0:T(8,128)S(1)}, f32[64,256]{1,0:T(8,128)S(1)}, u32[]{:S(2)}, u32[]{:S(2)}) %collective-permute-start.9) | collective-permute-done | bytes 65568 | tf_op jit(solution)/shard_map/ppermute | solution.py:717
  52.6 1.5 %outer_synthesis.1 = f32[1536,256]{1,0:T(8,128)} custom-call(f32[6,64,128]{2,1,0:T(8,128)S(1)} %get-tuple-element.37.own, f32[6,64,128]{2,1,0:T(8,128)S(1)} %collective-permute-done.6.even_in, f32[6,64,128]{2,1,0:T(8,128)S(1)} %collective-permute-done.7.odd_in, f32[64,256]{1,0:T(8,128)S(1)} %collective-permute-done.8.near_even, ...), custom_call_target="tpu_custom_call", output_to_operand_aliasing={{}: (7, {})} | custom-call | tf_op jit(solution)/shard_map/outer_synthesis/pallas_call | solution.py:691
  (9 shorter events, 0.0 us)
Async XLA Ops:
  0.6 24.5 %copy-start.2 = (bf16[4608,128]{1,0:T(8,128)(2,1)S(1)}, bf16[4608,128]{1,0:T(8,128)(2,1)}, u32[]{:S(2)}) copy-start(bf16[4608,128]{1,0:T(8,128)(2,1)} %constant.7.clone.wide) | copy-start | bytes 3538948
  0.6 24.5 %copy-start = (s32[1536,256]{1,0:T(8,128)S(1)}, s32[1536,256]{1,0:T(8,128)}, u32[]{:S(2)}) copy-start(s32[1536,256]{1,0:T(8,128)} %target.1) | copy-start | bytes 4718596
  5.7 12.3 %collective-permute-start.1 = (f32[64,256]{1,0:T(8,128)}, f32[64,256]{1,0:T(8,128)S(1)}, u32[]{:S(2)}, u32[]{:S(2)}) collective-permute-start(f32[64,256]{1,0:T(8,128)} %get-tuple-element.27), channel_id=1, source_target_pairs={{2,4},{4,2},{6,8},{8,6},{10,12},{12,10},{14,16},{16,14},{18,20},{2... | collective-permute-start | bytes 196616 | tf_op jit(solution)/shard_map/ppermute | solution.py:717
  10.0 1.0 %copy-start.3 = (f32[8,64,256]{2,1,0:T(8,128)S(1)}, f32[8,64,256]{2,1,0:T(8,128)}, u32[]{:S(2)}) copy-start(f32[8,64,256]{2,1,0:T(8,128)} %get-tuple-element.22.total) | copy-start | bytes 1572868
  11.1 6.9 %collective-permute-start = (f32[64,256]{1,0:T(8,128)S(1)}, f32[64,256]{1,0:T(8,128)S(1)}, u32[]{:S(2)}, u32[]{:S(2)}) collective-permute-start(f32[64,256]{1,0:T(8,128)S(1)} %get-tuple-element.26), channel_id=1, source_target_pairs={{0,2},{2,0},{4,6},{6,4},{8,10},{10,8},{12,14},{14,12},{16,18},{18,... | collective-permute-start | bytes 196616 | tf_op jit(solution)/shard_map/ppermute | solution.py:717
  11.8 9.0 %collective-permute-start.4 = (f32[3,64,128]{2,1,0:T(8,128)}, f32[3,64,128]{2,1,0:T(8,128)S(1)}, u32[]{:S(2)}, u32[]{:S(2)}) collective-permute-start(f32[3,64,128]{2,1,0:T(8,128)} %get-tuple-element.34), channel_id=1, source_target_pairs={{0,25},{1,24},{2,27},{3,26},{4,29},{5,28},{6,31},{7,30},{8,17},{9,... | collective-permute-start | bytes 294920 | tf_op jit(solution)/shard_map/ppermute | solution.py:725
  18.1 5.0 %collective-permute-start.2 = (f32[6,64,128]{2,1,0:T(8,128)S(1)}, f32[6,64,128]{2,1,0:T(8,128)S(1)}, u32[]{:S(2)}, u32[]{:S(2)}) collective-permute-start(f32[6,64,128]{2,1,0:T(8,128)S(1)} %get-tuple-element.29), channel_id=1, source_target_pairs={{0,32},{32,0},{64,96},{96,64},{128,160},{160,128},{192,224},{224,1... | collective-permute-start | bytes 589832 | tf_op jit(solution)/shard_map/ppermute | solution.py:717
  18.2 7.0 %collective-permute-start.3 = (f32[6,64,128]{2,1,0:T(8,128)S(1)}, f32[6,64,128]{2,1,0:T(8,128)S(1)}, u32[]{:S(2)}, u32[]{:S(2)}) collective-permute-start(f32[6,64,128]{2,1,0:T(8,128)S(1)} %get-tuple-element.30), channel_id=1, source_target_pairs={{32,64},{64,32},{96,128},{128,96},{160,192},{192,160},{33,65},{65,... | collective-permute-start | bytes 589832 | tf_op jit(solution)/shard_map/ppermute | solution.py:717
  20.9 2.1 %collective-permute-start.5 = (f32[3,64,128]{2,1,0:T(8,128)S(1)}, f32[3,64,128]{2,1,0:T(8,128)S(1)}, u32[]{:S(2)}, u32[]{:S(2)}) collective-permute-start(f32[3,64,128]{2,1,0:T(8,128)S(1)} %collective-permute-done.4.mine), channel_id=1, source_target_pairs={{0,32},{32,0},{64,96},{96,64},{128,160},{160,128},{192,224},{224,1... | collective-permute-start | bytes 294920 | tf_op jit(solution)/shard_map/ppermute | solution.py:717
  21.9 0.9 %copy-start.5 = (f32[6,64,128]{2,1,0:T(8,128)S(1)}, f32[6,64,128]{2,1,0:T(8,128)}, u32[]{:S(2)}) copy-start(f32[6,64,128]{2,1,0:T(8,128)} %get-tuple-element.31.own) | copy-start | bytes 589828
  25.2 21.1 %copy-start.1 = (f32[1536,256]{1,0:T(8,128)S(1)}, f32[1536,256]{1,0:T(8,128)}, u32[]{:S(2)}) copy-start(f32[1536,256]{1,0:T(8,128)} %get-tuple-element.40.slope) | copy-start | bytes 4718596
  25.2 21.1 %copy-start.4 = (bf16[1024,128]{1,0:T(8,128)(2,1)S(1)}, bf16[1024,128]{1,0:T(8,128)(2,1)}, u32[]{:S(2)}) copy-start(bf16[1024,128]{1,0:T(8,128)(2,1)} %constant.8.clone.tables) | copy-start | bytes 786436
  35.3 7.0 %collective-permute-start.7 = (f32[6,64,128]{2,1,0:T(8,128)S(1)}, f32[6,64,128]{2,1,0:T(8,128)S(1)}, u32[]{:S(2)}, u32[]{:S(2)}) collective-permute-start(f32[6,64,128]{2,1,0:T(8,128)S(1)} %get-tuple-element.37.own), channel_id=1, source_target_pairs={{32,64},{64,32},{96,128},{128,96},{160,192},{192,160},{33,65},{65,... | collective-permute-start | bytes 589832 | tf_op jit(solution)/shard_map/ppermute | solution.py:717
  37.8 4.5 %collective-permute-start.6 = (f32[6,64,128]{2,1,0:T(8,128)S(1)}, f32[6,64,128]{2,1,0:T(8,128)S(1)}, u32[]{:S(2)}, u32[]{:S(2)}) collective-permute-start(f32[6,64,128]{2,1,0:T(8,128)S(1)} %get-tuple-element.37.own), channel_id=1, source_target_pairs={{0,32},{32,0},{64,96},{96,64},{128,160},{160,128},{192,224},{224,1... | collective-permute-start | bytes 589832 | tf_op jit(solution)/shard_map/ppermute | solution.py:717
  42.4 5.9 %collective-permute-start.8 = (f32[64,256]{1,0:T(8,128)S(1)}, f32[64,256]{1,0:T(8,128)S(1)}, u32[]{:S(2)}, u32[]{:S(2)}) collective-permute-start(f32[64,256]{1,0:T(8,128)S(1)} %get-tuple-element.38), channel_id=1, source_target_pairs={{0,2},{2,0},{4,6},{6,4},{8,10},{10,8},{12,14},{14,12},{16,18},{18,... | collective-permute-start | bytes 196616 | tf_op jit(solution)/shard_map/ppermute | solution.py:717
  44.4 8.3 %collective-permute-start.9 = (f32[64,256]{1,0:T(8,128)S(1)}, f32[64,256]{1,0:T(8,128)S(1)}, u32[]{:S(2)}, u32[]{:S(2)}) collective-permute-start(f32[64,256]{1,0:T(8,128)S(1)} %get-tuple-element.39), channel_id=1, source_target_pairs={{2,4},{4,2},{6,8},{8,6},{10,12},{12,10},{14,16},{16,14},{18,20},{2... | collective-permute-start | bytes 196616 | tf_op jit(solution)/shard_map/ppermute | solution.py:717
